TPU v7x, 256 devices: a whole 4x4x8 slice. The times are simulated.
256 devices in a mesh: dp: 16 (over z, y_hi), tensor: 16 (over y_lo, x, core).
Axes of the slice: x: 4, y: 4 (y_hi: 2, y_lo: 2; y = y_hi * 2 + y_lo), z: 8, core: 2. Of those that a mesh axis runs over, the one named last changes fastest.
Arguments:
- inputs: bfloat16 [112, 16, 256, 128], P('tensor', 'dp'), may hold values from -6 to 6
- cotangent: bfloat16 [112, 16, 256, 128], P('tensor', 'dp'), may hold values from -6 to 6
- w_expand: bfloat16 [256, 1024], P('dp', 'tensor'), may hold values from -0.375 to 0.375
- w_project: bfloat16 [256, 1024], P('dp', 'tensor'), may hold values from -0.375 to 0.375
- dw_kernel: bfloat16 [1024, 9], P('tensor'), may hold values from -2 to 2
- se_down: bfloat16 [64, 1024], P(None, 'tensor'), may hold values from -0.75 to 0.75
- se_up: bfloat16 [64, 1024], P(None, 'tensor'), may hold values from -1.5 to 1.5
Outputs:
- block_out: bfloat16 [112, 16, 256, 128], P('tensor', 'dp')
- input_grad: bfloat16 [112, 16, 256, 128], P('tensor', 'dp')
- expand_grad: float32 [256, 1024], P('dp', 'tensor')
- project_grad: float32 [256, 1024], P('dp', 'tensor')
- kernel_grad: float32 [1024, 9], P('tensor')
- down_grad: float32 [64, 1024], P(None, 'tensor')
- up_grad: float32 [64, 1024], P(None, 'tensor')
All inputs are finite; a program needn't handle non-finite values.
Results may differ from a plain program's by a relative error of at most 0.025.
Values may be sent and summed in bfloat16 or wider, within the bound.
No kernel may reach another device: no remote copies, remote signals or barrier semaphores. Data moves between devices by JAX's collectives and lax.ppermute only.
A program may use at most 128 MiB of HBM per device.

v0:
```python
import jax
import jax.numpy as jnp
from jax import lax
from jax.sharding import PartitionSpec as P

gelu_scale = 0.7978845608
gelu_cubic = 0.044715


def gelu_pair(values):
    inner = gelu_scale * (values + gelu_cubic * values * values * values)
    tanh_part = jnp.tanh(inner)
    result = 0.5 * values * (1.0 + tanh_part)
    slope = 0.5 * (1.0 + tanh_part) + 0.5 * values * (1.0 - tanh_part * tanh_part) * gelu_scale * (
        1.0 + 3.0 * gelu_cubic * values * values
    )
    return (result, slope)


def shifted(source, shift_down, shift_right):
    height = source.shape[0]
    col_count = source.shape[3]
    padded = jnp.pad(source, ((1, 1), (0, 0), (0, 0), (1, 1)))
    return padded[
        1 + shift_down : 1 + shift_down + height,
        :,
        :,
        1 + shift_right : 1 + shift_right + col_count,
    ]


def depthwise(source, kernel):
    running = jnp.zeros_like(source)
    for tap_index in range(9):
        running = running + kernel[:, tap_index][None, None, :, None] * shifted(
            source, tap_index // 3 - 1, tap_index % 3 - 1
        )
    return running


def depthwise_back(grad_out, source, kernel):
    grad_in = jnp.zeros_like(grad_out)
    tap_sums = []
    for tap_index in range(9):
        shift_down = tap_index // 3 - 1
        shift_right = tap_index % 3 - 1
        grad_in = grad_in + kernel[:, tap_index][None, None, :, None] * shifted(
            grad_out, -shift_down, -shift_right
        )
        tap_sums.append(
            jnp.sum(grad_out * shifted(source, shift_down, shift_right), axis=(0, 1, 3))
        )
    return (grad_in, jnp.stack(tap_sums, axis=1))


def layer_norm(image):
    values = image.astype(jnp.float32)
    center = values - jnp.mean(values, axis=2, keepdims=True)
    inv_std = lax.rsqrt(jnp.mean(center * center, axis=2, keepdims=True) + 1e-05)
    return (center * inv_std, inv_std)


def channel_pass(cotangent, normed, exp_rows, proj_rows, dw_kernel, se_down, se_up):
    highest = lax.Precision.HIGHEST
    normed_all = lax.all_gather(normed, "tensor", axis=0, tiled=True)
    expanded = jnp.einsum(
        "hbcw,ce->hbew", normed_all, exp_rows, preferred_element_type=jnp.float32
    ).astype(jnp.bfloat16)
    kernel32 = dw_kernel.astype(jnp.float32)
    down32 = se_down.astype(jnp.float32)
    up_weight32 = se_up.astype(jnp.float32)
    act_one, slope_one = gelu_pair(expanded.astype(jnp.float32))
    mixed = depthwise(act_one, kernel32)
    act_two, slope_two = gelu_pair(mixed)
    pooled = jnp.mean(act_two, axis=(0, 1, 3))
    squeeze = lax.psum(jnp.dot(down32, pooled, precision=highest), "tensor")
    sig_squeeze = jax.nn.sigmoid(squeeze)
    swish_value = squeeze * sig_squeeze
    gating = jax.nn.sigmoid(jnp.dot(swish_value, up_weight32, precision=highest))
    hidden = (act_two * gating[None, None, :, None]).astype(jnp.bfloat16)
    row_piece = hidden
    projected = lax.psum_scatter(
        jnp.einsum(
            "hbew,ce->hbcw", row_piece, proj_rows, preferred_element_type=jnp.float32
        ).astype(jnp.bfloat16),
        "tensor",
        scatter_dimension=0,
        tiled=True,
    ).astype(jnp.float32)
    cot_all = lax.all_gather(cotangent, "tensor", axis=0, tiled=True)
    grad_hidden = jnp.einsum(
        "hbcw,ce->hbew", cot_all, proj_rows, preferred_element_type=jnp.float32
    ).astype(jnp.bfloat16)
    grad_h32 = grad_hidden.astype(jnp.float32)
    grad_gate = jnp.sum(grad_h32 * act_two, axis=(0, 1, 3))
    grad_excite = grad_gate * gating * (1.0 - gating)
    g_up = swish_value[:, None] * grad_excite[None, :]
    grad_swish = lax.psum(jnp.dot(up_weight32, grad_excite, precision=highest), "tensor")
    grad_squeeze = grad_swish * sig_squeeze * (1.0 + squeeze * (1.0 - sig_squeeze))
    g_down = grad_squeeze[:, None] * pooled[None, :]
    grad_pooled = jnp.dot(grad_squeeze, down32, precision=highest)
    map_cells = act_two.shape[0] * act_two.shape[3]
    grad_act_two = (
        grad_h32 * gating[None, None, :, None] + grad_pooled[None, None, :, None] / map_cells
    )
    grad_mixed = grad_act_two * slope_two
    grad_act_one, g_kernel = depthwise_back(grad_mixed, act_one, kernel32)
    grad_expanded = (grad_act_one * slope_one).astype(jnp.bfloat16)
    row_piece = grad_expanded
    grad_normed = lax.psum_scatter(
        jnp.einsum("hbew,ce->hbcw", row_piece, exp_rows, preferred_element_type=jnp.float32).astype(
            jnp.bfloat16
        ),
        "tensor",
        scatter_dimension=0,
        tiled=True,
    ).astype(jnp.float32)
    weight_grads = lax.psum_scatter(
        jnp.stack(
            [
                jnp.einsum(
                    "hbcw,hbew->ce", normed_all, grad_expanded, preferred_element_type=jnp.float32
                ),
                jnp.einsum("hbcw,hbew->ce", cot_all, hidden, preferred_element_type=jnp.float32),
            ],
            axis=1,
        ).astype(jnp.bfloat16),
        "dp",
        scatter_dimension=0,
        tiled=True,
    ).astype(jnp.float32)
    return (projected, grad_normed, weight_grads, g_kernel, g_down, g_up)


def body(inputs, cotangent, w_expand, w_project, dw_kernel, se_down, se_up):
    exp_rows, proj_rows = (
        lax.all_gather(w_expand, "dp", axis=0, tiled=True),
        lax.all_gather(w_project, "dp", axis=0, tiled=True),
    )
    normal32, inv_std = layer_norm(inputs)
    normed = normal32.astype(jnp.bfloat16)
    results = channel_pass(cotangent, normed, exp_rows, proj_rows, dw_kernel, se_down, se_up)
    projected, grad_normed, weight_grads, g_kernel, g_down, g_up = results
    block_out = (inputs.astype(jnp.float32) + projected).astype(jnp.bfloat16)
    grad32 = cotangent.astype(jnp.float32)
    mean_grad = jnp.mean(grad_normed, axis=2, keepdims=True)
    mean_inner = jnp.mean(grad_normed * normal32, axis=2, keepdims=True)
    input_grad = (grad32 + inv_std * (grad_normed - mean_grad - normal32 * mean_inner)).astype(
        jnp.bfloat16
    )
    kernel_grad, down_grad, up_grad = (
        lax.psum(g_kernel.astype(jnp.bfloat16), "dp").astype(jnp.float32),
        lax.psum(g_down.astype(jnp.bfloat16), "dp").astype(jnp.float32),
        lax.psum(g_up.astype(jnp.bfloat16), "dp").astype(jnp.float32),
    )
    return (
        block_out,
        input_grad,
        weight_grads[:, 0],
        weight_grads[:, 1],
        kernel_grad,
        down_grad,
        up_grad,
    )


def solution(mesh):
    placed = (
        P("tensor", "dp", None, None),
        P("tensor", "dp", None, None),
        P("dp", "tensor"),
        P("dp", "tensor"),
        P("tensor", None),
        P(None, "tensor"),
        P(None, "tensor"),
    )
    return jax.shard_map(
        body,
        mesh=mesh,
        in_specs=placed,
        out_specs=(
            P("tensor", "dp", None, None),
            P("tensor", "dp", None, None),
            P("dp", "tensor"),
            P("dp", "tensor"),
            P("tensor", None),
            P(None, "tensor"),
            P(None, "tensor"),
        ),
        check_vma=False,
    )
```

profile of v0, /device:TPU:2, one launch (start us, length us, event | category | flops | bytes accessed | tf_op | source)
XLA Modules:
  0.0 543.4 jit_solution(2860895212698422903)
XLA Ops:
  7.2 0.0 copy-start
  7.2 0.0 copy-start.4
  7.2 0.0 copy-start.5
  7.2 0.0 copy-start.6
  7.2 0.0 all-gather.3.cloned.1.call-start
  7.3 1.2 copy.23
  8.5 0.2 convert_reduce_fusion.1
  8.7 0.4 fusion.90
  9.1 0.3 fusion.85
  9.4 1.0 copy.24
  10.4 0.0 all-gather.3.cloned.1.call-update
  10.4 0.0 all-gather.5.cloned.1.call-start
  10.4 0.7 all-gather.5.cloned.1.call-update
  11.1 0.0 all-reduce.6.cloned.1.call-start
  11.2 0.0 copy-done.4
  11.2 0.0 copy-done.5
  11.2 44.3 %all_gather.13 = bf16[256,64]{1,0:T(8,128)(2,1)S(1)} all-gather(bf16[16,64]{1,0:T(8,128)(2,1)S(1)} %copy-done.5), channel_id=1, replica_groups=mesh['dp'=16,'tensor'=16] {'dp'}, dimensions={0}, use_global_device_ids=true | all-gather | bytes 34816 | tf_op jit(solution)/shard_map/all_gather | solution.py:137
  55.6 0.0 copy-done.6
  55.6 35.9 %all_gather.14 = bf16[256,64]{1,0:T(8,128)(2,1)S(1)} all-gather(bf16[16,64]{1,0:T(8,128)(2,1)S(1)} %copy-done.6), channel_id=1, replica_groups=mesh['dp'=16,'tensor'=16] {'dp'}, dimensions={0}, use_global_device_ids=true | all-gather | bytes 34816 | tf_op jit(solution)/shard_map/all_gather | solution.py:138
  91.4 6.8 %fusion.42 = (f32[112,1,64,128]{3,2,0,1:T(8,128)}, bf16[112,128,64]{1,2,0:T(8,128)(2,1)S(1)}) fusion(bf16[256,64]{1,0:T(8,128)(2,1)S(1)} %all_gather.13, bf16[112,1,256,128]{3,2,1,0:T(8,128)(2,1)} %all-gather.3.cloned.1.call-done), kind=kOutput, calls=%fused_computation.66 | convolution fusion | flops 478937088 | bytes 12877824 | tf_op jit(solution)/shard_map/hbcw,ce->hbew/dot_general | solution.py:66
  98.2 18.5 %all-gather.5.cloned.1.call-done = bf16[112,1,256,128]{3,2,1,0:T(8,128)(2,1)} async-done(((bf16[7,1,256,128]{3,2,1,0:T(8,128)(2,1)}), bf16[112,1,256,128]{3,2,1,0:T(8,128)(2,1)}) %all-gather.5.cloned.1.call-update) | async-done | bytes 7340048 | tf_op jit(solution)/shard_map/all_gather | solution.py:90
  116.7 22.6 %fusion.40 = (f32[64]{0:T(128)S(1)}, f32[64]{0:T(128)S(1)}, f32[112,1,64,128]{3,2,0,1:T(8,128)}, bf16[64,112,128]{2,0,1:T(8,128)(2,1)}) fusion(f32[64]{0:T(128)S(1)} %get-tuple-element.46, f32[64]{0:T(128)S(1)} %get-tuple-element.47, f32[64]{0:T(128)S(1)} %get-tuple-element.48, f32[64]{0:T(128)S(1)} %get-tuple-element.49, ...), kind=kOutput, calls=%fused_computation.63 | convolution fusion | flops 497287040 | bytes 16550656 | tf_op jit(solution)/shard_map/hbcw,ce->hbew/dot_general | solution.py:91
  139.4 0.0 copy-done.7
  139.4 0.1 convolution_bitcast_fusion.3
  139.5 26.2 %psum.35 = f32[64]{0:T(128)S(1)} all-reduce(f32[64]{0:T(128)S(1)} %convolution_bitcast_fusion.3), channel_id=1, replica_groups=mesh['dp'=16,'tensor'=16] {'tensor'}, use_global_device_ids=true, to_apply=%region_3.4 | all-reduce | flops 64 | bytes 512 | tf_op jit(solution)/shard_map/psum | solution.py:76
  165.7 0.0 copy-done
  165.7 0.1 subtract_multiply_fusion
  165.8 0.1 convolution_bitcast_fusion.1
  166.0 27.3 %psum.36 = f32[64]{0:T(128)S(1)} all-reduce(f32[64]{0:T(128)S(1)} %convolution_bitcast_fusion.1), channel_id=1, replica_groups=mesh['dp'=16,'tensor'=16] {'tensor'}, use_global_device_ids=true, to_apply=%region_6.7 | all-reduce | flops 64 | bytes 512 | tf_op jit(solution)/shard_map/psum | solution.py:98
  193.3 0.1 fusion.77
  193.5 16.5 %multiply_reduce_fusion = (bf16[64]{0:T(256)(128)(2,1)S(1)}, bf16[64]{0:T(256)(128)(2,1)S(1)}, bf16[64]{0:T(256)(128)(2,1)S(1)}, bf16[64]{0:T(256)(128)(2,1)S(1)...) fusion(f32[112,1,64,128]{3,2,0,1:T(8,128)} %get-tuple-element.5, ...), kind=kLoop, calls=%fused_computation.68 | loop fusion | flops 44039616 | bytes 14681728 | tf_op jit(solution)/shard_map/reduce_sum | solution.py:51
  209.9 0.0 slice-start
  209.9 7.3 %fusion.20 = bf16[112,1,64,128]{3,2,0,1:T(8,128)(2,1)S(1)} fusion(f32[112,1,64,128]{3,2,0,1:T(8,128)S(1)} %get-tuple-element.37, bf16[112,128,64]{1,2,0:T(8,128)(2,1)} %copy-done.1, f32[64]{0:T(128)S(1)} %get-tuple-element.46, f32[64]{0:T(128)S(1)} %get-tuple-element.47, f32[64]{0:T(128)S(1)} %get-tuple-element.48, f32[64]{0:T(128)S(1)} %get-tuple-element.49, ...), kind=kLoop, calls=%fused_computation.42 | loop fusion | flops 33947648 | bytes 7342336 | tf_op jit(solution)/shard_map/convert_element_type | solution.py:108
  217.2 0.0 copy-done.2
  217.2 0.0 slice-start.1
  217.3 5.7 %fusion.74 = bf16[256,1,64]{0,2,1:T(8,128)(2,1)S(1)} fusion(bf16[112,1,256,128]{3,2,1,0:T(8,128)(2,1)} %all-gather.5.cloned.1.call-done, f32[64]{0:T(128)S(1)} %get-tuple-element.58, f32[112,1,64,128]{3,2,0,1:T(8,128)S(1)} %copy-done.2), kind=kOutput, calls=%fused_computation.96 | convolution fusion | flops 478953472 | bytes 11043072 | tf_op jit(solution)/shard_map/hbcw,hbew->ce/dot_general | solution.py:124
  222.9 2.3 fusion.69
  225.3 0.8 copy.26
  226.1 0.0 all-reduce.6.cloned.1.call-update
  226.1 0.0 reduce-scatter.5.cloned.1.call-start
  226.1 5.1 convert_bitcast_fusion
  231.2 0.0 reduce-scatter.5.cloned.1.call-update
  231.2 0.0 reduce-scatter.3.cloned.1.call-start
  231.3 7.7 %convert_bitcast_fusion.1 = bf16[112,1,256,128]{2,3,0,1:T(8,128)(2,1)} fusion(bf16[256,64]{1,0:T(8,128)(2,1)S(1)} %all_gather.14, f32[64]{0:T(128)S(1)} %get-tuple-element.58, f32[112,1,64,128]{3,2,0,1:T(8,128)} %get-tuple-element.40), kind=kOutput, calls=%fused_computation.25 | convolution fusion | flops 482607104 | bytes 11043072 | tf_op jit(solution)/shard_map/hbew,ce->hbcw/dot_general | solution.py:83
  239.0 0.0 reduce-scatter.3.cloned.1.call-update
  239.0 1.0 copy-done.3
  240.0 0.2 copy.25
  240.2 0.6 dynamic-slice
  241.5 0.1 stack.64
  241.5 0.1 multiply_convert_fusion.1
  241.6 0.1 multiply_convert_fusion.2
  241.7 77.5 %all-reduce.3 = (bf16[64,9]{0,1:T(8,128)(2,1)S(1)}, bf16[64,64]{1,0:T(8,128)(2,1)S(1)}, bf16[64,64]{1,0:T(8,128)(2,1)S(1)}) all-reduce(bf16[64,9]{0,1:T(8,128)(2,1)S(1)} %stack.64, bf16[64,64]{1,0:T(8,128)(2,1)S(1)} %multiply_convert_fusion.2, bf16[64,64]{1,0:T(8,128)(2,1)S(1)} %multiply_convert_fusion.1), channel_id=1, replica_groups=mesh['dp'=16,'tensor'=16] {'dp'}, use_global_device_ids=true, to_apply=%region_20.21 | all-reduce | flops 8768 | bytes 35072 | tf_op jit(solution)/shard_map/psum | solution.py:152
  319.1 0.6 convert_element_type.165
  319.7 0.6 convert_element_type.167
  320.4 0.6 convert_element_type.169
  321.0 63.7 %all-reduce.6.cloned.1.call-done = bf16[256,2,64]{2,1,0:T(2,128)(2,1)} async-done(((bf16[256,2,64]{2,1,0:T(2,128)(2,1)}), bf16[256,2,64]{2,1,0:T(2,128)(2,1)}) %all-reduce.6.cloned.1.call-update) | async-done | bytes 65552
  384.7 0.7 dynamic-slice_convert_fusion
  385.4 0.6 fusion.106
  386.0 70.7 %reduce-scatter.5.cloned.1.call-done = bf16[7,1,256,128]{2,3,0,1:T(8,128)(2,1)} async-done(((bf16[112,1,256,128]{2,3,0,1:T(8,128)(2,1)}), bf16[7,1,256,128]{2,3,0,1:T(8,128)(2,1)}) %reduce-scatter.5.cloned.1.call-update) | async-done | bytes 458768 | tf_op jit(solution)/shard_map/reduce_scatter | solution.py:110
  456.7 1.6 convert_reduce_fusion
  458.3 74.9 %reduce-scatter.3.cloned.1.call-done = bf16[7,1,256,128]{2,3,0,1:T(8,128)(2,1)} async-done(((bf16[112,1,256,128]{2,3,0,1:T(8,128)(2,1)}), bf16[7,1,256,128]{2,3,0,1:T(8,128)(2,1)}) %reduce-scatter.3.cloned.1.call-update) | async-done | bytes 458768 | tf_op jit(solution)/shard_map/reduce_scatter | solution.py:82
  533.2 1.7 fusion.89
  535.0 1.0 copy.28
  535.9 1.0 copy.27
  (20 shorter events, 0.1 us)
Async XLA Ops:
  7.2 158.5 %copy-start = (bf16[64,64]{1,0:T(8,128)(2,1)S(1)}, bf16[64,64]{1,0:T(8,128)(2,1)}, u32[]{:S(2)}) copy-start(bf16[64,64]{1,0:T(8,128)(2,1)} %param.13) | copy-start | bytes 24580
  7.2 4.0 copy-start.4
  7.2 4.0 copy-start.5
  7.2 48.4 %copy-start.6 = (bf16[16,64]{1,0:T(8,128)(2,1)S(1)}, bf16[16,64]{1,0:T(8,128)(2,1)}, u32[]{:S(2)}) copy-start(bf16[16,64]{1,0:T(8,128)(2,1)} %param.10) | copy-start | bytes 6148
  7.2 84.2 %all-gather.3.cloned.1.call-start = ((), (), s32[]{:S(2)}) async-start(), calls=%async_computation.2 | async-start | bytes 7798784 | tf_op jit(solution)/shard_map/all_gather | solution.py:65
  10.4 106.3 %all-gather.5.cloned.1.call-start = ((), (), s32[]{:S(2)}) async-start(), calls=%async_computation.4 | async-start | bytes 7798784 | tf_op jit(solution)/shard_map/all_gather | solution.py:90
  11.1 373.5 %all-reduce.6.cloned.1.call-start = ((), (), s32[]{:S(2)}) async-start(), calls=%async_computation.6 | async-start | bytes 262144
  98.2 95.2 %copy-start.1 = (bf16[112,128,64]{1,2,0:T(8,128)(2,1)}, bf16[112,128,64]{1,2,0:T(8,128)(2,1)S(1)}, u32[]{:S(2)}) copy-start(bf16[112,128,64]{1,2,0:T(8,128)(2,1)S(1)} %get-tuple-element.55) | copy-start | bytes 5505028
  116.7 22.7 %copy-start.7 = (bf16[64,64]{1,0:T(8,128)(2,1)S(1)}, bf16[64,64]{1,0:T(8,128)(2,1)}, u32[]{:S(2)}) copy-start(bf16[64,64]{1,0:T(8,128)(2,1)} %param.12) | copy-start | bytes 24580
  209.9 7.3 %copy-start.2 = (f32[112,1,64,128]{3,2,0,1:T(8,128)S(1)}, f32[112,1,64,128]{3,2,0,1:T(8,128)}, u32[]{:S(2)}) copy-start(f32[112,1,64,128]{3,2,0,1:T(8,128)} %get-tuple-element.40) | copy-start | bytes 11010052
  209.9 13.0 %slice-start = ((s8[7340032]{0:T(1024)(128)(4,1)}), s8[3145728]{0:T(1024)(128)(4,1)S(1)}, s32[]{:S(2)}) async-start(s8[7340032]{0:T(1024)(128)(4,1)} %bitcast.213), calls=%async_computation.7 | async-start | bytes 6291456
  217.2 5.7 %slice-start.1 = ((s8[7340032]{0:T(1024)(128)(4,1)}), s8[4194304]{0:T(1024)(128)(4,1)S(1)}, s32[]{:S(2)}) async-start(s8[7340032]{0:T(1024)(128)(4,1)} %bitcast.213), calls=%async_computation.8 | async-start | bytes 8388608
  226.1 230.6 %reduce-scatter.5.cloned.1.call-start = ((), (), s32[]{:S(2)}) async-start(), calls=%async_computation.5 | async-start | bytes 7798784 | tf_op jit(solution)/shard_map/reduce_scatter | solution.py:110
  231.2 302.0 %reduce-scatter.3.cloned.1.call-start = ((), (), s32[]{:S(2)}) async-start(), calls=%async_computation.3 | async-start | bytes 7798784 | tf_op jit(solution)/shard_map/reduce_scatter | solution.py:82
  239.0 1.0 copy-start.3
  239.0 1.2 copy-start.8
Sparse Core Ops, SparseCore 0:
  10.5 52.5 all-gather.2
  65.0 51.7 all-gather.4
  226.2 158.4 all-reduce.5
  387.2 69.3 reduce-scatter.4
  459.2 73.9 reduce-scatter.2
where the time goes:
time: 548 us; the launch traced here: 543 us
  waiting for transfers between devices  229 us (42%)
  blocking collectives  211 us (39%)
  matrix products  50.7 us (9%)
  other arithmetic  30.8 us (6%)
  between operations  14.6 us (3%)
  local copies, waits for them, and re-layouts  7.42 us (1%)
    psum x1, blocking collectives, body(): lax.psum(g_kernel.astype(jnp.bfloat16), 'dp').astype(jnp.float32)  77.5 us
    reduce_scatter x1, waiting for transfers between devices, channel_pass(): lax.psum_scatter(jnp.einsum('hbew,ce->hbcw', row_piece, proj_rows, prefer...  74.9 us
    reduce_scatter x1, waiting for transfers between devices, channel_pass(): lax.psum_scatter(jnp.einsum('hbew,ce->hbcw', row_piece, exp_rows, preferr...  70.7 us
    unnamed x6, waiting for transfers between devices  64.5 us
    all_gather x1, blocking collectives, body(): lax.all_gather(w_expand, 'dp', axis=0, tiled=True)  44.3 us
    all_gather x1, blocking collectives, body(): lax.all_gather(w_project, 'dp', axis=0, tiled=True)  35.9 us
    psum x1, blocking collectives, channel_pass(): lax.psum(jnp.dot(up_weight32, grad_excite, precision=highest), 'tensor')  27.3 us
    psum x1, blocking collectives, channel_pass(): squeeze = lax.psum(jnp.dot(down32, pooled, precision=highest), 'tensor')  26.2 us
  transfers between devices with their start and end apart: 5, of which 4 were waited for; matrix products, arithmetic and copies ran while one was open for 5% of the time, Pallas kernels for 0%

commit v1 on v0

v1 whole, which is shorter than its diff:
```python
import jax
import jax.numpy as jnp
from jax import lax
from jax.experimental import pallas as pl
from jax.experimental.pallas import tpu as pltpu
from jax.sharding import PartitionSpec as P

bf16 = jnp.bfloat16
f32 = jnp.float32

gelu_scale = 0.7978845608
gelu_cubic = 0.044715

CH = 256
HALF = 512
SQ = 64
COLS = 128
ROWS = 14
EXT = ROWS + 4
CELLS = 112 * 128
BLOCKS = 4
GROUP = 16
BOTH = ("dp", "tensor")
VMEM = 48 * 1024 * 1024


def groups(count, steps):
    seen, found = set(), []
    for first in range(count):
        if first in seen:
            continue
        members = [first]
        for step in steps:
            members = members + [member ^ step for member in members]
        members = sorted(members)
        seen.update(members)
        found.append(members)
    return found


def exchange(pieces, axes, steps=None):
    members = None
    if steps is not None:
        members = groups(256 if axes == BOTH else 16, steps)
    return lax.all_to_all(pieces, axes, 0, 0, tiled=True, axis_index_groups=members)


def to_all(piece, count):
    return jnp.broadcast_to(piece[None], (count,) + piece.shape)


PLANE = (2, 4, 8, 16)
DEPTH = (2, 4, 8)


def gelu_pair(values):
    square = values * values
    inner = values * (gelu_scale + (gelu_scale * gelu_cubic) * square)
    part = 0.5 + 0.5 * jnp.tanh(inner)
    act = values * part
    slope = part + act * (1.0 - part) * (
        2.0 * gelu_scale + (6.0 * gelu_scale * gelu_cubic) * square
    )
    return act, slope


def params(**more):
    return pltpu.CompilerParams(vmem_limit_bytes=VMEM, **more)


def cost(flops, size):
    return pl.CostEstimate(flops=flops, bytes_accessed=size, transcendentals=0)


def join_low(first, second, low):
    return jnp.where(low, first, pltpu.roll(second, 64, 1))


def join_high(first, second, low):
    return jnp.where(low, pltpu.roll(first, 64, 1), second)


def lanes_of(shape):
    return lax.broadcasted_iota(jnp.int32, shape, 1)


def down_rows(row):
    return jnp.broadcast_to(row, (128, 128)).T


def norm_kernel(pos, own_x, other_x, own_c, other_c, top, bottom, normed, cot):
    row = pl.program_id(0)
    pair_row = row - 2
    mine = (pair_row >= 7).astype(jnp.int32) == pos[0]
    x = jnp.where(mine, own_x[0, 0], other_x[0, 0])
    c = jnp.where(mine, own_c[0, 0], other_c[0, 0])
    x = jnp.where(row < 2, top[0, 0], jnp.where(row >= ROWS + 2, bottom[0, 0], x))
    c = jnp.where(row < 2, top[1, 0], jnp.where(row >= ROWS + 2, bottom[1, 0], c))
    values = x.astype(f32)
    center = values - jnp.mean(values, axis=0, keepdims=True)
    inv_std = lax.rsqrt(jnp.mean(center * center, axis=0, keepdims=True) + 1e-05)
    normed[...] = (center * inv_std).astype(bf16)
    cot[...] = c


def norm_rows(pos, own_x, other_x, own_c, other_c, top, bottom):
    def own_map(i, pos):
        return (jnp.clip(i - 2 - 7 * pos[0], 0, 6), 0, 0, 0)

    def other_map(i, pos):
        return (jnp.clip(i - 2 - 7 * (1 - pos[0]), 0, 6), 0, 0, 0)

    row_block = (1, 1, CH, COLS)
    return pl.pallas_call(
        norm_kernel,
        grid_spec=pltpu.PrefetchScalarGridSpec(
            num_scalar_prefetch=1,
            grid=(EXT,),
            in_specs=[
                pl.BlockSpec(row_block, own_map),
                pl.BlockSpec(row_block, other_map),
                pl.BlockSpec(row_block, own_map),
                pl.BlockSpec(row_block, other_map),
                pl.BlockSpec((2, 1, CH, COLS), lambda i, pos: (0, jnp.clip(i, 0, 1), 0, 0)),
                pl.BlockSpec(
                    (2, 1, CH, COLS), lambda i, pos: (0, jnp.clip(i - ROWS - 2, 0, 1), 0, 0)
                ),
            ],
            out_specs=[
                pl.BlockSpec((CH, COLS), lambda i, pos: (0, i)),
                pl.BlockSpec((CH, COLS), lambda i, pos: (0, i)),
            ],
        ),
        out_shape=[jax.ShapeDtypeStruct((CH, EXT * COLS), bf16)] * 2,
        compiler_params=params(),
        cost_estimate=cost(10**9, 8 * 10**6),
        name="norm_rows",
    )(pos, own_x, other_x, own_c, other_c, top, bottom)


def spread_taps(small, taps, masked):
    low = lanes_of((16, 128)) < 64
    first = small[0, 0, 64:80, :].astype(f32)
    second = small[1, 0, 64:80, :].astype(f32)
    rows = join_low(first, second, low)
    lane = lanes_of((128, 128))
    for tap in range(9):
        spread = down_rows(rows[tap : tap + 1, :])
        if masked and tap % 3 == 0:
            spread = jnp.where(lane == 0, 0.0, spread)
        if masked and tap % 3 == 2:
            spread = jnp.where(lane == 127, 0.0, spread)
        taps[tap] = spread


def forward_kernel(
    pos, weights, small, normed, cot,
    act1, slope1, act2, part_p, part_q, proj_grad, w_exp, w_proj, sums,
    expanded, grad_hidden, taps, pool, gate,
):
    step = pl.program_id(0)
    low = lanes_of((16, 128)) < 64
    for z in range(8):
        for yh in range(2):
            first = weights[yh, 0, z].astype(f32)
            second = weights[yh, 1, z].astype(f32)
            rows = pl.ds((z * 2 + yh) * 16, 16)
            w_exp[rows, :] = join_low(first, second, low).astype(bf16)
            w_proj[rows, :] = join_high(first, second, low).astype(bf16)
    spread_taps(small, taps, True)
    w_exp_t = w_exp[...].astype(f32).T.astype(bf16)
    w_proj_t = w_proj[...].astype(f32).T.astype(bf16)
    for part in range(EXT // 2):
        cells = slice(part * 256, part * 256 + 256)
        expanded[:, cells] = jnp.dot(
            w_exp_t, normed[:, cells], preferred_element_type=f32
        ).astype(bf16)
    for part in range(ROWS // 2 + 1):
        cells = slice(part * 256, part * 256 + 256)
        source = slice(part * 256 + 128, part * 256 + 384)
        grad_hidden[:, cells] = jnp.dot(
            w_proj_t, cot[:, source], preferred_element_type=f32
        ).astype(bf16)
    first_chip = pos[1].astype(f32)
    last_chip = pos[2].astype(f32)

    def one_group(index, carry):
        rows = pl.ds(pl.multiple_of(index * GROUP, GROUP), GROUP)
        tap = [taps[k, rows, :] for k in range(9)]
        running = {}
        pool_sum = jnp.zeros((GROUP, COLS), f32)
        gate_sum = jnp.zeros((GROUP, COLS), f32)
        for h in range(EXT):
            value = expanded[rows, h * 128 : h * 128 + 128].astype(f32)
            act, slope = gelu_pair(value)
            act1[rows, h * 128 : h * 128 + 128] = act.astype(bf16)
            if 2 <= h < ROWS + 2:
                slope1[rows, (h - 2) * 128 : (h - 1) * 128] = slope.astype(bf16)
            left = pltpu.roll(act, 1, 1)
            right = pltpu.roll(act, 127, 1)
            for i in range(3):
                m = h + 1 - i
                if not 1 <= m <= ROWS + 2:
                    continue
                term = tap[3 * i] * left + tap[3 * i + 1] * act + tap[3 * i + 2] * right
                running[m] = running[m] + term if m in running else term
            m = h - 1
            if not 1 <= m <= ROWS + 2:
                continue
            act, slope = gelu_pair(running.pop(m))
            grad = grad_hidden[rows, (m - 1) * 128 : m * 128].astype(f32)
            if m == 1:
                slope = slope * first_chip
            if m == ROWS + 2:
                slope = slope * last_chip
            part_q[rows, (m - 1) * 128 : m * 128] = slope.astype(bf16)
            part_p[rows, (m - 1) * 128 : m * 128] = (slope * grad).astype(bf16)
            if 2 <= m < ROWS + 2:
                act2[rows, (m - 2) * 128 : (m - 1) * 128] = act.astype(bf16)
                pool_sum = pool_sum + act
                gate_sum = gate_sum + act * grad
        pool[rows, :] = pool_sum
        gate[rows, :] = gate_sum
        return carry

    lax.fori_loop(0, 128 // GROUP, one_group, 0)
    sums[pl.ds(step, 1), :] = jnp.sum(pool[...].T, axis=0, keepdims=True)
    sums[pl.ds(step + BLOCKS, 1), :] = jnp.sum(gate[...].T, axis=0, keepdims=True)
    proj_grad[...] = lax.dot_general(
        cot[:, 256 : 256 + ROWS * COLS],
        act2[...],
        (((1,), (1,)), ((), ())),
        preferred_element_type=f32,
    )


def forward(pos, weights, small, normed, cot):
    def along(width):
        return pl.BlockSpec((128, width * COLS), lambda g, pos: (g, 0))

    across = pl.BlockSpec((CH, 128), lambda g, pos: (0, g))
    whole = pl.BlockSpec((CH, EXT * COLS), lambda g, pos: (0, 0))
    return pl.pallas_call(
        forward_kernel,
        grid_spec=pltpu.PrefetchScalarGridSpec(
            num_scalar_prefetch=1,
            grid=(BLOCKS,),
            in_specs=[
                pl.BlockSpec((2, 2, 8, 16, 128), lambda g, pos: (0, g, 0, 0, 0)),
                pl.BlockSpec((2, 1, 80, 128), lambda g, pos: (g, pos[0], 0, 0)),
                whole,
                whole,
            ],
            out_specs=[
                along(EXT),
                along(ROWS),
                along(ROWS),
                along(ROWS + 2),
                along(ROWS + 2),
                across,
                across,
                across,
                pl.BlockSpec((8, 128), lambda g, pos: (0, 0)),
            ],
            scratch_shapes=[
                pltpu.VMEM((128, EXT * COLS), bf16),
                pltpu.VMEM((128, (ROWS + 2) * COLS), bf16),
                pltpu.VMEM((9, 128, 128), f32),
                pltpu.VMEM((128, 128), f32),
                pltpu.VMEM((128, 128), f32),
            ],
        ),
        out_shape=[
            jax.ShapeDtypeStruct((HALF, EXT * COLS), bf16),
            jax.ShapeDtypeStruct((HALF, ROWS * COLS), bf16),
            jax.ShapeDtypeStruct((HALF, ROWS * COLS), bf16),
            jax.ShapeDtypeStruct((HALF, (ROWS + 2) * COLS), bf16),
            jax.ShapeDtypeStruct((HALF, (ROWS + 2) * COLS), bf16),
            jax.ShapeDtypeStruct((CH, HALF), f32),
            jax.ShapeDtypeStruct((CH, HALF), bf16),
            jax.ShapeDtypeStruct((CH, HALF), bf16),
            jax.ShapeDtypeStruct((8, 128), f32),
        ],
        compiler_params=params(),
        cost_estimate=cost(10**10, 40 * 10**6),
        name="forward",
    )(pos, weights, small, normed, cot)


def excite_kernel(pos, sums, small, coef, vectors, pooled_all, gate_all):
    low = lanes_of((SQ, 128)) < 64
    totals = []
    for core in range(2):
        total = sums[core]
        for other in range(1, 8):
            total = total + sums[2 * other + core]
        totals.append(total)
    pooled, grad_gate, down, up = [], [], [], []
    for core in range(2):
        for block in range(BLOCKS):
            pooled.append(totals[core][block : block + 1] * (1.0 / CELLS))
            grad_gate.append(totals[core][BLOCKS + block : BLOCKS + block + 1])
            first = small[4 * block + core, 0:SQ, :].astype(f32)
            second = small[4 * block + 2 + core, 0:SQ, :].astype(f32)
            down.append(join_low(first, second, low))
            up.append(join_high(first, second, low))
    count = 2 * BLOCKS
    squeeze = sum(jnp.sum(down[b] * pooled[b], axis=1, keepdims=True) for b in range(count))
    sig = 1.0 / (1.0 + jnp.exp(-squeeze))
    swish = squeeze * sig
    gating, grad_excite = [], []
    for b in range(count):
        logit = jnp.sum(up[b] * swish, axis=0, keepdims=True)
        gating.append(1.0 / (1.0 + jnp.exp(-logit)))
        grad_excite.append(grad_gate[b] * gating[b] * (1.0 - gating[b]))
    grad_swish = sum(jnp.sum(up[b] * grad_excite[b], axis=1, keepdims=True) for b in range(count))
    grad_squeeze = grad_swish * sig * (1.0 + squeeze * (1.0 - sig))
    for core in range(2):

        @pl.when(pos[0] == core)
        def _():
            for block in range(BLOCKS):
                b = core * BLOCKS + block
                cells = slice(block * 128, block * 128 + 128)
                grad_pooled = jnp.sum(down[b] * grad_squeeze, axis=0, keepdims=True)
                coef[0:1, cells] = gating[b]
                coef[1:2, cells] = grad_pooled * (1.0 / CELLS)
                pooled_all[block] = pooled[b]
                gate_all[block] = grad_excite[b]

    coef[2:8, :] = jnp.zeros((6, HALF), f32)
    place = pos[3]
    turned = lax.rem(place, 2) == 1
    block = lax.div(place, 2)
    own_pool = pooled_all[block]
    own_gate = gate_all[block]
    row_low = lanes_of((1, 128)) < 64
    side = jnp.concatenate([swish, grad_squeeze], axis=0)
    vectors[0:1, :] = jnp.broadcast_to(side, (128, 128)).T[0:1, :]
    vectors[1:2, :] = jnp.where(
        turned,
        jnp.where(row_low, pltpu.roll(own_pool, 64, 1), own_gate),
        jnp.where(row_low, own_pool, pltpu.roll(own_gate, 64, 1)),
    )
    vectors[2:8, :] = jnp.zeros((6, 128), f32)


def excite(pos, sums, small):
    return pl.pallas_call(
        excite_kernel,
        in_specs=[
            pl.BlockSpec(memory_space=pltpu.SMEM),
            pl.BlockSpec(memory_space=pltpu.VMEM),
            pl.BlockSpec(memory_space=pltpu.VMEM),
        ],
        out_specs=[pl.BlockSpec(memory_space=pltpu.VMEM)] * 2,
        out_shape=[
            jax.ShapeDtypeStruct((8, HALF), f32),
            jax.ShapeDtypeStruct((8, 128), f32),
        ],
        scratch_shapes=[
            pltpu.VMEM((BLOCKS, 1, 128), f32),
            pltpu.VMEM((BLOCKS, 1, 128), f32),
        ],
        compiler_params=params(),
        cost_estimate=cost(10**8, 2 * 10**6),
        name="excite",
    )(pos, sums, small)


def backward_kernel(
    pos, coef, small, normed, act1, slope1, part_p, part_q, proj_grad,
    grad_expanded, pieces,
    taps, gates, pools, kernel_sums, tap_rows,
):
    spread_taps(small, taps, False)
    gates[...] = down_rows(coef[0:1, :])
    pools[...] = down_rows(coef[1:2, :])
    lane = lanes_of((GROUP, COLS))

    def one_group(index, carry):
        rows = pl.ds(pl.multiple_of(index * GROUP, GROUP), GROUP)
        tap = [taps[k, rows, :] for k in range(9)]
        gating = gates[rows, :]
        pooled = pools[rows, :]
        running = {}
        sums = [None] * 9
        for m in range(1, ROWS + 3):
            cells = slice((m - 1) * 128, m * 128)
            grad = part_p[rows, cells].astype(f32) * gating + part_q[rows, cells].astype(f32) * pooled
            turned = (
                jnp.where(lane == 127, 0.0, pltpu.roll(grad, 127, 1)),
                grad,
                jnp.where(lane == 0, 0.0, pltpu.roll(grad, 1, 1)),
            )
            for i in range(3):
                h = m + i - 1
                if 2 <= h < ROWS + 2:
                    term = tap[3 * i] * turned[0] + tap[3 * i + 1] * turned[1] + tap[3 * i + 2] * turned[2]
                    running[h] = running[h] + term if h in running else term
                if 2 <= m < ROWS + 2:
                    act = act1[rows, h * 128 : h * 128 + 128].astype(f32)
                    for j in range(3):
                        term = turned[j] * act
                        k = 3 * i + j
                        sums[k] = term if sums[k] is None else sums[k] + term
            h = m - 1
            if 2 <= h < ROWS + 2:
                out = slice((h - 2) * 128, (h - 1) * 128)
                grad_expanded[rows, out] = (running.pop(h) * slope1[rows, out].astype(f32)).astype(bf16)
        for k in range(9):
            kernel_sums[k, rows, :] = sums[k]
        return carry

    lax.fori_loop(0, 128 // GROUP, one_group, 0)
    exp_grad = lax.dot_general(
        normed[:, 256 : 256 + ROWS * COLS],
        grad_expanded[...],
        (((1,), (1,)), ((), ())),
        preferred_element_type=f32,
    )
    tap_rows[...] = jnp.zeros((16, 128), f32)
    for k in range(9):
        tap_rows[k : k + 1, :] = jnp.sum(kernel_sums[k].T, axis=0, keepdims=True)
    scaled = proj_grad[...] * coef[0:1, :]
    low = lanes_of((CH, 128)) < 64
    first = join_low(exp_grad, scaled, low).astype(bf16)
    second = join_high(exp_grad, scaled, low).astype(bf16)
    first_taps = tap_rows[...]
    second_taps = pltpu.roll(first_taps, 64, 1)
    for yh in range(2):
        for z in range(8):
            rows = slice((z * 2 + yh) * 16, (z * 2 + yh) * 16 + 16)
            pieces[yh, 0, z] = first[rows]
            pieces[yh, 1, z] = second[rows]
        pieces[yh, 0, 8] = first_taps.astype(bf16)
        pieces[yh, 1, 8] = second_taps.astype(bf16)


def backward(pos, coef, small, normed, act1, slope1, part_p, part_q, proj_grad):
    def along(width):
        return pl.BlockSpec((128, width * COLS), lambda g, pos: (g, 0))

    return pl.pallas_call(
        backward_kernel,
        grid_spec=pltpu.PrefetchScalarGridSpec(
            num_scalar_prefetch=1,
            grid=(BLOCKS,),
            in_specs=[
                pl.BlockSpec((8, 128), lambda g, pos: (0, g)),
                pl.BlockSpec((2, 1, 80, 128), lambda g, pos: (g, pos[0], 0, 0)),
                pl.BlockSpec((CH, EXT * COLS), lambda g, pos: (0, 0)),
                along(EXT),
                along(ROWS),
                along(ROWS + 2),
                along(ROWS + 2),
                pl.BlockSpec((CH, 128), lambda g, pos: (0, g)),
            ],
            out_specs=[
                along(ROWS),
                pl.BlockSpec((2, 2, 9, 16, 128), lambda g, pos: (0, g, 0, 0, 0)),
            ],
            scratch_shapes=[
                pltpu.VMEM((9, 128, 128), f32),
                pltpu.VMEM((128, 128), f32),
                pltpu.VMEM((128, 128), f32),
                pltpu.VMEM((9, 128, 128), f32),
                pltpu.VMEM((16, 128), f32),
            ],
        ),
        out_shape=[
            jax.ShapeDtypeStruct((HALF, ROWS * COLS), bf16),
            jax.ShapeDtypeStruct((2, 8, 9, 16, 128), bf16),
        ],
        compiler_params=params(),
        cost_estimate=cost(8 * 10**9, 30 * 10**6),
        name="backward",
    )(pos, coef, small, normed, act1, slope1, part_p, part_q, proj_grad)


def part_kernel(pos, coef, w_proj, w_exp, act2, grad_expanded, out):
    gated = (w_proj[...].astype(f32) * coef[0:1, :]).astype(bf16)
    for row in range(7):
        cells = slice(row * 128, row * 128 + 128)
        out[0, row] = jnp.dot(gated, act2[:, cells], preferred_element_type=f32).astype(bf16)
        out[1, row] = jnp.dot(
            w_exp[...], grad_expanded[:, cells], preferred_element_type=f32
        ).astype(bf16)


def other_part(pos, coef, w_proj, w_exp, act2, grad_expanded):
    weight = pl.BlockSpec((CH, HALF), lambda g, pos: (0, 0))
    other = pl.BlockSpec((HALF, 7 * COLS), lambda g, pos: (0, 1 - pos[0]))
    return pl.pallas_call(
        part_kernel,
        grid_spec=pltpu.PrefetchScalarGridSpec(
            num_scalar_prefetch=1,
            grid=(1,),
            in_specs=[
                pl.BlockSpec((8, HALF), lambda g, pos: (0, 0)),
                weight,
                weight,
                other,
                other,
            ],
            out_specs=pl.BlockSpec((2, 7, CH, COLS), lambda g, pos: (0, 0, 0, 0)),
        ),
        out_shape=jax.ShapeDtypeStruct((2, 7, CH, COLS), bf16),
        compiler_params=params(),
        cost_estimate=cost(2 * 10**9, 4 * 10**6),
        name="other_part",
    )(pos, coef, w_proj, w_exp, act2, grad_expanded)


def finish_kernel(pos, coef, w_proj, w_exp, act2, grad_expanded, arrived, x, c, block_out, input_grad):
    gated = (w_proj[...].astype(f32) * coef[0:1, :]).astype(bf16)
    for row in range(7):
        cells = slice(row * 128, row * 128 + 128)
        projected = jnp.dot(gated, act2[:, cells], preferred_element_type=f32)
        projected = projected + arrived[0, row].astype(f32)
        values = x[row, 0].astype(f32)
        block_out[row, 0] = (values + projected).astype(bf16)
        grad = jnp.dot(w_exp[...], grad_expanded[:, cells], preferred_element_type=f32)
        grad = grad + arrived[1, row].astype(f32)
        center = values - jnp.mean(values, axis=0, keepdims=True)
        inv_std = lax.rsqrt(jnp.mean(center * center, axis=0, keepdims=True) + 1e-05)
        normal = center * inv_std
        mean_grad = jnp.mean(grad, axis=0, keepdims=True)
        mean_inner = jnp.mean(grad * normal, axis=0, keepdims=True)
        input_grad[row, 0] = (
            c[row, 0].astype(f32) + inv_std * (grad - mean_grad - normal * mean_inner)
        ).astype(bf16)


def finish(pos, coef, w_proj, w_exp, act2, grad_expanded, arrived, x, c):
    weight = pl.BlockSpec((CH, HALF), lambda g, pos: (0, 0))
    own = pl.BlockSpec((HALF, 7 * COLS), lambda g, pos: (0, pos[0]))
    rows = pl.BlockSpec((7, 1, CH, COLS), lambda g, pos: (0, 0, 0, 0))
    return pl.pallas_call(
        finish_kernel,
        grid_spec=pltpu.PrefetchScalarGridSpec(
            num_scalar_prefetch=1,
            grid=(1,),
            in_specs=[
                pl.BlockSpec((8, HALF), lambda g, pos: (0, 0)),
                weight,
                weight,
                own,
                own,
                pl.BlockSpec((2, 7, CH, COLS), lambda g, pos: (0, 0, 0, 0)),
                rows,
                rows,
            ],
            out_specs=[rows, rows],
        ),
        out_shape=[jax.ShapeDtypeStruct((7, 1, CH, COLS), bf16)] * 2,
        compiler_params=params(),
        cost_estimate=cost(2 * 10**9, 6 * 10**6),
        name="finish",
    )(pos, coef, w_proj, w_exp, act2, grad_expanded, arrived, x, c)


def body(inputs, cotangent, w_expand, w_project, dw_kernel, se_down, se_up):
    place = lax.axis_index("tensor")
    core = lax.rem(place, 2)
    chip = lax.div(place, 2)
    pos = jnp.stack([core, (chip > 0), (chip < 7), chip]).astype(jnp.int32)
    swap = [(i, i ^ 1) for i in range(16)]
    with jax.named_scope("weights"):
        piece = jnp.concatenate([w_expand, w_project], axis=1)
        lines = exchange(to_all(piece, 8), "dp", DEPTH)
        weights = exchange(to_all(lines, 16), BOTH, PLANE).reshape(2, 8, 8, 16, 128)
    with jax.named_scope("small"):
        tap_rows = jnp.pad(dw_kernel.T, ((0, 7), (0, 64)))
        small = jnp.concatenate([jnp.concatenate([se_down, se_up], axis=1), tap_rows], axis=0)
        small = exchange(to_all(small, 16), "tensor")
        small_pairs = small.reshape(8, 2, 80, 128)
    with jax.named_scope("rows"):
        other_x = lax.ppermute(inputs, "tensor", swap)
        other_c = lax.ppermute(cotangent, "tensor", swap)
        last = jnp.where(
            core == 1,
            jnp.stack([inputs[5:7, 0], cotangent[5:7, 0]]),
            jnp.stack([other_x[5:7, 0], other_c[5:7, 0]]),
        )
        first = jnp.where(
            core == 0,
            jnp.stack([inputs[0:2, 0], cotangent[0:2, 0]]),
            jnp.stack([other_x[0:2, 0], other_c[0:2, 0]]),
        )
        top = lax.ppermute(last, "tensor", [(i, i + 2) for i in range(14)])
        bottom = lax.ppermute(first, "tensor", [(i + 2, i) for i in range(14)])
    normed, cot = norm_rows(pos, inputs, other_x, cotangent, other_c, top, bottom)
    act1, slope1, act2, part_p, part_q, proj_grad, w_exp, w_proj, sums = forward(
        pos, weights, small_pairs, normed, cot
    )
    with jax.named_scope("sums"):
        all_sums = exchange(to_all(sums, 16), "tensor")
    coef, vectors = excite(pos, all_sums, small)
    with jax.named_scope("vectors"):
        all_vectors = exchange(to_all(vectors, 16), "dp")
        swish, grad_squeeze = all_vectors[:, 0, :64], all_vectors[:, 0, 64:]
        pooled, grad_excite = all_vectors[:, 1, :64], all_vectors[:, 1, 64:]
        highest = lax.Precision.HIGHEST
        up_grad = jnp.einsum("is,ie->se", swish, grad_excite, precision=highest)
        down_grad = jnp.einsum("is,ie->se", grad_squeeze, pooled, precision=highest)
    grad_expanded, pieces = backward(
        pos, coef, small_pairs, normed, act1, slope1, part_p, part_q, proj_grad
    )
    with jax.named_scope("gradients"):
        pieces = exchange(pieces.reshape(16, 9, 16, 128), BOTH, PLANE)
        partial = jnp.sum(pieces.astype(f32), axis=0).astype(bf16)
        lines = jnp.stack([partial[:8], to_all(partial[8], 8)], axis=1)
        lines = exchange(lines, "dp", DEPTH)
        total = jnp.sum(lines.astype(f32), axis=0)
    with jax.named_scope("finish"):
        partial_out = other_part(pos, coef, w_proj, w_exp, act2, grad_expanded)
        arrived = lax.ppermute(partial_out, "tensor", swap)
        block_out, input_grad = finish(
            pos, coef, w_proj, w_exp, act2, grad_expanded, arrived, inputs, cotangent
        )
    return (
        block_out,
        input_grad,
        total[0, :, :64],
        total[0, :, 64:],
        total[1, :9, :64].T,
        down_grad,
        up_grad,
    )


def solution(mesh):
    placed = (
        P("tensor", "dp", None, None),
        P("tensor", "dp", None, None),
        P("dp", "tensor"),
        P("dp", "tensor"),
        P("tensor", None),
        P(None, "tensor"),
        P(None, "tensor"),
    )
    return jax.shard_map(
        body,
        mesh=mesh,
        in_specs=placed,
        out_specs=(
            P("tensor", "dp", None, None),
            P("tensor", "dp", None, None),
            P("dp", "tensor"),
            P("dp", "tensor"),
            P("tensor", None),
            P(None, "tensor"),
            P(None, "tensor"),
        ),
        check_vma=False,
    )
```

time: 548 us -> 153 us (0.28)
  waiting for transfers between devices: 229 us -> 28.9 us
  blocking collectives: 211 us -> 12.3 us
  matrix products: 50.7 us -> 1.71 us
  starting transfers between devices: 0.2 us -> 45.6 us
  Pallas kernels: 0 us -> 37.4 us
  other arithmetic: 30.8 us -> 4.89 us
  between operations: 14.6 us -> 0.81 us
  local copies, waits for them, and re-layouts: 7.42 us -> 20.6 us
    reduce_scatter x2 -> x0, waiting for transfers between devices: 146 us -> none  [the longest x1 74.9 us: channel_pass(): lax.psum_scatter(jnp.einsum('hbew,ce->hbcw', row_piece, proj_rows, prefer...]
    psum x3 -> x0, blocking collectives: 131 us -> none  [the longest x1 77.5 us: body(): lax.psum(g_kernel.astype(jnp.bfloat16), 'dp').astype(jnp.float32)]
    all_gather x2 -> x0, blocking collectives: 80.2 us -> none  [the longest x1 44.3 us: body(): lax.all_gather(w_expand, 'dp', axis=0, tiled=True)]
    unnamed x6 -> x0, waiting for transfers between devices: 64.5 us -> none
    dot_general x10 -> x2, matrix products: 50.7 us -> 1.71 us  [the longest x1 0.86 us: body(): up_grad = jnp.einsum('is,ie->se', swish, grad_excite, precision=highest)]
    all_to_all x0 -> x6, starting transfers between devices: none -> 39.4 us  [exchange(): lax.all_to_all(pieces, axes, 0, 0, tiled=True, axis_index_groups=members)]
    pallas_call x0 -> x6, Pallas kernels: none -> 37.4 us  [the longest x1 14.2 us: forward(): pl.pallas_call(forward_kernel, grid_spec=pltpu.PrefetchScalarGridSpec(num...]
    all_to_all x0 -> x6, waiting for transfers between devices: none -> 22.5 us  [exchange(): lax.all_to_all(pieces, axes, 0, 0, tiled=True, axis_index_groups=members)]
  transfers between devices with their start and end apart: 5 -> 11, of which waited for: 4 -> 6; matrix products, arithmetic and copies ran while one was open for 5% -> 7% of each run, Pallas kernels for 0% -> 13%
where the time goes in v1:
time: 153 us; the launch traced here: 152 us
  starting transfers between devices  45.6 us (30%)
  Pallas kernels  37.4 us (24%)
  waiting for transfers between devices  28.9 us (19%)
  local copies, waits for them, and re-layouts  20.6 us (13%)
  blocking collectives  12.3 us (8%)
  other arithmetic  4.89 us (3%)
  matrix products  1.71 us (1%)
    all_to_all x6, starting transfers between devices, exchange(): lax.all_to_all(pieces, axes, 0, 0, tiled=True, axis_index_groups=members)  39.4 us
    all_to_all x6, waiting for transfers between devices, exchange(): lax.all_to_all(pieces, axes, 0, 0, tiled=True, axis_index_groups=members)  22.5 us
    unnamed x26, local copies, waits for them, and re-layouts  14.4 us
    pallas_call x1, Pallas kernels, forward(): pl.pallas_call(forward_kernel, grid_spec=pltpu.PrefetchScalarGridSpec(num...  14.2 us
    pallas_call x1, Pallas kernels, backward(): pl.pallas_call(backward_kernel, grid_spec=pltpu.PrefetchScalarGridSpec(nu...  13 us
    all_to_all x1, blocking collectives, exchange(): lax.all_to_all(pieces, axes, 0, 0, tiled=True, axis_index_groups=members)  12.3 us
    ppermute x1, waiting for transfers between devices, body(): bottom = lax.ppermute(first, 'tensor', [(i + 2, i) for i in range(14)])  5.32 us
    ppermute x1, starting transfers between devices, body(): top = lax.ppermute(last, 'tensor', [(i, i + 2) for i in range(14)])  3.82 us
  transfers between devices with their start and end apart: 11, of which 6 were waited for; matrix products, arithmetic and copies ran while one was open for 7% of the time, Pallas kernels for 13%

profile of v1, /device:TPU:2, one launch (start us, length us, event | category | flops | bytes accessed | tf_op | source)
XLA Modules:
  0.0 152.1 jit_solution(6174571824729870382)
XLA Ops:
  0.6 0.1 collective-permute-start.1
  0.7 0.8 pad_maximum_fusion.1
  1.5 0.6 broadcast_in_dim.12
  2.1 8.5 %all-to-all-start = ((bf16[8,16,128]{2,1,0:T(8,128)(2,1)}), bf16[8,16,128]{2,1,0:T(8,128)(2,1)S(1)}, u32[]{:S(2)}, u32[]{:S(2)}) async-start(bf16[8,16,128]{2,1,0:T(8,128)(2,1)} %broadcast_in_dim.12), calls=%async_computation | async-start | bytes 65536 | tf_op jit(solution)/shard_map/weights/all_to_all | solution.py:45
  10.6 0.2 collective-permute-start
  10.8 1.8 %slice_bitcast_fusion.2 = (bf16[1,2,256,128]{3,2,1,0:T(8,128)(2,1)}, bf16[1,2,256,128]{3,2,1,0:T(8,128)(2,1)S(1)}, bf16[1,2,256,128]{3,2,1,0:T(8,128)(2,1)S(1)}, bf16[1,2,256,128]{3,2,1,0:T(8,128)(2,1)}) fusion(bf16[7,1,256,128]{3,2,0,1:T(8,128)(2,1)} %bitcast.60, bf16[7,1,256,128]{3,2,0,1:T(8,128)(2,1)} %bitcast.58), kind=kLoop, calls=%fused_computation.4 | loop fusion | bytes 1048576 | tf_op jit(solution)/shard_map/rows/stack;rows/squeeze | solution.py:588
  12.6 0.8 fusion.1
  13.5 5.2 %all-to-all-done = bf16[8,16,128]{2,1,0:T(8,128)(2,1)S(1)} async-done(((bf16[8,16,128]{2,1,0:T(8,128)(2,1)}), bf16[8,16,128]{2,1,0:T(8,128)(2,1)S(1)}, u32[]{:S(2)}, u32[]{:S(2)}) %all-to-all-start) | async-done | bytes 32800 | tf_op jit(solution)/shard_map/weights/all_to_all | solution.py:45
  18.6 0.8 broadcast_in_dim.14
  19.4 5.9 %all-to-all-start.2 = ((bf16[16,80,128]{2,1,0:T(8,128)(2,1)}), bf16[16,80,128]{2,1,0:T(8,128)(2,1)S(1)}, u32[]{:S(2)}, u32[]{:S(2)}) async-start(bf16[16,80,128]{2,1,0:T(8,128)(2,1)} %broadcast_in_dim.14), calls=%async_computation.2 | async-start | bytes 655360 | tf_op jit(solution)/shard_map/small/all_to_all | solution.py:45
  25.3 0.0 collective-permute-done.1
  25.3 0.0 copy-start
  25.3 0.0 copy-start.1
  25.3 0.0 collective-permute-done
  25.4 5.8 %all-to-all-done.2.small = bf16[16,80,128]{2,1,0:T(8,128)(2,1)S(1)} async-done(((bf16[16,80,128]{2,1,0:T(8,128)(2,1)}), bf16[16,80,128]{2,1,0:T(8,128)(2,1)S(1)}, u32[]{:S(2)}, u32[]{:S(2)}) %all-to-all-start.2) | async-done | bytes 327712 | tf_op jit(solution)/shard_map/small/all_to_all | solution.py:45
  31.2 0.9 broadcast_in_dim.13
  32.1 7.1 %all-to-all-start.1 = ((bf16[16,8,16,128]{3,2,1,0:T(8,128)(2,1)}), bf16[16,8,16,128]{3,2,1,0:T(8,128)(2,1)S(1)}, u32[]{:S(2)}, u32[]{:S(2)}) async-start(bf16[16,8,16,128]{3,2,1,0:T(8,128)(2,1)} %broadcast_in_dim.13), calls=%async_computation.1 | async-start | bytes 1048576 | tf_op jit(solution)/shard_map/weights/all_to_all | solution.py:45
  39.2 1.7 %maximum_select_fusion.1 = bf16[2,2,256,128]{3,2,1,0:T(8,128)(2,1)} fusion(bf16[1,2,256,128]{3,2,1,0:T(8,128)(2,1)} %get-tuple-element.47, bf16[1,2,256,128]{3,2,1,0:T(8,128)(2,1)} %get-tuple-element.56, bf16[1,2,256,128]{3,2,1,0:T(8,128)(2,1)S(1)} %get-tuple-element.43, bf16[1,2,256,128]{3,2,1,0:T(8,128)(2,1)S(1)} %get-tuple-element.41, pred[]{:T(512)S(6)} %eq.7), kind=kLoop, calls=%fused_computation.1 | loop fusion | flops 393216 | bytes 786433 | tf_op jit(solution)/shard_map/rows/jit(_where)/select_n | solution.py:586
  40.9 2.0 %collective-permute-start.3 = (bf16[2,2,256,128]{3,2,1,0:T(8,128)(2,1)}, bf16[2,2,256,128]{3,2,1,0:T(8,128)(2,1)S(1)}, u32[]{:S(2)}, u32[]{:S(2)}) collective-permute-start(bf16[2,2,256,128]{3,2,1,0:T(8,128)(2,1)} %maximum_select_fusion.1), channel_id=1, source_target_pairs={{2,0},{3,1},{4,2},{5,3},{6,4},{7,5},{8,6},{9,7},{10,8},{11,9},{12,... | collective-permute-start | bytes 786440 | tf_op jit(solution)/shard_map/rows/ppermute | solution.py:592
  42.9 0.8 maximum_select_fusion
  43.7 3.8 %collective-permute-start.2 = (bf16[2,2,256,128]{3,2,1,0:T(8,128)(2,1)}, bf16[2,2,256,128]{3,2,1,0:T(8,128)(2,1)S(1)}, u32[]{:S(2)}, u32[]{:S(2)}) collective-permute-start(bf16[2,2,256,128]{3,2,1,0:T(8,128)(2,1)} %maximum_select_fusion), channel_id=1, source_target_pairs={{0,2},{1,3},{2,4},{3,5},{4,6},{5,7},{6,8},{7,9},{8,10},{9,11},{10,... | collective-permute-start | bytes 786440 | tf_op jit(solution)/shard_map/rows/ppermute | solution.py:591
  47.5 0.1 pad_add_fusion.pos
  47.6 5.3 %collective-permute-done.3.bottom = bf16[2,2,256,128]{3,2,1,0:T(8,128)(2,1)S(1)} collective-permute-done((bf16[2,2,256,128]{3,2,1,0:T(8,128)(2,1)}, bf16[2,2,256,128]{3,2,1,0:T(8,128)(2,1)S(1)}, u32[]{:S(2)}, u32[]{:S(2)}) %collective-permute-start.3) | collective-permute-done | bytes 262176 | tf_op jit(solution)/shard_map/rows/ppermute | solution.py:592
  52.9 1.0 collective-permute-done.2.top
  53.9 0.0 copy-done
  53.9 0.0 copy-done.1
  53.9 3.7 %norm_rows.1 = (bf16[256,2304]{1,0:T(8,128)(2,1)S(1)}, bf16[256,2304]{1,0:T(8,128)(2,1)S(1)}) custom-call(s32[4]{0:T(128)S(1)} %pad_add_fusion.pos, bf16[7,1,256,128]{3,2,1,0:T(8,128)(2,1)S(1)} %copy-done, bf16[7,1,256,128]{3,2,1,0:T(8,128)(2,1)S(1)} %bitcast.56, bf16[7,1,256,128]{3,2,1,0:T(8,128)(2,1)S(1)} %copy-done.1, ...), custom_call_target="tpu_custom_call" | custom-call | flops 1000000000 | bytes 8000000 | tf_op jit(solution)/shard_map/norm_rows/pallas_call | solution.py:114
  57.6 0.0 copy-start.7
  57.6 1.0 copy-done.7
  58.7 0.0 copy-start.10
  58.7 1.0 copy-done.10
  59.7 0.0 all-to-all-done.1
  59.7 1.3 copy-done.8
  61.0 1.3 copy-done.11
  62.2 14.2 %forward.1 = (bf16[512,2304]{1,0:T(8,128)(2,1)}, bf16[512,1792]{1,0:T(8,128)(2,1)S(1)}, bf16[512,1792]{1,0:T(8,128)(2,1)}, bf16[512,2048]{1,0:T(8,128)(2,1)}, bf...) custom-call(s32[4]{0:T(128)S(1)} %pad_add_fusion.pos, ...), custom_call_target="tpu_custom_call" | custom-call | flops 10000000000 | bytes 40000000 | tf_op jit(solution)/shard_map/forward/pallas_call | solution.py:243
  76.5 1.3 copy-done.12
  77.8 12.3 %all_to_all.35.sums = f32[16,8,128]{2,1,0:T(8,128)S(1)} all-to-all(f32[16,8,128]{2,1,0:T(8,128)S(1)} %broadcast_in_dim.15), channel_id=1, replica_groups=mesh['dp'=16,'tensor'=16] {'tensor'}, dimensions={0} | all-to-all | bytes 131072 | tf_op jit(solution)/shard_map/sums/all_to_all | solution.py:45
  90.0 1.1 excite.1
  91.1 0.7 broadcast_in_dim.17
  91.8 4.5 %all-to-all-start.6 = ((f32[16,8,128]{2,1,0:T(8,128)}), f32[16,8,128]{2,1,0:T(8,128)S(1)}, u32[]{:S(2)}, u32[]{:S(2)}) async-start(f32[16,8,128]{2,1,0:T(8,128)} %broadcast_in_dim.17), calls=%async_computation.6 | async-start | bytes 131072 | tf_op jit(solution)/shard_map/vectors/all_to_all | solution.py:45
  96.2 0.0 copy-start.9
  96.2 1.3 copy-done.9
  97.5 13.0 %backward.1 = (bf16[512,1792]{1,0:T(8,128)(2,1)S(1)}, bf16[2,8,9,16,128]{4,3,2,1,0:T(8,128)(2,1)}) custom-call(s32[4]{0:T(128)S(1)} %pad_add_fusion.pos, f32[8,512]{1,0:T(8,128)S(1)} %get-tuple-element.27.coef, bf16[8,2,80,128]{3,2,1,0:T(8,128)(2,1)S(1)} %bitcast.53, bf16[256,2304]{1,0:T(8,128)(2,1)S(1)} %copy-done.9, ...), custom_call_target="tpu_custom_call" | custom-call | flops 8000000000 | bytes 30000000 | tf_op jit(solution)/shard_map/backward/pallas_call | solution.py:444
  110.5 1.3 copy-done.4
  111.7 0.0 all-to-all-done.6
  111.7 6.9 %all-to-all-start.4 = ((bf16[16,9,16,128]{3,2,1,0:T(8,128)(2,1)}), bf16[16,9,16,128]{3,2,1,0:T(8,128)(2,1)S(1)}, u32[]{:S(2)}, u32[]{:S(2)}) async-start(bf16[16,9,16,128]{3,2,1,0:T(8,128)(2,1)} %bitcast.23), calls=%async_computation.4 | async-start | bytes 1179648 | tf_op jit(solution)/shard_map/gradients/all_to_all | solution.py:45
  118.6 1.5 copy-done.2
  120.1 1.5 copy-done.5
  121.6 2.6 %other_part.1 = bf16[2,7,256,128]{3,2,1,0:T(8,128)(2,1)} custom-call(s32[4]{0:T(128)S(1)} %pad_add_fusion.pos, f32[8,512]{1,0:T(8,128)S(1)} %get-tuple-element.27.coef, bf16[256,512]{1,0:T(8,128)(2,1)S(1)} %get-tuple-element.28.w_proj, bf16[256,512]{1,0:T(8,128)(2,1)S(1)} %get-tuple-element.29.w_exp, bf16[512,1792]{1,0:T(8,128)(2,1)S(1)} %copy-done.2, ...), custom_call_target="tpu_custom_call" | custom-call | flops 2000000000 | bytes 4000000 | tf_op jit(solution)/shard_map/finish/other_part/pallas_call | solution.py:494
  124.2 0.0 collective-permute-start.4
  124.3 0.1 fusion.2
  124.4 0.9 fusion.4
  125.2 4.0 %all-to-all-done.4 = bf16[16,9,16,128]{3,2,1,0:T(8,128)(2,1)S(1)} async-done(((bf16[16,9,16,128]{3,2,1,0:T(8,128)(2,1)}), bf16[16,9,16,128]{3,2,1,0:T(8,128)(2,1)S(1)}, u32[]{:S(2)}, u32[]{:S(2)}) %all-to-all-start.4) | async-done | bytes 589856 | tf_op jit(solution)/shard_map/gradients/all_to_all | solution.py:45
  129.2 0.1 reduce_sum.21
  129.3 0.6 pad_maximum_fusion
  130.0 6.7 %all-to-all-start.5 = ((bf16[8,2,16,128]{3,2,1,0:T(8,128)(2,1)}), bf16[8,2,16,128]{3,2,1,0:T(8,128)(2,1)S(1)}, u32[]{:S(2)}, u32[]{:S(2)}) async-start(bf16[8,2,16,128]{3,2,1,0:T(8,128)(2,1)} %pad_maximum_fusion), calls=%async_computation.5 | async-start | bytes 131072 | tf_op jit(solution)/shard_map/gradients/all_to_all | solution.py:45
  136.6 0.8 fusion.3
  137.5 7.5 %all-to-all-done.5 = bf16[8,2,16,128]{3,2,1,0:T(8,128)(2,1)S(1)} async-done(((bf16[8,2,16,128]{3,2,1,0:T(8,128)(2,1)}), bf16[8,2,16,128]{3,2,1,0:T(8,128)(2,1)S(1)}, u32[]{:S(2)}, u32[]{:S(2)}) %all-to-all-start.5) | async-done | bytes 65568 | tf_op jit(solution)/shard_map/gradients/all_to_all | solution.py:45
  145.0 0.6 slice_bitcast_fusion.9
  145.6 0.7 slice_bitcast_fusion.10
  146.3 0.0 collective-permute-done.4.arrived
  146.3 1.5 copy-done.3
  147.8 1.5 copy-done.6
  149.3 2.8 %finish.1 = (bf16[7,1,256,128]{3,2,1,0:T(8,128)(2,1)}, bf16[7,1,256,128]{3,2,1,0:T(8,128)(2,1)}) custom-call(s32[4]{0:T(128)S(1)} %pad_add_fusion.pos, f32[8,512]{1,0:T(8,128)S(1)} %get-tuple-element.27.coef, bf16[256,512]{1,0:T(8,128)(2,1)S(1)} %get-tuple-element.28.w_proj, bf16[256,512]{1,0:T(8,128)(2,1)S(1)} %get-tuple-element.29.w_exp, ...), custom_call_target="tpu_custom_call" | custom-call | flops 2000000000 | bytes 6000000 | tf_op jit(solution)/shard_map/finish/finish/pallas_call | solution.py:539
  (15 shorter events, 0.1 us)
Async XLA Ops:
  0.6 24.6 %collective-permute-start.1 = (bf16[7,1,256,128]{3,2,0,1:T(8,128)(2,1)}, bf16[7,1,256,128]{3,2,0,1:T(8,128)(2,1)S(1)}, u32[]{:S(2)}, u32[]{:S(2)}) collective-permute-start(bf16[7,1,256,128]{3,2,0,1:T(8,128)(2,1)} %bitcast.59), channel_id=1, source_target_pairs={{0,1},{1,0},{2,3},{3,2},{4,5},{5,4},{6,7},{7,6},{8,9},{9,8},{10,11... | collective-permute-start | bytes 1376264 | tf_op jit(solution)/shard_map/rows/ppermute | solution.py:580
  2.1 16.5 %all-to-all-start = ((bf16[8,16,128]{2,1,0:T(8,128)(2,1)}), bf16[8,16,128]{2,1,0:T(8,128)(2,1)S(1)}, u32[]{:S(2)}, u32[]{:S(2)}) async-start(bf16[8,16,128]{2,1,0:T(8,128)(2,1)} %broadcast_in_dim.12), calls=%async_computation | async-start | bytes 65536 | tf_op jit(solution)/shard_map/weights/all_to_all | solution.py:45
  10.6 14.7 %collective-permute-start = (bf16[7,1,256,128]{3,2,0,1:T(8,128)(2,1)}, bf16[7,1,256,128]{3,2,0,1:T(8,128)(2,1)S(1)}, u32[]{:S(2)}, u32[]{:S(2)}) collective-permute-start(bf16[7,1,256,128]{3,2,0,1:T(8,128)(2,1)} %bitcast.57), channel_id=1, source_target_pairs={{0,1},{1,0},{2,3},{3,2},{4,5},{5,4},{6,7},{7,6},{8,9},{9,8},{10,11... | collective-permute-start | bytes 1376264 | tf_op jit(solution)/shard_map/rows/ppermute | solution.py:579
  19.4 11.8 %all-to-all-start.2 = ((bf16[16,80,128]{2,1,0:T(8,128)(2,1)}), bf16[16,80,128]{2,1,0:T(8,128)(2,1)S(1)}, u32[]{:S(2)}, u32[]{:S(2)}) async-start(bf16[16,80,128]{2,1,0:T(8,128)(2,1)} %broadcast_in_dim.14), calls=%async_computation.2 | async-start | bytes 655360 | tf_op jit(solution)/shard_map/small/all_to_all | solution.py:45
  25.3 28.6 %copy-start = (bf16[7,1,256,128]{3,2,1,0:T(8,128)(2,1)S(1)}, bf16[7,1,256,128]{3,2,1,0:T(8,128)(2,1)}, u32[]{:S(2)}) copy-start(bf16[7,1,256,128]{3,2,1,0:T(8,128)(2,1)} %x.3) | copy-start | bytes 1376260
  25.3 28.6 %copy-start.1 = (bf16[7,1,256,128]{3,2,1,0:T(8,128)(2,1)S(1)}, bf16[7,1,256,128]{3,2,1,0:T(8,128)(2,1)}, u32[]{:S(2)}) copy-start(bf16[7,1,256,128]{3,2,1,0:T(8,128)(2,1)} %c.1) | copy-start | bytes 1376260
  32.1 27.6 %all-to-all-start.1 = ((bf16[16,8,16,128]{3,2,1,0:T(8,128)(2,1)}), bf16[16,8,16,128]{3,2,1,0:T(8,128)(2,1)S(1)}, u32[]{:S(2)}, u32[]{:S(2)}) async-start(bf16[16,8,16,128]{3,2,1,0:T(8,128)(2,1)} %broadcast_in_dim.13), calls=%async_computation.1 | async-start | bytes 1048576 | tf_op jit(solution)/shard_map/weights/all_to_all | solution.py:45
  40.9 12.0 %collective-permute-start.3 = (bf16[2,2,256,128]{3,2,1,0:T(8,128)(2,1)}, bf16[2,2,256,128]{3,2,1,0:T(8,128)(2,1)S(1)}, u32[]{:S(2)}, u32[]{:S(2)}) collective-permute-start(bf16[2,2,256,128]{3,2,1,0:T(8,128)(2,1)} %maximum_select_fusion.1), channel_id=1, source_target_pairs={{2,0},{3,1},{4,2},{5,3},{6,4},{7,5},{8,6},{9,7},{10,8},{11,9},{12,... | collective-permute-start | bytes 786440 | tf_op jit(solution)/shard_map/rows/ppermute | solution.py:592
  43.7 10.3 %collective-permute-start.2 = (bf16[2,2,256,128]{3,2,1,0:T(8,128)(2,1)}, bf16[2,2,256,128]{3,2,1,0:T(8,128)(2,1)S(1)}, u32[]{:S(2)}, u32[]{:S(2)}) collective-permute-start(bf16[2,2,256,128]{3,2,1,0:T(8,128)(2,1)} %maximum_select_fusion), channel_id=1, source_target_pairs={{0,2},{1,3},{2,4},{3,5},{4,6},{5,7},{6,8},{7,9},{8,10},{9,11},{10,... | collective-permute-start | bytes 786440 | tf_op jit(solution)/shard_map/rows/ppermute | solution.py:591
  57.6 1.0 copy-start.7
  58.7 1.0 copy-start.10
  59.7 1.3 copy-start.8
  61.0 1.3 copy-start.11
  76.5 1.3 copy-start.12
  91.8 20.0 %all-to-all-start.6 = ((f32[16,8,128]{2,1,0:T(8,128)}), f32[16,8,128]{2,1,0:T(8,128)S(1)}, u32[]{:S(2)}, u32[]{:S(2)}) async-start(f32[16,8,128]{2,1,0:T(8,128)} %broadcast_in_dim.17), calls=%async_computation.6 | async-start | bytes 131072 | tf_op jit(solution)/shard_map/vectors/all_to_all | solution.py:45
  96.2 1.3 copy-start.9
  110.5 1.3 copy-start.4
  111.7 17.5 %all-to-all-start.4 = ((bf16[16,9,16,128]{3,2,1,0:T(8,128)(2,1)}), bf16[16,9,16,128]{3,2,1,0:T(8,128)(2,1)S(1)}, u32[]{:S(2)}, u32[]{:S(2)}) async-start(bf16[16,9,16,128]{3,2,1,0:T(8,128)(2,1)} %bitcast.23), calls=%async_computation.4 | async-start | bytes 1179648 | tf_op jit(solution)/shard_map/gradients/all_to_all | solution.py:45
  118.6 1.5 copy-start.2
  120.1 1.5 copy-start.5
  124.2 22.1 %collective-permute-start.4 = (bf16[2,7,256,128]{3,2,1,0:T(8,128)(2,1)}, bf16[2,7,256,128]{3,2,1,0:T(8,128)(2,1)S(1)}, u32[]{:S(2)}, u32[]{:S(2)}) collective-permute-start(bf16[2,7,256,128]{3,2,1,0:T(8,128)(2,1)} %other_part.1), channel_id=1, source_target_pairs={{0,1},{1,0},{2,3},{3,2},{4,5},{5,4},{6,7},{7,6},{8,9},{9,8},{10,11... | collective-permute-start | bytes 2752520 | tf_op jit(solution)/shard_map/finish/ppermute | solution.py:618
  130.0 15.0 %all-to-all-start.5 = ((bf16[8,2,16,128]{3,2,1,0:T(8,128)(2,1)}), bf16[8,2,16,128]{3,2,1,0:T(8,128)(2,1)S(1)}, u32[]{:S(2)}, u32[]{:S(2)}) async-start(bf16[8,2,16,128]{3,2,1,0:T(8,128)(2,1)} %pad_maximum_fusion), calls=%async_computation.5 | async-start | bytes 131072 | tf_op jit(solution)/shard_map/gradients/all_to_all | solution.py:45
  146.3 1.5 copy-start.3
  147.8 1.5 copy-start.6

commit v2 on v0

v2 whole, which is shorter than its diff:
```python
import jax
import jax.numpy as jnp
from jax import lax
from jax.experimental import pallas as pl
from jax.experimental.pallas import tpu as pltpu
from jax.sharding import PartitionSpec as P

bf16 = jnp.bfloat16
f32 = jnp.float32

gelu_scale = 0.7978845608
gelu_cubic = 0.044715

CH = 256
HALF = 512
SQ = 64
COLS = 128
ROWS = 14
EXT = ROWS + 4
CELLS = 112 * 128
BLOCKS = 4
GROUP = 16
BOTH = ("dp", "tensor")
VMEM = 16 * 1024 * 1024
SMALL = 10**5


def groups(count, steps):
    seen, found = set(), []
    for first in range(count):
        if first in seen:
            continue
        members = [first]
        for step in steps:
            members = members + [member ^ step for member in members]
        members = sorted(members)
        seen.update(members)
        found.append(members)
    return found


def exchange(pieces, axes, steps=None):
    members = None
    if steps is not None:
        members = groups(256 if axes == BOTH else 16, steps)
    return lax.all_to_all(pieces, axes, 0, 0, tiled=True, axis_index_groups=members)


def to_all(piece, count):
    return jnp.broadcast_to(piece[None], (count,) + piece.shape)


PLANE = (2, 4, 8, 16)
DEPTH = (2, 4, 8)


def gelu_pair(values):
    square = values * values
    inner = values * (gelu_scale + (gelu_scale * gelu_cubic) * square)
    part = 0.5 + 0.5 * jnp.tanh(inner)
    act = values * part
    slope = part + act * (1.0 - part) * (
        2.0 * gelu_scale + (6.0 * gelu_scale * gelu_cubic) * square
    )
    return act, slope


def params(**more):
    return pltpu.CompilerParams(vmem_limit_bytes=VMEM, **more)


def cost(flops, size):
    return pl.CostEstimate(flops=flops, bytes_accessed=size, transcendentals=0)


def join_low(first, second, low):
    return jnp.where(low, first, pltpu.roll(second, 64, 1))


def join_high(first, second, low):
    return jnp.where(low, pltpu.roll(first, 64, 1), second)


def full(*shape):
    return pl.BlockSpec(shape, lambda *unused: (0,) * len(shape))


def in_vmem(count):
    return [pl.BlockSpec(memory_space=pltpu.VMEM)] * count


def in_hbm(count):
    return [pl.BlockSpec(memory_space=pltpu.HBM)] * count


def held(shape, kind):
    return pltpu.VMEM(shape, kind)


def kept(*arrays):
    return [pltpu.with_memory_space_constraint(array, pltpu.VMEM) for array in arrays]


def far_memory(*arrays):
    return [pltpu.with_memory_space_constraint(array, pltpu.HBM) for array in arrays]


def tensor_place():
    place = lax.axis_index("tensor")
    return lax.rem(place, 2), lax.div(place, 2)


def image_place():
    image = lax.axis_index("dp")
    return lax.div(image, 2), lax.rem(image, 2)


def lanes_of(shape):
    return lax.broadcasted_iota(jnp.int32, shape, 1)


def down_rows(row):
    return jnp.broadcast_to(row, (128, 128)).T


def start_kernel(
    x, c, w_expand, w_project, dw_rows, se_down, se_up,
    packed, edge,
    tall, wide, expand_in, project_in, dw_in, down_in, up_in, sems,
):
    core, _ = tensor_place()
    z, yh = image_place()
    pairs = (
        (w_expand, expand_in),
        (w_project, project_in),
        (dw_rows, dw_in),
        (se_down, down_in),
        (se_up, up_in),
        (x.at[pl.ds(5 * core, 2)], edge.at[0]),
        (c.at[pl.ds(5 * core, 2)], edge.at[1]),
    )
    copies = [pltpu.make_async_copy(a, b, sems.at[i]) for i, (a, b) in enumerate(pairs)]
    for copy in copies:
        copy.start()
    wide[0:16, :] = jnp.zeros((16, 128), f32)
    for copy in copies[:5]:
        copy.wait()
    wide[0:9, 0:64] = dw_in[...].astype(f32)
    tall[0:64, 0:64] = down_in[...].astype(f32)
    tall[0:64, 64:128] = up_in[...].astype(f32)
    wide[16:32, 0:64] = expand_in[...].astype(f32)
    wide[16:32, 64:128] = project_in[...].astype(f32)
    squeeze_rows = tall[pl.ds(yh * 32 + z * 4, 4), :]
    tap_row = wide[pl.ds(yh * 8 + z, 1), :]
    tall[16:32, :] = jnp.zeros((16, 128), f32)
    tall[16:20, :] = squeeze_rows
    tall[20:21, :] = tap_row
    piece = jnp.concatenate([wide[16:32, :], tall[16:32, :]], axis=0).astype(bf16)
    for other in range(8):
        packed[other] = piece
    for copy in copies[5:]:
        copy.wait()


def start(x, c, w_expand, w_project, dw_rows, se_down, se_up):
    return pl.pallas_call(
        start_kernel,
        in_specs=in_hbm(7),
        out_specs=in_vmem(2),
        out_shape=[
            jax.ShapeDtypeStruct((8, 32, 128), bf16),
            held((2, 2, 1, CH, COLS), bf16),
        ],
        scratch_shapes=[
            pltpu.VMEM((64, 128), f32),
            pltpu.VMEM((32, 128), f32),
            pltpu.VMEM((16, 64), bf16),
            pltpu.VMEM((16, 64), bf16),
            pltpu.VMEM((9, 64), bf16),
            pltpu.VMEM((64, 64), bf16),
            pltpu.VMEM((64, 64), bf16),
            pltpu.SemaphoreType.DMA((7,)),
        ],
        compiler_params=params(),
        cost_estimate=cost(SMALL, SMALL),
        name="start",
    )(*far_memory(x, c, w_expand, w_project, dw_rows, se_down, se_up))


def spread_kernel(lines, first, second, out, squeeze_rows, tap_rows):
    tap_rows[...] = jnp.zeros((16, 128), f32)
    for z in range(8):
        small = lines[z, 16:32, :].astype(f32)
        squeeze_rows[z * 4 : z * 4 + 4, :] = small[0:4]
        tap_rows[z : z + 1, :] = small[4:5]
    squeeze_piece = squeeze_rows[...].astype(bf16)
    tap_piece = tap_rows[...].astype(bf16)
    for other in range(16):
        for z in range(8):
            out[other, z] = lines[z, 0:16, :]
        out[other, 8] = squeeze_piece[0:16]
        out[other, 9] = squeeze_piece[16:32]
        out[other, 10] = tap_piece


def spread(lines, first, second):
    return pl.pallas_call(
        spread_kernel,
        in_specs=in_vmem(3),
        out_specs=in_vmem(1)[0],
        out_shape=jax.ShapeDtypeStruct((16, 11, 16, 128), bf16),
        scratch_shapes=[pltpu.VMEM((32, 128), f32), pltpu.VMEM((16, 128), f32)],
        compiler_params=params(),
        cost_estimate=cost(SMALL, SMALL),
        name="spread",
    )(lines, first, second)


def normal_of(x):
    values = x.astype(f32)
    center = values - jnp.mean(values, axis=0, keepdims=True)
    inv_std = lax.rsqrt(jnp.mean(center * center, axis=0, keepdims=True) + 1e-05)
    return (center * inv_std).astype(bf16)


def lane_block(row):
    return pl.ds(pl.multiple_of(row * 128, 128), 128)


def main_norm_kernel(own_x, other_x, own_c, other_c, normed, cot, done):
    done[...] = jnp.zeros((8, 128), f32)
    core, _ = tensor_place()
    for x, c, first in ((own_x, own_c, 7 * core), (other_x, other_c, 7 - 7 * core)):
        for row in range(7):
            normed[:, lane_block(first + row)] = normal_of(x[row, 0])
            cot[:, lane_block(first + row)] = c[row, 0]


def main_norm(own_x, other_x, own_c, other_c):
    return pl.pallas_call(
        main_norm_kernel,
        in_specs=in_vmem(4),
        out_specs=in_vmem(3),
        out_shape=[held((CH, ROWS * COLS), bf16)] * 2 + [jax.ShapeDtypeStruct((8, 128), f32)],
        compiler_params=params(),
        cost_estimate=cost(SMALL, SMALL),
        name="main_norm",
    )(own_x, other_x, own_c, other_c)


def edge_norm_kernel(near, far, normed, cot, done):
    done[...] = jnp.zeros((8, 128), f32)
    core, _ = tensor_place()
    for edge, first in ((near, 2 * core), (far, 2 - 2 * core)):
        for row in range(2):
            normed[:, lane_block(first + row)] = normal_of(edge[0, row, 0])
            cot[:, lane_block(first + row)] = edge[1, row, 0]


def edge_norm(near, far):
    return pl.pallas_call(
        edge_norm_kernel,
        in_specs=in_vmem(2),
        out_specs=in_vmem(3),
        out_shape=[held((CH, 4 * COLS), bf16)] * 2 + [jax.ShapeDtypeStruct((8, 128), f32)],
        compiler_params=params(),
        cost_estimate=cost(SMALL, SMALL),
        name="edge_norm",
    )(near, far)


def spread_taps(sources, taps, place, masked):
    low = lanes_of((16, 128)) < 64
    early = join_low(sources[0][0].astype(f32), sources[0][1].astype(f32), low)
    late = join_low(sources[1][0].astype(f32), sources[1][1].astype(f32), low)
    lane = lanes_of((128, 128))
    for tap in range(9):
        spread = down_rows(early[tap : tap + 1, :] if tap < 8 else late[0:1, :])
        if masked and tap % 3 == 0:
            spread = jnp.where(lane == 0, 0.0, spread)
        if masked and tap % 3 == 2:
            spread = jnp.where(lane == 127, 0.0, spread)
        taps[tap, place : place + 128, :] = spread


def forward_kernel(
    weights, normed, cot, normed_edge, cot_edge,
    normed_out, act1, slope1, act2, part_p, part_q, proj_grad, w_exp, w_proj, squeeze_rows, sums,
    expanded, grad_hidden, taps, pool, gate,
):
    _, chip = tensor_place()
    normed_out[...] = normed[...]
    low = lanes_of((16, 128)) < 64
    for block in range(BLOCKS):
        cells = slice(block * 128, block * 128 + 128)
        for z in range(8):
            for yh in range(2):
                first = weights[yh, 2 * block, z].astype(f32)
                second = weights[yh, 2 * block + 1, z].astype(f32)
                rows = slice((z * 2 + yh) * 16, (z * 2 + yh) * 16 + 16)
                w_exp[rows, cells] = join_low(first, second, low).astype(bf16)
                w_proj[rows, cells] = join_high(first, second, low).astype(bf16)
        spread_taps(
            [[weights[yh, 2 * block + j, 10] for j in range(2)] for yh in range(2)],
            taps,
            block * 128,
            True,
        )
    squeeze_rows[...] = weights[:, :, 8:10]
    w_exp_t = w_exp[...].astype(f32).T.astype(bf16)
    w_proj_t = w_proj[...].astype(f32).T.astype(bf16)

    def multiply(weight, source, target, place):
        target[:, place * 128 : place * 128 + source.shape[1]] = jnp.dot(
            weight, source, preferred_element_type=f32
        ).astype(bf16)

    multiply(w_exp_t, normed_edge[:, 0:256], expanded, 0)
    multiply(w_exp_t, normed_edge[:, 256:512], expanded, ROWS + 2)
    multiply(w_proj_t, cot_edge[:, 128:256], grad_hidden, 0)
    multiply(w_proj_t, cot_edge[:, 256:384], grad_hidden, ROWS + 1)
    for part in range(ROWS // 2):
        cells = slice(part * 256, part * 256 + 256)
        multiply(w_exp_t, normed[:, cells], expanded, 2 + 2 * part)
        multiply(w_proj_t, cot[:, cells], grad_hidden, 1 + 2 * part)
    first_chip = jnp.where(chip > 0, 1.0, 0.0)
    last_chip = jnp.where(chip < 7, 1.0, 0.0)

    def one_group(index, carry):
        rows = pl.ds(pl.multiple_of(index * GROUP, GROUP), GROUP)
        tap = [taps[k, rows, :] for k in range(9)]
        running = {}
        pool_sum = jnp.zeros((GROUP, COLS), f32)
        gate_sum = jnp.zeros((GROUP, COLS), f32)
        for h in range(EXT):
            value = expanded[rows, h * 128 : h * 128 + 128].astype(f32)
            act, slope = gelu_pair(value)
            act1[rows, h * 128 : h * 128 + 128] = act.astype(bf16)
            if 2 <= h < ROWS + 2:
                slope1[rows, (h - 2) * 128 : (h - 1) * 128] = slope.astype(bf16)
            left = pltpu.roll(act, 1, 1)
            right = pltpu.roll(act, 127, 1)
            for i in range(3):
                m = h + 1 - i
                if not 1 <= m <= ROWS + 2:
                    continue
                term = tap[3 * i] * left + tap[3 * i + 1] * act + tap[3 * i + 2] * right
                running[m] = running[m] + term if m in running else term
            m = h - 1
            if not 1 <= m <= ROWS + 2:
                continue
            act, slope = gelu_pair(running.pop(m))
            grad = grad_hidden[rows, (m - 1) * 128 : m * 128].astype(f32)
            if m == 1:
                slope = slope * first_chip
            if m == ROWS + 2:
                slope = slope * last_chip
            part_q[rows, (m - 1) * 128 : m * 128] = slope.astype(bf16)
            part_p[rows, (m - 1) * 128 : m * 128] = (slope * grad).astype(bf16)
            if 2 <= m < ROWS + 2:
                act2[rows, (m - 2) * 128 : (m - 1) * 128] = act.astype(bf16)
                pool_sum = pool_sum + act
                gate_sum = gate_sum + act * grad
        pool[rows, :] = pool_sum
        gate[rows, :] = gate_sum
        return carry

    lax.fori_loop(0, HALF // GROUP, one_group, 0)
    for block in range(BLOCKS):
        cells = slice(block * 128, block * 128 + 128)
        pool_row = jnp.sum(pool[cells, :].T, axis=0, keepdims=True)
        gate_row = jnp.sum(gate[cells, :].T, axis=0, keepdims=True)
        for other in range(16):
            sums[other, block : block + 1, :] = pool_row
            sums[other, BLOCKS + block : BLOCKS + block + 1, :] = gate_row
    proj_grad[...] = lax.dot_general(
        cot[...], act2[...], (((1,), (1,)), ((), ())), preferred_element_type=f32
    )


def forward(weights, normed, cot, normed_edge, cot_edge):
    return pl.pallas_call(
        forward_kernel,
        in_specs=in_vmem(5),
        out_specs=in_vmem(11),
        scratch_shapes=[
            pltpu.VMEM((HALF, EXT * COLS), bf16),
            pltpu.VMEM((HALF, (ROWS + 2) * COLS), bf16),
            pltpu.VMEM((9, HALF, 128), f32),
            pltpu.VMEM((HALF, 128), f32),
            pltpu.VMEM((HALF, 128), f32),
        ],
        out_shape=[
            held((CH, ROWS * COLS), bf16),
            held((HALF, EXT * COLS), bf16),
            held((HALF, ROWS * COLS), bf16),
            held((HALF, ROWS * COLS), bf16),
            held((HALF, (ROWS + 2) * COLS), bf16),
            held((HALF, (ROWS + 2) * COLS), bf16),
            held((CH, HALF), f32),
            held((CH, HALF), bf16),
            held((CH, HALF), bf16),
            held((2, 8, 2, 16, 128), bf16),
            jax.ShapeDtypeStruct((16, 8, 128), f32),
        ],
        compiler_params=params(),
        cost_estimate=cost(10**9, 50 * 10**6),
        name="forward",
    )(weights, *kept(normed, cot, normed_edge, cot_edge))


def excite_kernel(sums, own_rows, other_rows, coef):
    low = lanes_of((SQ, 128)) < 64
    totals = []
    for half in range(2):
        total = sums[half]
        for other in range(1, 8):
            total = total + sums[2 * other + half]
        totals.append(total)
    core, _ = tensor_place()
    is_first = core == 0
    ordered = (
        jnp.where(is_first, totals[0], totals[1]),
        jnp.where(is_first, totals[1], totals[0]),
    )
    pooled, grad_gate, down, up = [], [], [], []
    for total, rows in zip(ordered, (own_rows, other_rows)):
        for block in range(BLOCKS):
            pooled.append(total[block : block + 1] * (1.0 / CELLS))
            grad_gate.append(total[BLOCKS + block : BLOCKS + block + 1])
            halves = [
                jnp.concatenate(
                    [rows[yh, 2 * block + j, part].astype(f32) for yh in range(2) for part in range(2)],
                    axis=0,
                )
                for j in range(2)
            ]
            down.append(join_low(halves[0], halves[1], low))
            up.append(join_high(halves[0], halves[1], low))
    count = 2 * BLOCKS
    squeeze = sum(jnp.sum(down[b] * pooled[b], axis=1, keepdims=True) for b in range(count))
    sig = 1.0 / (1.0 + jnp.exp(-squeeze))
    swish = squeeze * sig
    gating, grad_excite = [], []
    for b in range(count):
        logit = jnp.sum(up[b] * swish, axis=0, keepdims=True)
        gating.append(1.0 / (1.0 + jnp.exp(-logit)))
        grad_excite.append(grad_gate[b] * gating[b] * (1.0 - gating[b]))
    grad_swish = sum(jnp.sum(up[b] * grad_excite[b], axis=1, keepdims=True) for b in range(count))
    grad_squeeze = grad_swish * sig * (1.0 + squeeze * (1.0 - sig))
    side = jnp.concatenate([swish, grad_squeeze], axis=0)
    side_row = jnp.broadcast_to(side, (128, 128)).T[0:1, :]
    for b in range(BLOCKS):
        cells = slice(b * 128, b * 128 + 128)
        grad_pooled = jnp.sum(down[b] * grad_squeeze, axis=0, keepdims=True)
        coef[0:1, cells] = gating[b]
        coef[1:2, cells] = grad_pooled * (1.0 / CELLS)
        coef[2:3, cells] = pooled[b]
        coef[3:4, cells] = grad_excite[b]
        coef[4:5, cells] = side_row
    coef[5:8, :] = jnp.zeros((3, HALF), f32)


def excite(sums, own_rows, other_rows):
    return pl.pallas_call(
        excite_kernel,
        in_specs=in_vmem(3),
        out_specs=in_vmem(1)[0],
        out_shape=held((8, HALF), f32),
        compiler_params=params(),
        cost_estimate=cost(SMALL, 4 * 10**6),
        name="excite",
    )(sums, *kept(own_rows), other_rows)


def backward_kernel(
    coef, weights, normed, act1, slope1, part_p, part_q, proj_grad, w_proj, w_exp, act2,
    grad_out, pieces, other_out,
    grad_expanded, copied,
    taps, gates, pools, kernel_sums, tap_rows,
):
    for block in range(BLOCKS):
        cells = slice(block * 128, block * 128 + 128)
        spread_taps(
            [[weights[yh, 2 * block + j, 10] for j in range(2)] for yh in range(2)],
            taps,
            block * 128,
            False,
        )
        gates[cells, :] = down_rows(coef[0:1, cells])
        pools[cells, :] = down_rows(coef[1:2, cells])
    lane = lanes_of((GROUP, COLS))

    def one_group(index, carry):
        rows = pl.ds(pl.multiple_of(index * GROUP, GROUP), GROUP)
        tap = [taps[k, rows, :] for k in range(9)]
        gating = gates[rows, :]
        pooled = pools[rows, :]
        running = {}
        sums = [None] * 9
        for m in range(1, ROWS + 3):
            cells = slice((m - 1) * 128, m * 128)
            grad = part_p[rows, cells].astype(f32) * gating + part_q[rows, cells].astype(f32) * pooled
            turned = (
                jnp.where(lane == 127, 0.0, pltpu.roll(grad, 127, 1)),
                grad,
                jnp.where(lane == 0, 0.0, pltpu.roll(grad, 1, 1)),
            )
            for i in range(3):
                h = m + i - 1
                if 2 <= h < ROWS + 2:
                    term = tap[3 * i] * turned[0] + tap[3 * i + 1] * turned[1] + tap[3 * i + 2] * turned[2]
                    running[h] = running[h] + term if h in running else term
                if 2 <= m < ROWS + 2:
                    act = act1[rows, h * 128 : h * 128 + 128].astype(f32)
                    for j in range(3):
                        term = turned[j] * act
                        k = 3 * i + j
                        sums[k] = term if sums[k] is None else sums[k] + term
            h = m - 1
            if 2 <= h < ROWS + 2:
                out = slice((h - 2) * 128, (h - 1) * 128)
                grad_expanded[rows, out] = (running.pop(h) * slope1[rows, out].astype(f32)).astype(bf16)
        for k in range(9):
            kernel_sums[k, rows, :] = sums[k]
        return carry

    lax.fori_loop(0, HALF // GROUP, one_group, 0)
    copy_out = pltpu.make_async_copy(grad_expanded, grad_out, copied)
    copy_out.start()
    core, _ = tensor_place()
    cells = pl.ds(pl.multiple_of((1 - core) * (7 * COLS), 7 * COLS), 7 * COLS)
    gated = (w_proj[...].astype(f32) * coef[0:1, :]).astype(bf16)
    projected = jnp.dot(gated, act2[:, cells], preferred_element_type=f32).astype(bf16)
    grad = jnp.dot(w_exp[...], grad_expanded[:, cells], preferred_element_type=f32).astype(bf16)
    for row in range(7):
        other_out[0, row] = projected[:, row * 128 : row * 128 + 128]
        other_out[1, row] = grad[:, row * 128 : row * 128 + 128]
    exp_grad = lax.dot_general(
        normed[...], grad_expanded[...], (((1,), (1,)), ((), ())), preferred_element_type=f32
    )
    low = lanes_of((CH, 128)) < 64
    tap_low = lanes_of((1, 128)) < 64
    tap_rows[...] = jnp.zeros((16, 128), f32)
    for block in range(BLOCKS):
        cells = slice(block * 128, block * 128 + 128)
        scaled = proj_grad[:, cells] * coef[0:1, cells]
        first = join_low(exp_grad[:, cells], scaled, low).astype(bf16)
        second = join_high(exp_grad[:, cells], scaled, low).astype(bf16)
        for k in range(9):
            tap_rows[k : k + 1, :] = jnp.sum(kernel_sums[k, cells, :].T, axis=0, keepdims=True)
        tap_rows[9:10, :] = join_low(coef[2:3, cells], coef[3:4, cells], tap_low)
        tap_rows[10:11, :] = coef[4:5, cells]
        first_taps = tap_rows[...].astype(bf16)
        tap_rows[0:9, :] = pltpu.roll(tap_rows[...], 64, 1)[0:9]
        tap_rows[9:10, :] = join_high(coef[2:3, cells], coef[3:4, cells], tap_low)
        second_taps = tap_rows[...].astype(bf16)
        for yh in range(2):
            for z in range(8):
                rows = slice((z * 2 + yh) * 16, (z * 2 + yh) * 16 + 16)
                pieces[yh, 2 * block, z] = first[rows]
                pieces[yh, 2 * block + 1, z] = second[rows]
            pieces[yh, 2 * block, 8] = first_taps
            pieces[yh, 2 * block + 1, 8] = second_taps
    copy_out.wait()


def backward(coef, weights, normed, act1, slope1, part_p, part_q, proj_grad, w_proj, w_exp, act2):
    return pl.pallas_call(
        backward_kernel,
        in_specs=in_vmem(11),
        out_specs=in_hbm(1) + in_vmem(2),
        scratch_shapes=[
            pltpu.VMEM((HALF, ROWS * COLS), bf16),
            pltpu.SemaphoreType.DMA,
            pltpu.VMEM((9, HALF, 128), f32),
            pltpu.VMEM((HALF, 128), f32),
            pltpu.VMEM((HALF, 128), f32),
            pltpu.VMEM((9, HALF, 128), f32),
            pltpu.VMEM((16, 128), f32),
        ],
        out_shape=[
            pltpu.HBM((HALF, ROWS * COLS), bf16),
            pltpu.HBM((2, 8, 9, 16, 128), bf16),
            jax.ShapeDtypeStruct((2, 7, CH, COLS), bf16),
        ],
        compiler_params=params(),
        cost_estimate=cost(10**9, 45 * 10**6),
        name="backward",
    )(
        *kept(
            coef, weights, normed, act1, slope1, part_p, part_q, proj_grad, w_proj, w_exp, act2
        )
    )


def finish_kernel(coef, w_proj, w_exp, act2, grad_expanded, arrived, x, c, block_out, input_grad, done):
    core, _ = tensor_place()
    cells = pl.ds(pl.multiple_of(core * (7 * COLS), 7 * COLS), 7 * COLS)
    gated = (w_proj[...].astype(f32) * coef[0:1, :]).astype(bf16)
    done[...] = jnp.zeros((8, 128), f32)
    all_projected = jnp.dot(gated, act2[:, cells], preferred_element_type=f32)
    all_grad = jnp.dot(w_exp[...], grad_expanded[:, cells], preferred_element_type=f32)
    for row in range(7):
        projected = all_projected[:, row * 128 : row * 128 + 128] + arrived[0, row].astype(f32)
        values = x[row, 0].astype(f32)
        block_out[row, 0] = (values + projected).astype(bf16)
        grad = all_grad[:, row * 128 : row * 128 + 128] + arrived[1, row].astype(f32)
        center = values - jnp.mean(values, axis=0, keepdims=True)
        inv_std = lax.rsqrt(jnp.mean(center * center, axis=0, keepdims=True) + 1e-05)
        normal = center * inv_std
        mean_grad = jnp.mean(grad, axis=0, keepdims=True)
        mean_inner = jnp.mean(grad * normal, axis=0, keepdims=True)
        input_grad[row, 0] = (
            c[row, 0].astype(f32) + inv_std * (grad - mean_grad - normal * mean_inner)
        ).astype(bf16)


def finish(coef, w_proj, w_exp, act2, grad_expanded, arrived, x, c):
    return pl.pallas_call(
        finish_kernel,
        in_specs=in_vmem(8),
        out_specs=in_vmem(3),
        out_shape=[
            jax.ShapeDtypeStruct((7, 1, CH, COLS), bf16),
            jax.ShapeDtypeStruct((7, 1, CH, COLS), bf16),
            jax.ShapeDtypeStruct((8, 128), f32),
        ],
        compiler_params=params(),
        cost_estimate=cost(SMALL, SMALL),
        name="finish",
    )(*kept(coef, w_proj, w_exp, act2), grad_expanded, arrived, x, c)


def middle_kernel(pieces, after, out):
    for slot in range(9):
        total = pieces[0, slot].astype(f32)
        for other in range(1, 16):
            total = total + pieces[other, slot].astype(f32)
        total = total.astype(bf16)
        if slot < 8:
            out[slot, 0] = total
        else:
            for z in range(8):
                out[z, 1] = total
    low = lanes_of((SQ, 128)) < 64
    outer = jnp.zeros((SQ, 128), f32)
    for yh in range(2):
        vectors = pieces[yh * 8, 8].astype(f32)
        column = down_rows(vectors[10:11, :])
        outer = outer + jnp.where(low, column[64:128], column[0:64]) * vectors[9:10, :]
    outer = outer.astype(bf16)
    for z in range(8):
        for part in range(4):
            out[z, 2 + part] = outer[part * 16 : part * 16 + 16]


def middle(pieces, after):
    return pl.pallas_call(
        middle_kernel,
        in_specs=in_vmem(2),
        out_specs=in_vmem(1)[0],
        out_shape=jax.ShapeDtypeStruct((8, 6, 16, 128), bf16),
        compiler_params=params(),
        cost_estimate=cost(10**6, 4 * 10**6),
        name="middle",
    )(pieces, after)


def tail_kernel(lines, exp_grad, proj_grad, kernel_grad, down_grad, up_grad):
    def total_of(slot):
        total = lines[0, slot].astype(f32)
        for z in range(1, 8):
            total = total + lines[z, slot].astype(f32)
        return total

    first = total_of(0)
    exp_grad[...] = first[:, 0:64]
    proj_grad[...] = pltpu.roll(first, 64, 1)[:, 0:64]
    kernel_grad[...] = total_of(1)[0:9, 0:64]
    for part in range(4):
        both = total_of(2 + part)
        down_grad[part * 16 : part * 16 + 16, :] = both[:, 0:64]
        up_grad[part * 16 : part * 16 + 16, :] = pltpu.roll(both, 64, 1)[:, 0:64]


def tail(lines):
    return pl.pallas_call(
        tail_kernel,
        in_specs=in_vmem(1),
        out_specs=in_vmem(5),
        out_shape=[
            jax.ShapeDtypeStruct((16, 64), f32),
            jax.ShapeDtypeStruct((16, 64), f32),
            jax.ShapeDtypeStruct((9, 64), f32),
            jax.ShapeDtypeStruct((64, 64), f32),
            jax.ShapeDtypeStruct((64, 64), f32),
        ],
        compiler_params=params(),
        cost_estimate=cost(10**6, 2 * 10**6),
        name="tail",
    )(lines)


def body(inputs, cotangent, w_expand, w_project, dw_kernel, se_down, se_up):
    swap = [(i, i ^ 1) for i in range(16)]
    edges = [(i, i + 1) for i in range(1, 14, 2)] + [(i + 1, i) for i in range(1, 14, 2)]
    far_edges = [(i, i + 2) for i in range(1, 14, 2)] + [(i, i - 2) for i in range(2, 16, 2)]
    packed, edge = start(inputs, cotangent, w_expand, w_project, dw_kernel.T, se_down, se_up)
    with jax.named_scope("rows"):
        near = lax.ppermute(edge, "tensor", edges)
        far = lax.ppermute(edge, "tensor", far_edges)
        other_x = lax.ppermute(inputs, "tensor", swap)
        other_c = lax.ppermute(cotangent, "tensor", swap)
        normed, cot, main_done = main_norm(inputs, other_x, cotangent, other_c)
        normed_edge, cot_edge, edge_done = edge_norm(near, far)
    with jax.named_scope("weights"):
        lines = exchange(packed, "dp", DEPTH)
        copies = spread(lines, main_done, edge_done)
        weights = exchange(copies, BOTH, PLANE).reshape(2, 8, 11, 16, 128)
    (
        normed, act1, slope1, act2, part_p, part_q, proj_grad, w_exp, w_proj, own_rows, sums
    ) = forward(weights, normed, cot, normed_edge, cot_edge)
    with jax.named_scope("sums"):
        other_rows = lax.ppermute(own_rows, "tensor", swap)
        all_sums = exchange(sums, "tensor")
    coef = excite(all_sums, own_rows, other_rows)
    grad_expanded, pieces, partial_out = backward(
        coef, weights, normed, act1, slope1, part_p, part_q, proj_grad, w_proj, w_exp, act2
    )
    with jax.named_scope("finish"):
        arrived = lax.ppermute(partial_out, "tensor", swap)
        block_out, input_grad, done = finish(
            coef, w_proj, w_exp, act2, grad_expanded, arrived, inputs, cotangent
        )
    with jax.named_scope("gradients"):
        pieces = exchange(pieces.reshape(16, 9, 16, 128), BOTH, PLANE)
        lines = exchange(middle(pieces, done), "dp", DEPTH)
        exp_grad, proj_grad, kernel_grad, down_grad, up_grad = tail(lines)
    return (block_out, input_grad, exp_grad, proj_grad, kernel_grad.T, down_grad, up_grad)


def solution(mesh):
    placed = (
        P("tensor", "dp", None, None),
        P("tensor", "dp", None, None),
        P("dp", "tensor"),
        P("dp", "tensor"),
        P("tensor", None),
        P(None, "tensor"),
        P(None, "tensor"),
    )
    return jax.shard_map(
        body,
        mesh=mesh,
        in_specs=placed,
        out_specs=(
            P("tensor", "dp", None, None),
            P("tensor", "dp", None, None),
            P("dp", "tensor"),
            P("dp", "tensor"),
            P("tensor", None),
            P(None, "tensor"),
            P(None, "tensor"),
        ),
        check_vma=False,
    )
```

time: 548 us -> 107 us (0.20)
  waiting for transfers between devices: 229 us -> 9.47 us
  blocking collectives: 211 us -> 41.8 us
  matrix products: 50.7 us -> 0 us
  other arithmetic: 30.8 us -> 0 us
  Pallas kernels: 0 us -> 28.5 us
  starting transfers between devices: 0.2 us -> 19.8 us
  between operations: 14.6 us -> 0.82 us
    reduce_scatter x2 -> x0, waiting for transfers between devices: 146 us -> none  [the longest x1 74.9 us: channel_pass(): lax.psum_scatter(jnp.einsum('hbew,ce->hbcw', row_piece, proj_rows, prefer...]
    psum x3 -> x0, blocking collectives: 131 us -> none  [the longest x1 77.5 us: body(): lax.psum(g_kernel.astype(jnp.bfloat16), 'dp').astype(jnp.float32)]
    all_gather x2 -> x0, blocking collectives: 80.2 us -> none  [the longest x1 44.3 us: body(): lax.all_gather(w_expand, 'dp', axis=0, tiled=True)]
    unnamed x6 -> x0, waiting for transfers between devices: 64.5 us -> none
    dot_general x10 -> x0, matrix products: 50.7 us -> none  [the longest x1 22.6 us: channel_pass(): jnp.einsum('hbcw,ce->hbew', cot_all, proj_rows, preferred_element_type=jn...]
    all_to_all x0 -> x3, blocking collectives: none -> 41.8 us  [exchange(): lax.all_to_all(pieces, axes, 0, 0, tiled=True, axis_index_groups=members)]
    pallas_call x0 -> x10, Pallas kernels: none -> 28.5 us  [the longest x1 10.9 us: forward(): pl.pallas_call(forward_kernel, in_specs=in_vmem(5), out_specs=in_vmem(11)...]
    reduce_sum x4 -> x0, other arithmetic: 18.7 us -> none  [the longest x1 16.5 us: depthwise_back(): jnp.sum(grad_out * shifted(source, shift_down, shift_right), axis=(0, 1, 3))]
  transfers between devices with their start and end apart: 5 -> 8, of which waited for: 4 -> 2; matrix products, arithmetic and copies ran while one was open for 5% -> 0% of each run, Pallas kernels for 0% -> 5%
where the time goes in v2:
time: 107 us
  blocking collectives  41.8 us (39%)
  Pallas kernels  28.5 us (27%)
  starting transfers between devices  19.8 us (19%)
  waiting for transfers between devices  9.47 us (9%)
  local copies, waits for them, and re-layouts  6.38 us (6%)
    all_to_all x3, blocking collectives, exchange(): lax.all_to_all(pieces, axes, 0, 0, tiled=True, axis_index_groups=members)  41.8 us
    all_to_all x2, starting transfers between devices, exchange(): lax.all_to_all(pieces, axes, 0, 0, tiled=True, axis_index_groups=members)  12.8 us
    pallas_call x1, Pallas kernels, forward(): pl.pallas_call(forward_kernel, in_specs=in_vmem(5), out_specs=in_vmem(11)...  10.9 us
    pallas_call x1, Pallas kernels, backward(): pl.pallas_call(backward_kernel, in_specs=in_vmem(11), out_specs=in_hbm(1)...  10.3 us
    all_to_all x2, waiting for transfers between devices, exchange(): lax.all_to_all(pieces, axes, 0, 0, tiled=True, axis_index_groups=members)  9.45 us
    unnamed x22, local copies, waits for them, and re-layouts  6.38 us
    ppermute x1, starting transfers between devices, body(): far = lax.ppermute(edge, 'tensor', far_edges)  4.18 us
    pallas_call x1, Pallas kernels, finish(): pl.pallas_call(finish_kernel, in_specs=in_vmem(8), out_specs=in_vmem(3),...  3.14 us
  transfers between devices with their start and end apart: 8, of which 2 were waited for; matrix products, arithmetic and copies ran while one was open for 0% of the time, Pallas kernels for 5%

profile of v2, /device:TPU:2, one launch (start us, length us, event | category | flops | bytes accessed | tf_op | source)
XLA Modules:
  0.0 106.8 jit_solution(15517511868061357023)
XLA Ops:
  0.6 0.1 collective-permute-start
  0.7 0.5 collective-permute-start.1
  1.2 1.7 %start.1 = (bf16[8,32,128]{2,1,0:T(8,128)(2,1)}, bf16[2,2,1,256,128]{4,3,2,1,0:T(8,128)(2,1)S(1)}) custom-call(bf16[7,1,256,128]{3,2,1,0:T(8,128)(2,1)} %x.3, bf16[7,1,256,128]{3,2,1,0:T(8,128)(2,1)} %c.3, bf16[16,64]{1,0:T(8,128)(2,1)} %w_expand.1, bf16[16,64]{1,0:T(8,128)(2,1)} %w_project.1, bf16[9,64]{1,0:T(8,128)(2,1)} %bitcast.7, ...), custom_call_target="tpu_custom_call" | custom-call | flops 100000 | bytes 100000 | tf_op jit(solution)/shard_map/start/pallas_call | solution.py:166
  3.0 4.2 %collective-permute-start.3 = (bf16[2,2,1,256,128]{4,3,2,1,0:T(8,128)(2,1)S(1)}, bf16[2,2,1,256,128]{4,3,2,1,0:T(8,128)(2,1)S(1)}, u32[]{:S(2)}, u32[]{:S(2)}) collective-permute-start(bf16[2,2,1,256,128]{4,3,2,1,0:T(8,128)(2,1)S(1)} %get-tuple-element.39), channel_id=1, source_target_pairs={{1,3},{3,5},{5,7},{7,9},{9,11},{11,13},{13,15},{2,0},{4,2},{6,4},{... | collective-permute-start | bytes 786440 | tf_op jit(solution)/shard_map/rows/ppermute | solution.py:712
  7.2 1.9 %collective-permute-start.2 = (bf16[2,2,1,256,128]{4,3,2,1,0:T(8,128)(2,1)S(1)}, bf16[2,2,1,256,128]{4,3,2,1,0:T(8,128)(2,1)S(1)}, u32[]{:S(2)}, u32[]{:S(2)}) collective-permute-start(bf16[2,2,1,256,128]{4,3,2,1,0:T(8,128)(2,1)S(1)} %get-tuple-element.39), channel_id=1, source_target_pairs={{1,2},{3,4},{5,6},{7,8},{9,10},{11,12},{13,14},{2,1},{4,3},{6,5},{... | collective-permute-start | bytes 786440 | tf_op jit(solution)/shard_map/rows/ppermute | solution.py:711
  9.1 7.7 %all-to-all-start = ((bf16[8,32,128]{2,1,0:T(8,128)(2,1)}), bf16[8,32,128]{2,1,0:T(8,128)(2,1)S(1)}, u32[]{:S(2)}, u32[]{:S(2)}) async-start(bf16[8,32,128]{2,1,0:T(8,128)(2,1)} %get-tuple-element.37), calls=%async_computation | async-start | bytes 131072 | tf_op jit(solution)/shard_map/weights/all_to_all | solution.py:46
  16.8 0.0 collective-permute-done.3.far
  16.8 0.0 collective-permute-done.2.near
  16.8 0.2 edge_norm.1
  17.0 0.0 collective-permute-done.other_x
  17.0 0.0 collective-permute-done.1.other_c
  17.0 0.0 copy-start
  17.0 1.0 copy-done
  18.0 0.0 copy-start.2
  18.0 1.0 copy-done.2
  19.0 0.8 main_norm.1
  19.8 0.0 copy-start.9
  19.8 0.9 copy-done.9
  20.7 4.5 %all-to-all-done.lines = bf16[8,32,128]{2,1,0:T(8,128)(2,1)S(1)} async-done(((bf16[8,32,128]{2,1,0:T(8,128)(2,1)}), bf16[8,32,128]{2,1,0:T(8,128)(2,1)S(1)}, u32[]{:S(2)}, u32[]{:S(2)}) %all-to-all-start) | async-done | bytes 65568 | tf_op jit(solution)/shard_map/weights/all_to_all | solution.py:46
  25.3 0.0 copy-start.10
  25.3 0.1 spread.1
  25.4 20.8 %all_to_all.25 = bf16[16,11,16,128]{3,2,1,0:T(8,128)(2,1)S(1)} all-to-all(bf16[16,11,16,128]{3,2,1,0:T(8,128)(2,1)S(1)} %spread.1), channel_id=1, replica_groups={{0,2,4,6,8,10,12,14,16,18,20,22,24,26,28,30},{1,3,5,7,9,11,13,15,17,19,..., dimensions={0} | all-to-all | bytes 1441792 | tf_op jit(solution)/shard_map/weights/all_to_all | solution.py:46
  46.2 0.0 copy-done.10
  46.2 10.9 %forward.1 = (bf16[256,1792]{1,0:T(8,128)(2,1)S(1)}, bf16[512,2304]{1,0:T(8,128)(2,1)S(1)}, bf16[512,1792]{1,0:T(8,128)(2,1)S(1)}, bf16[512,1792]{1,0:T(8,128)(2...) custom-call(bf16[2,8,11,16,128]{4,3,2,1,0:T(8,128)(2,1)S(1)} %bitcas, ...), custom_call_target="tpu_custom_call" | custom-call | flops 1000000000 | bytes 50000000 | tf_op jit(solution)/shard_map/forward/pallas_call | solution.py:382
  57.0 0.0 copy-start.5
  57.0 0.0 copy-start.7
  57.0 0.1 collective-permute-start.4
  57.1 8.7 %all_to_all.26.sums = f32[16,8,128]{2,1,0:T(8,128)S(1)} all-to-all(f32[16,8,128]{2,1,0:T(8,128)S(1)} %get-tuple-element.45), channel_id=1, replica_groups=mesh['dp'=16,'tensor'=16] {'tensor'}, dimensions={0} | all-to-all | bytes 131072 | tf_op jit(solution)/shard_map/sums/all_to_all | solution.py:46
  65.8 0.0 collective-permute-done.4.other_rows
  65.9 0.5 excite.1.coef
  66.4 0.0 copy-start.1
  66.4 0.0 copy-start.3
  66.4 10.3 %backward.1 = (bf16[512,1792]{1,0:T(8,128)(2,1)}, bf16[2,8,9,16,128]{4,3,2,1,0:T(8,128)(2,1)}, bf16[2,7,256,128]{3,2,1,0:T(8,128)(2,1)}) custom-call(f32[8,512]{1,0:T(8,128)S(1)} %excite.1.coef, bf16[2,8,11,16,128]{4,3,2,1,0:T(8,128)(2,1)S(1)} %bitcast.5, bf16[256,1792]{1,0:T(8,128)(2,1)S(1)} %get-tuple-element.50.normed, ...), custom_call_target="tpu_custom_call" | custom-call | flops 1000000000 | bytes 45000000 | tf_op jit(solution)/shard_map/backward/pallas_call | solution.py:569
  76.7 0.0 copy-done.5
  76.7 0.0 copy-done.7
  76.7 0.2 collective-permute-start.5
  76.9 5.2 %all-to-all-start.3 = ((bf16[16,9,16,128]{3,2,1,0:T(8,128)(2,1)}), bf16[16,9,16,128]{3,2,1,0:T(8,128)(2,1)S(1)}, u32[]{:S(2)}, u32[]{:S(2)}) async-start(bf16[16,9,16,128]{3,2,1,0:T(8,128)(2,1)} %bitcast.6), calls=%async_computation.3 | async-start | bytes 1179648 | tf_op jit(solution)/shard_map/gradients/all_to_all | solution.py:46
  82.1 0.0 collective-permute-done.5.arrived
  82.1 0.0 copy-done.1
  82.1 0.0 copy-done.3
  82.1 0.0 copy-start.4
  82.1 1.5 %copy-done.4 = bf16[512,1792]{1,0:T(8,128)(2,1)S(1)} copy-done((bf16[512,1792]{1,0:T(8,128)(2,1)S(1)}, bf16[512,1792]{1,0:T(8,128)(2,1)}, u32[]{:S(2)}) %copy-start.4) | copy-done | bytes 1835032
  83.6 0.0 copy-start.6
  83.6 0.9 copy-done.6
  84.6 0.0 copy-start.8
  84.6 0.9 copy-done.8
  85.5 3.1 %finish.1 = (bf16[7,1,256,128]{3,2,1,0:T(8,128)(2,1)}, bf16[7,1,256,128]{3,2,1,0:T(8,128)(2,1)}, f32[8,128]{1,0:T(8,128)S(1)}) custom-call(f32[8,512]{1,0:T(8,128)S(1)} %excite.1.coef, bf16[256,512]{1,0:T(8,128)(2,1)S(1)} %copy-done.8, bf16[256,512]{1,0:T(8,128)(2,1)S(1)} %copy-done.6, bf16[512,1792]{1,0:T(8,128)(2,1)S(1)} %get-tuple-element.49.act2, ...), custom_call_target="tpu_custom_call" | custom-call | flops 100000 | bytes 100000 | tf_op jit(solution)/shard_map/finish/finish/pallas_call | solution.py:620
  88.7 4.9 %all-to-all-done.3.pieces = bf16[16,9,16,128]{3,2,1,0:T(8,128)(2,1)S(1)} async-done(((bf16[16,9,16,128]{3,2,1,0:T(8,128)(2,1)}), bf16[16,9,16,128]{3,2,1,0:T(8,128)(2,1)S(1)}, u32[]{:S(2)}, u32[]{:S(2)}) %all-to-all-start.3) | async-done | bytes 589856 | tf_op jit(solution)/shard_map/gradients/all_to_all | solution.py:46
  93.6 0.2 middle.1
  93.7 12.4 %all_to_all.27.lines = bf16[8,6,16,128]{3,2,1,0:T(8,128)(2,1)S(1)} all-to-all(bf16[8,6,16,128]{3,2,1,0:T(8,128)(2,1)S(1)} %middle.1), channel_id=1, replica_groups={{0,32,64,96,128,160,192,224},{16,48,80,112,144,176,208,240},{1,33,65,97..., dimensions={0} | all-to-all | bytes 393216 | tf_op jit(solution)/shard_map/gradients/all_to_all | solution.py:46
  106.1 0.7 tail.1
Async XLA Ops:
  0.6 16.4 %collective-permute-start = (bf16[7,1,256,128]{3,2,1,0:T(8,128)(2,1)}, bf16[7,1,256,128]{3,2,1,0:T(8,128)(2,1)S(1)}, u32[]{:S(2)}, u32[]{:S(2)}) collective-permute-start(bf16[7,1,256,128]{3,2,1,0:T(8,128)(2,1)} %x.3), channel_id=1, source_target_pairs={{0,1},{1,0},{2,3},{3,2},{4,5},{5,4},{6,7},{7,6},{8,9},{9,8},{10,11... | collective-permute-start | bytes 1376264 | tf_op jit(solution)/shard_map/rows/ppermute | solution.py:713
  0.7 16.3 %collective-permute-start.1 = (bf16[7,1,256,128]{3,2,1,0:T(8,128)(2,1)}, bf16[7,1,256,128]{3,2,1,0:T(8,128)(2,1)S(1)}, u32[]{:S(2)}, u32[]{:S(2)}) collective-permute-start(bf16[7,1,256,128]{3,2,1,0:T(8,128)(2,1)} %c.3), channel_id=1, source_target_pairs={{0,1},{1,0},{2,3},{3,2},{4,5},{5,4},{6,7},{7,6},{8,9},{9,8},{10,11... | collective-permute-start | bytes 1376264 | tf_op jit(solution)/shard_map/rows/ppermute | solution.py:714
  3.0 13.8 %collective-permute-start.3 = (bf16[2,2,1,256,128]{4,3,2,1,0:T(8,128)(2,1)S(1)}, bf16[2,2,1,256,128]{4,3,2,1,0:T(8,128)(2,1)S(1)}, u32[]{:S(2)}, u32[]{:S(2)}) collective-permute-start(bf16[2,2,1,256,128]{4,3,2,1,0:T(8,128)(2,1)S(1)} %get-tuple-element.39), channel_id=1, source_target_pairs={{1,3},{3,5},{5,7},{7,9},{9,11},{11,13},{13,15},{2,0},{4,2},{6,4},{... | collective-permute-start | bytes 786440 | tf_op jit(solution)/shard_map/rows/ppermute | solution.py:712
  7.2 9.6 %collective-permute-start.2 = (bf16[2,2,1,256,128]{4,3,2,1,0:T(8,128)(2,1)S(1)}, bf16[2,2,1,256,128]{4,3,2,1,0:T(8,128)(2,1)S(1)}, u32[]{:S(2)}, u32[]{:S(2)}) collective-permute-start(bf16[2,2,1,256,128]{4,3,2,1,0:T(8,128)(2,1)S(1)} %get-tuple-element.39), channel_id=1, source_target_pairs={{1,2},{3,4},{5,6},{7,8},{9,10},{11,12},{13,14},{2,1},{4,3},{6,5},{... | collective-permute-start | bytes 786440 | tf_op jit(solution)/shard_map/rows/ppermute | solution.py:711
  9.1 16.2 %all-to-all-start = ((bf16[8,32,128]{2,1,0:T(8,128)(2,1)}), bf16[8,32,128]{2,1,0:T(8,128)(2,1)S(1)}, u32[]{:S(2)}, u32[]{:S(2)}) async-start(bf16[8,32,128]{2,1,0:T(8,128)(2,1)} %get-tuple-element.37), calls=%async_computation | async-start | bytes 131072 | tf_op jit(solution)/shard_map/weights/all_to_all | solution.py:46
  17.0 1.0 copy-start
  18.0 1.0 copy-start.2
  19.8 0.9 copy-start.9
  25.3 20.9 %copy-start.10 = (bf16[256,1792]{1,0:T(8,128)(2,1)S(1)}, bf16[256,1792]{1,0:T(8,128)(2,1)}, u32[]{:S(2)}) copy-start(bf16[256,1792]{1,0:T(8,128)(2,1)} %copy-done.9) | copy-start | bytes 2752516
  57.0 19.7 %copy-start.5 = (bf16[256,512]{1,0:T(8,128)(2,1)}, bf16[256,512]{1,0:T(8,128)(2,1)S(1)}, u32[]{:S(2)}) copy-start(bf16[256,512]{1,0:T(8,128)(2,1)S(1)} %get-tuple-element.48.w_exp) | copy-start | bytes 786436
  57.0 19.7 %copy-start.7 = (bf16[256,512]{1,0:T(8,128)(2,1)}, bf16[256,512]{1,0:T(8,128)(2,1)S(1)}, u32[]{:S(2)}) copy-start(bf16[256,512]{1,0:T(8,128)(2,1)S(1)} %get-tuple-element.47.w_proj) | copy-start | bytes 786436
  57.0 8.8 %collective-permute-start.4 = (bf16[2,8,2,16,128]{4,3,2,1,0:T(8,128)(2,1)S(1)}, bf16[2,8,2,16,128]{4,3,2,1,0:T(8,128)(2,1)S(1)}, u32[]{:S(2)}, u32[]{:S(2)}) collective-permute-start(bf16[2,8,2,16,128]{4,3,2,1,0:T(8,128)(2,1)S(1)} %get-tuple-element.46.own_rows), channel_id=1, source_target_pairs={{0,1},{1,0},{2,3},{3,2},{4,5},{5,4},{6,7},{7,6},{8,9},{9,8},{10,11... | collective-permute-start | bytes 393224 | tf_op jit(solution)/shard_map/sums/ppermute | solution.py:725
  66.4 15.7 %copy-start.1 = (bf16[7,1,256,128]{3,2,1,0:T(8,128)(2,1)S(1)}, bf16[7,1,256,128]{3,2,1,0:T(8,128)(2,1)}, u32[]{:S(2)}) copy-start(bf16[7,1,256,128]{3,2,1,0:T(8,128)(2,1)} %x.3) | copy-start | bytes 1376260
  66.4 15.7 %copy-start.3 = (bf16[7,1,256,128]{3,2,1,0:T(8,128)(2,1)S(1)}, bf16[7,1,256,128]{3,2,1,0:T(8,128)(2,1)}, u32[]{:S(2)}) copy-start(bf16[7,1,256,128]{3,2,1,0:T(8,128)(2,1)} %c.3) | copy-start | bytes 1376260
  76.7 5.4 %collective-permute-start.5 = (bf16[2,7,256,128]{3,2,1,0:T(8,128)(2,1)}, bf16[2,7,256,128]{3,2,1,0:T(8,128)(2,1)}, u32[]{:S(2)}, u32[]{:S(2)}) collective-permute-start(bf16[2,7,256,128]{3,2,1,0:T(8,128)(2,1)} %get-tuple-element.57), channel_id=1, source_target_pairs={{0,1},{1,0},{2,3},{3,2},{4,5},{5,4},{6,7},{7,6},{8,9},{9,8},{10,11... | collective-permute-start | bytes 2752520 | tf_op jit(solution)/shard_map/finish/ppermute | solution.py:732
  76.9 16.6 %all-to-all-start.3 = ((bf16[16,9,16,128]{3,2,1,0:T(8,128)(2,1)}), bf16[16,9,16,128]{3,2,1,0:T(8,128)(2,1)S(1)}, u32[]{:S(2)}, u32[]{:S(2)}) async-start(bf16[16,9,16,128]{3,2,1,0:T(8,128)(2,1)} %bitcast.6), calls=%async_computation.3 | async-start | bytes 1179648 | tf_op jit(solution)/shard_map/gradients/all_to_all | solution.py:46
  82.1 1.5 %copy-start.4 = (bf16[512,1792]{1,0:T(8,128)(2,1)S(1)}, bf16[512,1792]{1,0:T(8,128)(2,1)}, u32[]{:S(2)}) copy-start(bf16[512,1792]{1,0:T(8,128)(2,1)} %get-tuple-element.56.grad_expanded) | copy-start | bytes 5505028
  83.6 0.9 copy-start.6
  84.6 0.9 copy-start.8

commit v3 on v2

--- a/solution.py
+++ b/solution.py
@@ -57,11 +57,24 @@
 def gelu_pair(values):
     square = values * values
     inner = values * (gelu_scale + (gelu_scale * gelu_cubic) * square)
-    part = 0.5 + 0.5 * jnp.tanh(inner)
-    act = values * part
-    slope = part + act * (1.0 - part) * (
-        2.0 * gelu_scale + (6.0 * gelu_scale * gelu_cubic) * square
-    )
+    tanh_part = jnp.tanh(inner)
+    above = 1.0 + tanh_part
+    act = values * above
+    slope = above + act * (1.0 - tanh_part) * (
+        gelu_scale + (3.0 * gelu_scale * gelu_cubic) * square
+    )
+    return act, slope
+
+
+stretch = (gelu_scale * gelu_cubic) ** (1.0 / 3.0)
+
+
+def stretched_gelu_pair(values):
+    base = values * values + gelu_scale / stretch
+    tanh_part = jnp.tanh(values * base)
+    above = 1.0 + tanh_part
+    act = values * above
+    slope = above + act * (1.0 - tanh_part) * (3.0 * base - 2.0 * gelu_scale / stretch)
     return act, slope
 
 
@@ -187,7 +200,7 @@
     )(*far_memory(x, c, w_expand, w_project, dw_rows, se_down, se_up))
 
 
-def spread_kernel(lines, first, second, out, squeeze_rows, tap_rows):
+def spread_kernel(lines, after, out, squeeze_rows, tap_rows):
     tap_rows[...] = jnp.zeros((16, 128), f32)
     for z in range(8):
         small = lines[z, 16:32, :].astype(f32)
@@ -203,17 +216,17 @@
         out[other, 10] = tap_piece
 
 
-def spread(lines, first, second):
+def spread(lines, after):
     return pl.pallas_call(
         spread_kernel,
-        in_specs=in_vmem(3),
+        in_specs=in_vmem(2),
         out_specs=in_vmem(1)[0],
         out_shape=jax.ShapeDtypeStruct((16, 11, 16, 128), bf16),
         scratch_shapes=[pltpu.VMEM((32, 128), f32), pltpu.VMEM((16, 128), f32)],
         compiler_params=params(),
         cost_estimate=cost(SMALL, SMALL),
         name="spread",
-    )(lines, first, second)
+    )(lines, after)
 
 
 def normal_of(x):
@@ -227,69 +240,104 @@
     return pl.ds(pl.multiple_of(row * 128, 128), 128)
 
 
-def main_norm_kernel(own_x, other_x, own_c, other_c, normed, cot, done):
+def copy_all(pairs, sems):
+    copies = [pltpu.make_async_copy(a, b, sems.at[i]) for i, (a, b) in enumerate(pairs)]
+    for copy in copies:
+        copy.start()
+    return copies
+
+
+def main_norm_kernel(own_x, other_x, normed_out, done, own_x_in, other_x_in, normed, sems):
     done[...] = jnp.zeros((8, 128), f32)
     core, _ = tensor_place()
-    for x, c, first in ((own_x, own_c, 7 * core), (other_x, other_c, 7 - 7 * core)):
+    copies = copy_all(((own_x, own_x_in), (other_x, other_x_in)), sems)
+    sent = []
+    for i, (x, first) in enumerate(((own_x_in, 7 * core), (other_x_in, 7 - 7 * core))):
+        copies[i].wait()
         for row in range(7):
-            normed[:, lane_block(first + row)] = normal_of(x[row, 0])
-            cot[:, lane_block(first + row)] = c[row, 0]
-
-
-def main_norm(own_x, other_x, own_c, other_c):
+            normed[i, :, row * 128 : row * 128 + 128] = normal_of(x[row, 0])
+        part = pl.ds(pl.multiple_of(first * 128, 7 * 128), 7 * 128)
+        sent.append(pltpu.make_async_copy(normed.at[i], normed_out.at[:, part], sems.at[i]))
+        sent[i].start()
+    for copy in sent:
+        copy.wait()
+
+
+def main_norm(own_x, other_x):
     return pl.pallas_call(
         main_norm_kernel,
-        in_specs=in_vmem(4),
-        out_specs=in_vmem(3),
-        out_shape=[held((CH, ROWS * COLS), bf16)] * 2 + [jax.ShapeDtypeStruct((8, 128), f32)],
+        in_specs=in_hbm(2),
+        out_specs=in_hbm(1) + in_vmem(1),
+        out_shape=[
+            pltpu.HBM((CH, ROWS * COLS), bf16),
+            jax.ShapeDtypeStruct((8, 128), f32),
+        ],
+        scratch_shapes=[pltpu.VMEM((7, 1, CH, COLS), bf16)] * 2
+        + [pltpu.VMEM((2, CH, 7 * COLS), bf16), pltpu.SemaphoreType.DMA((2,))],
         compiler_params=params(),
         cost_estimate=cost(SMALL, SMALL),
         name="main_norm",
-    )(own_x, other_x, own_c, other_c)
-
-
-def edge_norm_kernel(near, far, normed, cot, done):
-    done[...] = jnp.zeros((8, 128), f32)
-    core, _ = tensor_place()
-    for edge, first in ((near, 2 * core), (far, 2 - 2 * core)):
-        for row in range(2):
-            normed[:, lane_block(first + row)] = normal_of(edge[0, row, 0])
-            cot[:, lane_block(first + row)] = edge[1, row, 0]
-
-
-def edge_norm(near, far):
+    )(*far_memory(own_x, other_x))
+
+
+def edge_norm_kernel(near, after, edge_out, done, edge, sem):
+    done[...] = after[...]
+    for row in range(2):
+        edge[0, :, row * 128 : row * 128 + 128] = normal_of(near[0, row, 0])
+        edge[1, :, row * 128 : row * 128 + 128] = near[1, row, 0]
+    copy = pltpu.make_async_copy(edge, edge_out, sem)
+    copy.start()
+    copy.wait()
+
+
+def edge_norm(near, after):
     return pl.pallas_call(
         edge_norm_kernel,
         in_specs=in_vmem(2),
-        out_specs=in_vmem(3),
-        out_shape=[held((CH, 4 * COLS), bf16)] * 2 + [jax.ShapeDtypeStruct((8, 128), f32)],
+        out_specs=in_hbm(1) + in_vmem(1),
+        out_shape=[pltpu.HBM((2, CH, 2 * COLS), bf16), jax.ShapeDtypeStruct((8, 128), f32)],
+        scratch_shapes=[
+            pltpu.VMEM((2, CH, 2 * COLS), bf16),
+            pltpu.SemaphoreType.DMA,
+        ],
         compiler_params=params(),
         cost_estimate=cost(SMALL, SMALL),
         name="edge_norm",
-    )(near, far)
-
-
-def spread_taps(sources, taps, place, masked):
+    )(near, after)
+
+
+def spread_taps(sources, taps, place, turned, scale):
     low = lanes_of((16, 128)) < 64
     early = join_low(sources[0][0].astype(f32), sources[0][1].astype(f32), low)
     late = join_low(sources[1][0].astype(f32), sources[1][1].astype(f32), low)
+    early = early * scale
+    late = late * scale
     lane = lanes_of((128, 128))
     for tap in range(9):
         spread = down_rows(early[tap : tap + 1, :] if tap < 8 else late[0:1, :])
-        if masked and tap % 3 == 0:
+        if tap % 3 == (2 if turned else 0):
             spread = jnp.where(lane == 0, 0.0, spread)
-        if masked and tap % 3 == 2:
+        if tap % 3 == (0 if turned else 2):
             spread = jnp.where(lane == 127, 0.0, spread)
         taps[tap, place : place + 128, :] = spread
 
 
 def forward_kernel(
-    weights, normed, cot, normed_edge, cot_edge,
-    normed_out, act1, slope1, act2, part_p, part_q, proj_grad, w_exp, w_proj, squeeze_rows, sums,
-    expanded, grad_hidden, taps, pool, gate,
+    weights, normed_in, near_in, far_in, own_c, other_c,
+    normed, act1, slope1, act2, slope2, grad_hidden, proj_grad, w_exp, w_proj, squeeze_rows, sums,
+    cot, own_c_in, other_c_in, near, far, expanded, taps, pool, gate, sems,
 ):
-    _, chip = tensor_place()
-    normed_out[...] = normed[...]
+    core, chip = tensor_place()
+    copies = copy_all(
+        (
+            (near_in, near),
+            (far_in, far),
+            (normed_in, normed),
+            (own_c, own_c_in),
+            (other_c, other_c_in),
+        ),
+        sems,
+    )
     low = lanes_of((16, 128)) < 64
     for block in range(BLOCKS):
         cells = slice(block * 128, block * 128 + 128)
@@ -304,25 +352,35 @@
             [[weights[yh, 2 * block + j, 10] for j in range(2)] for yh in range(2)],
             taps,
             block * 128,
-            True,
+            False,
+            0.5 * stretch,
         )
     squeeze_rows[...] = weights[:, :, 8:10]
-    w_exp_t = w_exp[...].astype(f32).T.astype(bf16)
-    w_proj_t = w_proj[...].astype(f32).T.astype(bf16)
 
     def multiply(weight, source, target, place):
-        target[:, place * 128 : place * 128 + source.shape[1]] = jnp.dot(
-            weight, source, preferred_element_type=f32
-        ).astype(bf16)
-
-    multiply(w_exp_t, normed_edge[:, 0:256], expanded, 0)
-    multiply(w_exp_t, normed_edge[:, 256:512], expanded, ROWS + 2)
-    multiply(w_proj_t, cot_edge[:, 128:256], grad_hidden, 0)
-    multiply(w_proj_t, cot_edge[:, 256:384], grad_hidden, ROWS + 1)
+        target[:, place * 128 : place * 128 + source.shape[1]] = lax.dot_general(
+            weight[...], source, (((0,), (0,)), ((), ())), preferred_element_type=f32
+        ).astype(target.dtype)
+
+    for copy in copies[:3]:
+        copy.wait()
+    near_first = core == 0
+    multiply(w_exp, jnp.where(near_first, near[0], far[0]), expanded, 0)
+    multiply(w_exp, jnp.where(near_first, far[0], near[0]), expanded, ROWS + 2)
+    above = jnp.where(near_first, near[1, :, 128:256], far[1, :, 128:256])
+    below = jnp.where(near_first, far[1, :, 0:128], near[1, :, 0:128])
+    multiply(w_proj, above, grad_hidden, 0)
+    multiply(w_proj, below, grad_hidden, ROWS + 1)
     for part in range(ROWS // 2):
         cells = slice(part * 256, part * 256 + 256)
-        multiply(w_exp_t, normed[:, cells], expanded, 2 + 2 * part)
-        multiply(w_proj_t, cot[:, cells], grad_hidden, 1 + 2 * part)
+        multiply(w_exp, normed[:, cells], expanded, 2 + 2 * part)
+    for copy, c, first in ((copies[3], own_c_in, 7 * core), (copies[4], other_c_in, 7 - 7 * core)):
+        copy.wait()
+        for row in range(7):
+            cot[:, lane_block(first + row)] = c[row, 0]
+    for part in range(ROWS // 2):
+        cells = slice(part * 256, part * 256 + 256)
+        multiply(w_proj, cot[:, cells], grad_hidden, 1 + 2 * part)
     first_chip = jnp.where(chip > 0, 1.0, 0.0)
     last_chip = jnp.where(chip < 7, 1.0, 0.0)
 
@@ -333,8 +391,7 @@
         pool_sum = jnp.zeros((GROUP, COLS), f32)
         gate_sum = jnp.zeros((GROUP, COLS), f32)
         for h in range(EXT):
-            value = expanded[rows, h * 128 : h * 128 + 128].astype(f32)
-            act, slope = gelu_pair(value)
+            act, slope = gelu_pair(expanded[rows, h * 128 : h * 128 + 128])
             act1[rows, h * 128 : h * 128 + 128] = act.astype(bf16)
             if 2 <= h < ROWS + 2:
                 slope1[rows, (h - 2) * 128 : (h - 1) * 128] = slope.astype(bf16)
@@ -349,27 +406,26 @@
             m = h - 1
             if not 1 <= m <= ROWS + 2:
                 continue
-            act, slope = gelu_pair(running.pop(m))
-            grad = grad_hidden[rows, (m - 1) * 128 : m * 128].astype(f32)
+            act, slope = stretched_gelu_pair(running.pop(m))
             if m == 1:
                 slope = slope * first_chip
             if m == ROWS + 2:
                 slope = slope * last_chip
-            part_q[rows, (m - 1) * 128 : m * 128] = slope.astype(bf16)
-            part_p[rows, (m - 1) * 128 : m * 128] = (slope * grad).astype(bf16)
+            slope2[rows, (m - 1) * 128 : m * 128] = slope.astype(bf16)
             if 2 <= m < ROWS + 2:
                 act2[rows, (m - 2) * 128 : (m - 1) * 128] = act.astype(bf16)
                 pool_sum = pool_sum + act
+                grad = grad_hidden[rows, (m - 1) * 128 : m * 128].astype(f32)
                 gate_sum = gate_sum + act * grad
         pool[rows, :] = pool_sum
         gate[rows, :] = gate_sum
         return carry
 
-    lax.fori_loop(0, HALF // GROUP, one_group, 0)
+    lax.fori_loop(0, HALF // GROUP, one_group, 0, unroll=2)
     for block in range(BLOCKS):
         cells = slice(block * 128, block * 128 + 128)
-        pool_row = jnp.sum(pool[cells, :].T, axis=0, keepdims=True)
-        gate_row = jnp.sum(gate[cells, :].T, axis=0, keepdims=True)
+        pool_row = jnp.sum(pool[cells, :].T, axis=0, keepdims=True) * (0.5 / stretch)
+        gate_row = jnp.sum(gate[cells, :].T, axis=0, keepdims=True) * (0.5 / stretch)
         for other in range(16):
             sums[other, block : block + 1, :] = pool_row
             sums[other, BLOCKS + block : BLOCKS + block + 1, :] = gate_row
@@ -378,17 +434,22 @@
     )
 
 
-def forward(weights, normed, cot, normed_edge, cot_edge):
+def forward(weights, normed, near, far, own_c, other_c):
     return pl.pallas_call(
         forward_kernel,
-        in_specs=in_vmem(5),
+        in_specs=in_vmem(1) + in_hbm(5),
         out_specs=in_vmem(11),
         scratch_shapes=[
-            pltpu.VMEM((HALF, EXT * COLS), bf16),
-            pltpu.VMEM((HALF, (ROWS + 2) * COLS), bf16),
+            pltpu.VMEM((CH, ROWS * COLS), bf16),
+            pltpu.VMEM((7, 1, CH, COLS), bf16),
+            pltpu.VMEM((7, 1, CH, COLS), bf16),
+            pltpu.VMEM((2, CH, 2 * COLS), bf16),
+            pltpu.VMEM((2, CH, 2 * COLS), bf16),
+            pltpu.VMEM((HALF, EXT * COLS), f32),
             pltpu.VMEM((9, HALF, 128), f32),
             pltpu.VMEM((HALF, 128), f32),
             pltpu.VMEM((HALF, 128), f32),
+            pltpu.SemaphoreType.DMA((5,)),
         ],
         out_shape=[
             held((CH, ROWS * COLS), bf16),
@@ -406,7 +467,7 @@
         compiler_params=params(),
         cost_estimate=cost(10**9, 50 * 10**6),
         name="forward",
-    )(weights, *kept(normed, cot, normed_edge, cot_edge))
+    )(weights, *far_memory(normed, near, far, own_c, other_c))
 
 
 def excite_kernel(sums, own_rows, other_rows, coef):
@@ -474,9 +535,9 @@
 
 
 def backward_kernel(
-    coef, weights, normed, act1, slope1, part_p, part_q, proj_grad, w_proj, w_exp, act2,
-    grad_out, pieces, other_out,
-    grad_expanded, copied,
+    coef, weights, normed, act1, slope1, slope2, grad_hidden, proj_grad, w_proj, w_exp, act2,
+    grad_out, pieces_out, other_out,
+    grad_expanded, pieces, other, copied, pieces_copied, other_copied,
     taps, gates, pools, kernel_sums, tap_rows,
 ):
     for block in range(BLOCKS):
@@ -485,10 +546,21 @@
             [[weights[yh, 2 * block + j, 10] for j in range(2)] for yh in range(2)],
             taps,
             block * 128,
-            False,
+            True,
+            0.5,
         )
-        gates[cells, :] = down_rows(coef[0:1, cells])
-        pools[cells, :] = down_rows(coef[1:2, cells])
+        gates[cells, :] = down_rows(coef[0:1, cells] * 0.5)
+        pools[cells, :] = down_rows(coef[1:2, cells] * 0.5)
+    core, _ = tensor_place()
+    cells = pl.ds(pl.multiple_of((1 - core) * (7 * COLS), 7 * COLS), 7 * COLS)
+    gated = (w_proj[...].astype(f32) * (coef[0:1, :] * (0.5 / stretch))).astype(bf16)
+    projected = jnp.dot(gated, act2[:, cells], preferred_element_type=f32).astype(bf16)
+    for row in range(7):
+        other[0, row] = projected[:, row * 128 : row * 128 + 128]
+    other_copies = [
+        pltpu.make_async_copy(other.at[i], other_out.at[i], other_copied.at[i]) for i in range(2)
+    ]
+    other_copies[0].start()
     lane = lanes_of((GROUP, COLS))
 
     def one_group(index, carry):
@@ -497,24 +569,24 @@
         gating = gates[rows, :]
         pooled = pools[rows, :]
         running = {}
+        acts = {}
         sums = [None] * 9
         for m in range(1, ROWS + 3):
             cells = slice((m - 1) * 128, m * 128)
-            grad = part_p[rows, cells].astype(f32) * gating + part_q[rows, cells].astype(f32) * pooled
-            turned = (
-                jnp.where(lane == 127, 0.0, pltpu.roll(grad, 127, 1)),
-                grad,
-                jnp.where(lane == 0, 0.0, pltpu.roll(grad, 1, 1)),
-            )
+            grad = grad_hidden[rows, cells].astype(f32) * gating + pooled
+            grad = grad * slope2[rows, cells].astype(f32)
+            turned = (pltpu.roll(grad, 127, 1), grad, pltpu.roll(grad, 1, 1))
+            for h in ((1, 2) if m == 1 else (m + 1,)):
+                if h <= ROWS + 2:
+                    acts[h] = act1[rows, h * 128 : h * 128 + 128].astype(f32)
             for i in range(3):
                 h = m + i - 1
                 if 2 <= h < ROWS + 2:
                     term = tap[3 * i] * turned[0] + tap[3 * i + 1] * turned[1] + tap[3 * i + 2] * turned[2]
                     running[h] = running[h] + term if h in running else term
                 if 2 <= m < ROWS + 2:
-                    act = act1[rows, h * 128 : h * 128 + 128].astype(f32)
                     for j in range(3):
-                        term = turned[j] * act
+                        term = turned[j] * acts[h]
                         k = 3 * i + j
                         sums[k] = term if sums[k] is None else sums[k] + term
             h = m - 1
@@ -522,29 +594,45 @@
                 out = slice((h - 2) * 128, (h - 1) * 128)
                 grad_expanded[rows, out] = (running.pop(h) * slope1[rows, out].astype(f32)).astype(bf16)
         for k in range(9):
-            kernel_sums[k, rows, :] = sums[k]
+            total = sums[k] * 0.5
+            if k % 3 == 0:
+                total = jnp.where(lane == 127, 0.0, total)
+            if k % 3 == 2:
+                total = jnp.where(lane == 0, 0.0, total)
+            kernel_sums[k, rows, :] = total
         return carry
 
-    lax.fori_loop(0, HALF // GROUP, one_group, 0)
-    copy_out = pltpu.make_async_copy(grad_expanded, grad_out, copied)
-    copy_out.start()
-    core, _ = tensor_place()
-    cells = pl.ds(pl.multiple_of((1 - core) * (7 * COLS), 7 * COLS), 7 * COLS)
-    gated = (w_proj[...].astype(f32) * coef[0:1, :]).astype(bf16)
-    projected = jnp.dot(gated, act2[:, cells], preferred_element_type=f32).astype(bf16)
+    def block_copy(block):
+        rows = pl.ds(pl.multiple_of(block * 128, 128), 128)
+        return pltpu.make_async_copy(grad_expanded.at[rows], grad_out.at[rows], copied.at[block])
+
+    def one_block(block, carry):
+        first = block * (128 // GROUP)
+        lax.fori_loop(0, 128 // GROUP, lambda i, c: one_group(first + i, c), 0, unroll=2)
+        block_copy(block).start()
+        return carry
+
+    lax.fori_loop(0, BLOCKS, one_block, 0)
     grad = jnp.dot(w_exp[...], grad_expanded[:, cells], preferred_element_type=f32).astype(bf16)
     for row in range(7):
-        other_out[0, row] = projected[:, row * 128 : row * 128 + 128]
-        other_out[1, row] = grad[:, row * 128 : row * 128 + 128]
+        other[1, row] = grad[:, row * 128 : row * 128 + 128]
+    other_copies[1].start()
     exp_grad = lax.dot_general(
         normed[...], grad_expanded[...], (((1,), (1,)), ((), ())), preferred_element_type=f32
     )
     low = lanes_of((CH, 128)) < 64
     tap_low = lanes_of((1, 128)) < 64
     tap_rows[...] = jnp.zeros((16, 128), f32)
+
+    def pieces_copy(block):
+        part = pl.ds(2 * block, 2)
+        return pltpu.make_async_copy(
+            pieces.at[:, part], pieces_out.at[:, part], pieces_copied.at[block]
+        )
+
     for block in range(BLOCKS):
         cells = slice(block * 128, block * 128 + 128)
-        scaled = proj_grad[:, cells] * coef[0:1, cells]
+        scaled = proj_grad[:, cells] * (coef[0:1, cells] * (0.5 / stretch))
         first = join_low(exp_grad[:, cells], scaled, low).astype(bf16)
         second = join_high(exp_grad[:, cells], scaled, low).astype(bf16)
         for k in range(9):
@@ -562,17 +650,26 @@
                 pieces[yh, 2 * block + 1, z] = second[rows]
             pieces[yh, 2 * block, 8] = first_taps
             pieces[yh, 2 * block + 1, 8] = second_taps
-    copy_out.wait()
-
-
-def backward(coef, weights, normed, act1, slope1, part_p, part_q, proj_grad, w_proj, w_exp, act2):
+        pieces_copy(block).start()
+    for block in range(BLOCKS):
+        block_copy(block).wait()
+        pieces_copy(block).wait()
+    for copy in other_copies:
+        copy.wait()
+
+
+def backward(coef, weights, normed, act1, slope1, slope2, grad_hidden, proj_grad, w_proj, w_exp, act2):
     return pl.pallas_call(
         backward_kernel,
         in_specs=in_vmem(11),
-        out_specs=in_hbm(1) + in_vmem(2),
+        out_specs=in_hbm(3),
         scratch_shapes=[
             pltpu.VMEM((HALF, ROWS * COLS), bf16),
-            pltpu.SemaphoreType.DMA,
+            pltpu.VMEM((2, 8, 9, 16, 128), bf16),
+            pltpu.VMEM((2, 7, CH, COLS), bf16),
+            pltpu.SemaphoreType.DMA((BLOCKS,)),
+            pltpu.SemaphoreType.DMA((BLOCKS,)),
+            pltpu.SemaphoreType.DMA((2,)),
             pltpu.VMEM((9, HALF, 128), f32),
             pltpu.VMEM((HALF, 128), f32),
             pltpu.VMEM((HALF, 128), f32),
@@ -582,14 +679,14 @@
         out_shape=[
             pltpu.HBM((HALF, ROWS * COLS), bf16),
             pltpu.HBM((2, 8, 9, 16, 128), bf16),
-            jax.ShapeDtypeStruct((2, 7, CH, COLS), bf16),
+            pltpu.HBM((2, 7, CH, COLS), bf16),
         ],
         compiler_params=params(),
         cost_estimate=cost(10**9, 45 * 10**6),
         name="backward",
     )(
         *kept(
-            coef, weights, normed, act1, slope1, part_p, part_q, proj_grad, w_proj, w_exp, act2
+            coef, weights, normed, act1, slope1, slope2, grad_hidden, proj_grad, w_proj, w_exp, act2
         )
     )
 
@@ -597,7 +694,7 @@
 def finish_kernel(coef, w_proj, w_exp, act2, grad_expanded, arrived, x, c, block_out, input_grad, done):
     core, _ = tensor_place()
     cells = pl.ds(pl.multiple_of(core * (7 * COLS), 7 * COLS), 7 * COLS)
-    gated = (w_proj[...].astype(f32) * coef[0:1, :]).astype(bf16)
+    gated = (w_proj[...].astype(f32) * (coef[0:1, :] * (0.5 / stretch))).astype(bf16)
     done[...] = jnp.zeros((8, 128), f32)
     all_projected = jnp.dot(gated, act2[:, cells], preferred_element_type=f32)
     all_grad = jnp.dot(w_exp[...], grad_expanded[:, cells], preferred_element_type=f32)
@@ -705,28 +802,27 @@
 def body(inputs, cotangent, w_expand, w_project, dw_kernel, se_down, se_up):
     swap = [(i, i ^ 1) for i in range(16)]
     edges = [(i, i + 1) for i in range(1, 14, 2)] + [(i + 1, i) for i in range(1, 14, 2)]
-    far_edges = [(i, i + 2) for i in range(1, 14, 2)] + [(i, i - 2) for i in range(2, 16, 2)]
     packed, edge = start(inputs, cotangent, w_expand, w_project, dw_kernel.T, se_down, se_up)
     with jax.named_scope("rows"):
         near = lax.ppermute(edge, "tensor", edges)
-        far = lax.ppermute(edge, "tensor", far_edges)
         other_x = lax.ppermute(inputs, "tensor", swap)
         other_c = lax.ppermute(cotangent, "tensor", swap)
-        normed, cot, main_done = main_norm(inputs, other_x, cotangent, other_c)
-        normed_edge, cot_edge, edge_done = edge_norm(near, far)
+        normed, main_done = main_norm(inputs, other_x)
+        near, edge_done = edge_norm(near, main_done)
+        far = lax.ppermute(near, "tensor", swap)
     with jax.named_scope("weights"):
         lines = exchange(packed, "dp", DEPTH)
-        copies = spread(lines, main_done, edge_done)
+        copies = spread(lines, edge_done)
         weights = exchange(copies, BOTH, PLANE).reshape(2, 8, 11, 16, 128)
     (
-        normed, act1, slope1, act2, part_p, part_q, proj_grad, w_exp, w_proj, own_rows, sums
-    ) = forward(weights, normed, cot, normed_edge, cot_edge)
+        normed, act1, slope1, act2, slope2, grad_hidden, proj_grad, w_exp, w_proj, own_rows, sums
+    ) = forward(weights, normed, near, far, cotangent, other_c)
     with jax.named_scope("sums"):
         other_rows = lax.ppermute(own_rows, "tensor", swap)
         all_sums = exchange(sums, "tensor")
     coef = excite(all_sums, own_rows, other_rows)
     grad_expanded, pieces, partial_out = backward(
-        coef, weights, normed, act1, slope1, part_p, part_q, proj_grad, w_proj, w_exp, act2
+        coef, weights, normed, act1, slope1, slope2, grad_hidden, proj_grad, w_proj, w_exp, act2
     )
     with jax.named_scope("finish"):
         arrived = lax.ppermute(partial_out, "tensor", swap)

time: 107 us -> 103 us (0.963)
  blocking collectives: 41.8 us -> 22.1 us
  waiting for transfers between devices: 9.47 us -> 21 us
  starting transfers between devices: 19.8 us -> 24 us
  Pallas kernels: 28.5 us -> 30.7 us
  local copies, waits for them, and re-layouts: 6.38 us -> 4.19 us
    all_to_all x3 -> x2, blocking collectives: 41.8 us -> 22.1 us  [exchange(): lax.all_to_all(pieces, axes, 0, 0, tiled=True, axis_index_groups=members)]
    all_to_all x2 -> x3, waiting for transfers between devices: 9.45 us -> 19.3 us  [exchange(): lax.all_to_all(pieces, axes, 0, 0, tiled=True, axis_index_groups=members)]
    all_to_all x2 -> x3, starting transfers between devices: 12.8 us -> 18.8 us  [exchange(): lax.all_to_all(pieces, axes, 0, 0, tiled=True, axis_index_groups=members)]
    ppermute x1, starting transfers between devices: 4.18 us -> 0.49 us  [body(): far = lax.ppermute(near, 'tensor', swap)]
    ppermute x1, starting transfers between devices: 1.92 us -> 4.27 us  [body(): near = lax.ppermute(edge, 'tensor', edges)]
    unnamed x22 -> x24, local copies, waits for them, and re-layouts: 6.38 us -> 4.19 us
    pallas_call x5, Pallas kernels: 22.2 us -> 24.3 us  [the longest x1 11.2 us: forward(): pl.pallas_call(forward_kernel, in_specs=in_vmem(1) + in_hbm(5), out_specs...]
    ppermute x1, waiting for transfers between devices: 0.01 us -> 1.3 us  [body(): other_c = lax.ppermute(cotangent, 'tensor', swap)]
  transfers between devices with their start and end apart: 8 -> 9, of which waited for: 2 -> 5; matrix products, arithmetic and copies ran while one was open for 0% -> 0% of each run, Pallas kernels for 5% -> 8%
where the time goes in v3:
time: 103 us
  Pallas kernels  30.7 us (30%)
  starting transfers between devices  24 us (23%)
  blocking collectives  22.1 us (21%)
  waiting for transfers between devices  21 us (20%)
  local copies, waits for them, and re-layouts  4.19 us (4%)
    all_to_all x2, blocking collectives, exchange(): lax.all_to_all(pieces, axes, 0, 0, tiled=True, axis_index_groups=members)  22.1 us
    all_to_all x3, waiting for transfers between devices, exchange(): lax.all_to_all(pieces, axes, 0, 0, tiled=True, axis_index_groups=members)  19.3 us
    all_to_all x3, starting transfers between devices, exchange(): lax.all_to_all(pieces, axes, 0, 0, tiled=True, axis_index_groups=members)  18.8 us
    pallas_call x1, Pallas kernels, forward(): pl.pallas_call(forward_kernel, in_specs=in_vmem(1) + in_hbm(5), out_specs...  11.2 us
    pallas_call x1, Pallas kernels, backward(): pl.pallas_call(backward_kernel, in_specs=in_vmem(11), out_specs=in_hbm(3)...  8.85 us
    ppermute x1, starting transfers between devices, body(): near = lax.ppermute(edge, 'tensor', edges)  4.27 us
    unnamed x24, local copies, waits for them, and re-layouts  4.19 us
    pallas_call x1, Pallas kernels, finish(): pl.pallas_call(finish_kernel, in_specs=in_vmem(8), out_specs=in_vmem(3),...  3.14 us
  transfers between devices with their start and end apart: 9, of which 5 were waited for; matrix products, arithmetic and copies ran while one was open for 0% of the time, Pallas kernels for 8%

profile of v3, /device:TPU:2, one launch (start us, length us, event | category | flops | bytes accessed | tf_op | source)
XLA Modules:
  0.0 102.7 jit_solution(18009516100051206209)
XLA Ops:
  0.6 0.1 collective-permute-start.1
  0.7 0.0 copy-start.1
  0.7 1.8 %start.1 = (bf16[8,32,128]{2,1,0:T(8,128)(2,1)}, bf16[2,2,1,256,128]{4,3,2,1,0:T(8,128)(2,1)S(1)}) custom-call(bf16[7,1,256,128]{3,2,1,0:T(8,128)(2,1)} %x.3, bf16[7,1,256,128]{3,2,1,0:T(8,128)(2,1)} %c.3, bf16[16,64]{1,0:T(8,128)(2,1)} %w_expand.1, bf16[16,64]{1,0:T(8,128)(2,1)} %w_project.1, bf16[9,64]{1,0:T(8,128)(2,1)} %bitcast.7, ...), custom_call_target="tpu_custom_call" | custom-call | flops 100000 | bytes 100000 | tf_op jit(solution)/shard_map/start/pallas_call | solution.py:179
  2.5 4.3 %collective-permute-start = (bf16[2,2,1,256,128]{4,3,2,1,0:T(8,128)(2,1)S(1)}, bf16[2,2,1,256,128]{4,3,2,1,0:T(8,128)(2,1)S(1)}, u32[]{:S(2)}, u32[]{:S(2)}) collective-permute-start(bf16[2,2,1,256,128]{4,3,2,1,0:T(8,128)(2,1)S(1)} %get-tuple-element.36), channel_id=1, source_target_pairs={{1,2},{3,4},{5,6},{7,8},{9,10},{11,12},{13,14},{2,1},{4,3},{6,5},{... | collective-permute-start | bytes 786440 | tf_op jit(solution)/shard_map/rows/ppermute | solution.py:807
  6.8 6.7 %all-to-all-start = ((bf16[8,32,128]{2,1,0:T(8,128)(2,1)}), bf16[8,32,128]{2,1,0:T(8,128)(2,1)S(1)}, u32[]{:S(2)}, u32[]{:S(2)}) async-start(bf16[8,32,128]{2,1,0:T(8,128)(2,1)} %get-tuple-element.35), calls=%async_computation | async-start | bytes 131072 | tf_op jit(solution)/shard_map/weights/all_to_all | solution.py:46
  13.6 0.0 collective-permute-done.1.other_x
  13.6 0.0 copy-start.8
  13.6 0.8 copy-done.8
  14.3 2.4 %main_norm.1 = (bf16[256,1792]{1,0:T(8,128)(2,1)}, f32[8,128]{1,0:T(8,128)S(1)}) custom-call(bf16[7,1,256,128]{3,2,1,0:T(8,128)(2,1)} %x.3, bf16[7,1,256,128]{3,2,1,0:T(8,128)(2,1)} %copy-done.8), custom_call_target="tpu_custom_call" | custom-call | flops 100000 | bytes 100000 | tf_op jit(solution)/shard_map/rows/main_norm/pallas_call | solution.py:267
  16.8 0.0 collective-permute-done.near
  16.8 0.8 edge_norm.1
  17.7 0.0 copy-start.10
  17.7 4.7 %all-to-all-done.lines = bf16[8,32,128]{2,1,0:T(8,128)(2,1)S(1)} async-done(((bf16[8,32,128]{2,1,0:T(8,128)(2,1)}), bf16[8,32,128]{2,1,0:T(8,128)(2,1)S(1)}, u32[]{:S(2)}, u32[]{:S(2)}) %all-to-all-start) | async-done | bytes 65568 | tf_op jit(solution)/shard_map/weights/all_to_all | solution.py:46
  22.4 1.0 spread.1
  23.3 7.2 %all-to-all-start.1 = ((bf16[16,11,16,128]{3,2,1,0:T(8,128)(2,1)}), bf16[16,11,16,128]{3,2,1,0:T(8,128)(2,1)S(1)}, u32[]{:S(2)}, u32[]{:S(2)}) async-start(bf16[16,11,16,128]{3,2,1,0:T(8,128)(2,1)} %spread.1), calls=%async_computation.1 | async-start | bytes 1441792 | tf_op jit(solution)/shard_map/weights/all_to_all | solution.py:46
  30.5 0.0 copy-done.1
  30.5 0.1 collective-permute-start.3
  30.6 0.0 copy-done.10
  30.7 0.5 collective-permute-start.2
  31.1 1.3 %collective-permute-done.3.other_c = bf16[7,1,256,128]{3,2,1,0:T(8,128)(2,1)S(1)} collective-permute-done((bf16[7,1,256,128]{3,2,1,0:T(8,128)(2,1)S(1)}, bf16[7,1,256,128]{3,2,1,0:T(8,128)(2,1)S(1)}, u32[]{:S(2)}, u32[]{:S(2)}) %collective-permute-start.3) | collective-permute-done | bytes 458784 | tf_op jit(solution)/shard_map/rows/ppermute | solution.py:809
  32.4 0.0 copy-start.9
  32.5 0.4 collective-permute-done.2.far_in
  32.8 0.0 copy-start.11
  32.8 9.3 %all-to-all-done.1 = bf16[16,11,16,128]{3,2,1,0:T(8,128)(2,1)S(1)} async-done(((bf16[16,11,16,128]{3,2,1,0:T(8,128)(2,1)}), bf16[16,11,16,128]{3,2,1,0:T(8,128)(2,1)S(1)}, u32[]{:S(2)}, u32[]{:S(2)}) %all-to-all-start.1) | async-done | bytes 720928 | tf_op jit(solution)/shard_map/weights/all_to_all | solution.py:46
  42.1 0.0 copy-done.11
  42.1 0.0 copy-done.9
  42.1 11.2 %forward.1 = (bf16[256,1792]{1,0:T(8,128)(2,1)S(1)}, bf16[512,2304]{1,0:T(8,128)(2,1)S(1)}, bf16[512,1792]{1,0:T(8,128)(2,1)S(1)}, bf16[512,1792]{1,0:T(8,128)(2...) custom-call(bf16[2,8,11,16,128]{4,3,2,1,0:T(8,128)(2,1)S(1)} %bitcas, ...), custom_call_target="tpu_custom_call" | custom-call | flops 1000000000 | bytes 50000000 | tf_op jit(solution)/shard_map/forward/pallas_call | solution.py:438
  53.4 0.0 copy-start.4
  53.4 0.0 copy-start.6
  53.4 0.1 collective-permute-start.4
  53.5 8.7 %all_to_all.25.sums = f32[16,8,128]{2,1,0:T(8,128)S(1)} all-to-all(f32[16,8,128]{2,1,0:T(8,128)S(1)} %get-tuple-element.41), channel_id=1, replica_groups=mesh['dp'=16,'tensor'=16] {'tensor'}, dimensions={0} | all-to-all | bytes 131072 | tf_op jit(solution)/shard_map/sums/all_to_all | solution.py:46
  62.2 0.0 collective-permute-done.4.other_rows
  62.2 0.5 excite.1.coef
  62.8 0.0 copy-start
  62.8 0.0 copy-start.2
  62.8 8.9 %backward.1 = (bf16[512,1792]{1,0:T(8,128)(2,1)}, bf16[2,8,9,16,128]{4,3,2,1,0:T(8,128)(2,1)}, bf16[2,7,256,128]{3,2,1,0:T(8,128)(2,1)}) custom-call(f32[8,512]{1,0:T(8,128)S(1)} %excite.1.coef, bf16[2,8,11,16,128]{4,3,2,1,0:T(8,128)(2,1)S(1)} %bitcast.5, bf16[256,1792]{1,0:T(8,128)(2,1)S(1)} %get-tuple-element.46.normed, ...), custom_call_target="tpu_custom_call" | custom-call | flops 1000000000 | bytes 45000000 | tf_op jit(solution)/shard_map/backward/pallas_call | solution.py:662
  71.6 0.0 copy-done.4
  71.6 0.0 copy-done.6
  71.6 0.2 collective-permute-start.5
  71.8 4.8 %all-to-all-start.3 = ((bf16[16,9,16,128]{3,2,1,0:T(8,128)(2,1)}), bf16[16,9,16,128]{3,2,1,0:T(8,128)(2,1)S(1)}, u32[]{:S(2)}, u32[]{:S(2)}) async-start(bf16[16,9,16,128]{3,2,1,0:T(8,128)(2,1)} %bitcast.6), calls=%async_computation.3 | async-start | bytes 1179648 | tf_op jit(solution)/shard_map/gradients/all_to_all | solution.py:46
  76.6 0.0 collective-permute-done.5.arrived
  76.7 0.0 copy-done
  76.7 0.0 copy-done.2
  76.7 0.0 copy-start.3
  76.7 1.5 %copy-done.3 = bf16[512,1792]{1,0:T(8,128)(2,1)S(1)} copy-done((bf16[512,1792]{1,0:T(8,128)(2,1)S(1)}, bf16[512,1792]{1,0:T(8,128)(2,1)}, u32[]{:S(2)}) %copy-start.3) | copy-done | bytes 1835032
  78.2 0.0 copy-start.5
  78.2 0.9 copy-done.5
  79.1 0.0 copy-start.7
  79.1 0.9 copy-done.7
  80.1 3.1 %finish.1 = (bf16[7,1,256,128]{3,2,1,0:T(8,128)(2,1)}, bf16[7,1,256,128]{3,2,1,0:T(8,128)(2,1)}, f32[8,128]{1,0:T(8,128)S(1)}) custom-call(f32[8,512]{1,0:T(8,128)S(1)} %excite.1.coef, bf16[256,512]{1,0:T(8,128)(2,1)S(1)} %copy-done.7, bf16[256,512]{1,0:T(8,128)(2,1)S(1)} %copy-done.5, bf16[512,1792]{1,0:T(8,128)(2,1)S(1)} %get-tuple-element.45.act2, ...), custom_call_target="tpu_custom_call" | custom-call | flops 100000 | bytes 100000 | tf_op jit(solution)/shard_map/finish/finish/pallas_call | solution.py:717
  83.2 5.3 %all-to-all-done.3.pieces = bf16[16,9,16,128]{3,2,1,0:T(8,128)(2,1)S(1)} async-done(((bf16[16,9,16,128]{3,2,1,0:T(8,128)(2,1)}), bf16[16,9,16,128]{3,2,1,0:T(8,128)(2,1)S(1)}, u32[]{:S(2)}, u32[]{:S(2)}) %all-to-all-start.3) | async-done | bytes 589856 | tf_op jit(solution)/shard_map/gradients/all_to_all | solution.py:46
  88.5 0.2 middle.1
  88.7 13.4 %all_to_all.26.lines = bf16[8,6,16,128]{3,2,1,0:T(8,128)(2,1)S(1)} all-to-all(bf16[8,6,16,128]{3,2,1,0:T(8,128)(2,1)S(1)} %middle.1), channel_id=1, replica_groups={{0,32,64,96,128,160,192,224},{16,48,80,112,144,176,208,240},{1,33,65,97..., dimensions={0} | all-to-all | bytes 393216 | tf_op jit(solution)/shard_map/gradients/all_to_all | solution.py:46
  102.0 0.7 tail.1
Async XLA Ops:
  0.6 12.9 %collective-permute-start.1 = (bf16[7,1,256,128]{3,2,1,0:T(8,128)(2,1)}, bf16[7,1,256,128]{3,2,1,0:T(8,128)(2,1)S(1)}, u32[]{:S(2)}, u32[]{:S(2)}) collective-permute-start(bf16[7,1,256,128]{3,2,1,0:T(8,128)(2,1)} %x.3), channel_id=1, source_target_pairs={{0,1},{1,0},{2,3},{3,2},{4,5},{5,4},{6,7},{7,6},{8,9},{9,8},{10,11... | collective-permute-start | bytes 1376264 | tf_op jit(solution)/shard_map/rows/ppermute | solution.py:808
  0.7 29.8 %copy-start.1 = (bf16[7,1,256,128]{3,2,1,0:T(8,128)(2,1)S(1)}, bf16[7,1,256,128]{3,2,1,0:T(8,128)(2,1)}, u32[]{:S(2)}) copy-start(bf16[7,1,256,128]{3,2,1,0:T(8,128)(2,1)} %c.3) | copy-start | bytes 1376260
  2.5 14.3 %collective-permute-start = (bf16[2,2,1,256,128]{4,3,2,1,0:T(8,128)(2,1)S(1)}, bf16[2,2,1,256,128]{4,3,2,1,0:T(8,128)(2,1)S(1)}, u32[]{:S(2)}, u32[]{:S(2)}) collective-permute-start(bf16[2,2,1,256,128]{4,3,2,1,0:T(8,128)(2,1)S(1)} %get-tuple-element.36), channel_id=1, source_target_pairs={{1,2},{3,4},{5,6},{7,8},{9,10},{11,12},{13,14},{2,1},{4,3},{6,5},{... | collective-permute-start | bytes 786440 | tf_op jit(solution)/shard_map/rows/ppermute | solution.py:807
  6.8 15.6 %all-to-all-start = ((bf16[8,32,128]{2,1,0:T(8,128)(2,1)}), bf16[8,32,128]{2,1,0:T(8,128)(2,1)S(1)}, u32[]{:S(2)}, u32[]{:S(2)}) async-start(bf16[8,32,128]{2,1,0:T(8,128)(2,1)} %get-tuple-element.35), calls=%async_computation | async-start | bytes 131072 | tf_op jit(solution)/shard_map/weights/all_to_all | solution.py:46
  13.6 0.8 copy-start.8
  17.7 13.0 %copy-start.10 = (bf16[2,256,256]{2,1,0:T(8,128)(2,1)S(1)}, bf16[2,256,256]{2,1,0:T(8,128)(2,1)}, u32[]{:S(2)}) copy-start(bf16[2,256,256]{2,1,0:T(8,128)(2,1)} %get-tuple-element.40.near_in) | copy-start | bytes 786436
  23.3 18.8 %all-to-all-start.1 = ((bf16[16,11,16,128]{3,2,1,0:T(8,128)(2,1)}), bf16[16,11,16,128]{3,2,1,0:T(8,128)(2,1)S(1)}, u32[]{:S(2)}, u32[]{:S(2)}) async-start(bf16[16,11,16,128]{3,2,1,0:T(8,128)(2,1)} %spread.1), calls=%async_computation.1 | async-start | bytes 1441792 | tf_op jit(solution)/shard_map/weights/all_to_all | solution.py:46
  30.5 1.9 %collective-permute-start.3 = (bf16[7,1,256,128]{3,2,1,0:T(8,128)(2,1)S(1)}, bf16[7,1,256,128]{3,2,1,0:T(8,128)(2,1)S(1)}, u32[]{:S(2)}, u32[]{:S(2)}) collective-permute-start(bf16[7,1,256,128]{3,2,1,0:T(8,128)(2,1)S(1)} %copy-done.1), channel_id=1, source_target_pairs={{0,1},{1,0},{2,3},{3,2},{4,5},{5,4},{6,7},{7,6},{8,9},{9,8},{10,11... | collective-permute-start | bytes 1376264 | tf_op jit(solution)/shard_map/rows/ppermute | solution.py:809
  30.7 2.2 %collective-permute-start.2 = (bf16[2,256,256]{2,1,0:T(8,128)(2,1)S(1)}, bf16[2,256,256]{2,1,0:T(8,128)(2,1)S(1)}, u32[]{:S(2)}, u32[]{:S(2)}) collective-permute-start(bf16[2,256,256]{2,1,0:T(8,128)(2,1)S(1)} %copy-done.10), channel_id=1, source_target_pairs={{0,1},{1,0},{2,3},{3,2},{4,5},{5,4},{6,7},{7,6},{8,9},{9,8},{10,11... | collective-permute-start | bytes 786440 | tf_op jit(solution)/shard_map/rows/ppermute | solution.py:812
  32.4 9.7 %copy-start.9 = (bf16[7,1,256,128]{3,2,1,0:T(8,128)(2,1)}, bf16[7,1,256,128]{3,2,1,0:T(8,128)(2,1)S(1)}, u32[]{:S(2)}) copy-start(bf16[7,1,256,128]{3,2,1,0:T(8,128)(2,1)S(1)} %collective-permute-done.3.other_c) | copy-start | bytes 1376260
  32.8 9.3 %copy-start.11 = (bf16[2,256,256]{2,1,0:T(8,128)(2,1)}, bf16[2,256,256]{2,1,0:T(8,128)(2,1)S(1)}, u32[]{:S(2)}) copy-start(bf16[2,256,256]{2,1,0:T(8,128)(2,1)S(1)} %collective-permute-done.2.far_in) | copy-start | bytes 786436
  53.4 18.2 %copy-start.4 = (bf16[256,512]{1,0:T(8,128)(2,1)}, bf16[256,512]{1,0:T(8,128)(2,1)S(1)}, u32[]{:S(2)}) copy-start(bf16[256,512]{1,0:T(8,128)(2,1)S(1)} %get-tuple-element.44.w_exp) | copy-start | bytes 786436
  53.4 18.2 %copy-start.6 = (bf16[256,512]{1,0:T(8,128)(2,1)}, bf16[256,512]{1,0:T(8,128)(2,1)S(1)}, u32[]{:S(2)}) copy-start(bf16[256,512]{1,0:T(8,128)(2,1)S(1)} %get-tuple-element.43.w_proj) | copy-start | bytes 786436
  53.4 8.8 %collective-permute-start.4 = (bf16[2,8,2,16,128]{4,3,2,1,0:T(8,128)(2,1)S(1)}, bf16[2,8,2,16,128]{4,3,2,1,0:T(8,128)(2,1)S(1)}, u32[]{:S(2)}, u32[]{:S(2)}) collective-permute-start(bf16[2,8,2,16,128]{4,3,2,1,0:T(8,128)(2,1)S(1)} %get-tuple-element.42.own_rows), channel_id=1, source_target_pairs={{0,1},{1,0},{2,3},{3,2},{4,5},{5,4},{6,7},{7,6},{8,9},{9,8},{10,11... | collective-permute-start | bytes 393224 | tf_op jit(solution)/shard_map/sums/ppermute | solution.py:821
  62.8 13.9 %copy-start = (bf16[7,1,256,128]{3,2,1,0:T(8,128)(2,1)S(1)}, bf16[7,1,256,128]{3,2,1,0:T(8,128)(2,1)}, u32[]{:S(2)}) copy-start(bf16[7,1,256,128]{3,2,1,0:T(8,128)(2,1)} %x.3) | copy-start | bytes 1376260
  62.8 13.9 %copy-start.2 = (bf16[7,1,256,128]{3,2,1,0:T(8,128)(2,1)S(1)}, bf16[7,1,256,128]{3,2,1,0:T(8,128)(2,1)}, u32[]{:S(2)}) copy-start(bf16[7,1,256,128]{3,2,1,0:T(8,128)(2,1)} %c.3) | copy-start | bytes 1376260
  71.6 5.0 %collective-permute-start.5 = (bf16[2,7,256,128]{3,2,1,0:T(8,128)(2,1)}, bf16[2,7,256,128]{3,2,1,0:T(8,128)(2,1)}, u32[]{:S(2)}, u32[]{:S(2)}) collective-permute-start(bf16[2,7,256,128]{3,2,1,0:T(8,128)(2,1)} %get-tuple-element.53), channel_id=1, source_target_pairs={{0,1},{1,0},{2,3},{3,2},{4,5},{5,4},{6,7},{7,6},{8,9},{9,8},{10,11... | collective-permute-start | bytes 2752520 | tf_op jit(solution)/shard_map/finish/ppermute | solution.py:828
  71.8 16.7 %all-to-all-start.3 = ((bf16[16,9,16,128]{3,2,1,0:T(8,128)(2,1)}), bf16[16,9,16,128]{3,2,1,0:T(8,128)(2,1)S(1)}, u32[]{:S(2)}, u32[]{:S(2)}) async-start(bf16[16,9,16,128]{3,2,1,0:T(8,128)(2,1)} %bitcast.6), calls=%async_computation.3 | async-start | bytes 1179648 | tf_op jit(solution)/shard_map/gradients/all_to_all | solution.py:46
  76.7 1.5 %copy-start.3 = (bf16[512,1792]{1,0:T(8,128)(2,1)S(1)}, bf16[512,1792]{1,0:T(8,128)(2,1)}, u32[]{:S(2)}) copy-start(bf16[512,1792]{1,0:T(8,128)(2,1)} %get-tuple-element.52.grad_expanded) | copy-start | bytes 5505028
  78.2 0.9 copy-start.5
  79.1 0.9 copy-start.7

commit v4 on v3

--- a/solution.py
+++ b/solution.py
@@ -325,7 +325,7 @@
 def forward_kernel(
     weights, normed_in, near_in, far_in, own_c, other_c,
     normed, act1, slope1, act2, slope2, grad_hidden, proj_grad, w_exp, w_proj, squeeze_rows, sums,
-    cot, own_c_in, other_c_in, near, far, expanded, taps, pool, gate, sems,
+    cot, own_c_in, other_c_in, near, far, expanded, taps, sems,
 ):
     core, chip = tensor_place()
     copies = copy_all(
@@ -367,20 +367,9 @@
     near_first = core == 0
     multiply(w_exp, jnp.where(near_first, near[0], far[0]), expanded, 0)
     multiply(w_exp, jnp.where(near_first, far[0], near[0]), expanded, ROWS + 2)
-    above = jnp.where(near_first, near[1, :, 128:256], far[1, :, 128:256])
-    below = jnp.where(near_first, far[1, :, 0:128], near[1, :, 0:128])
-    multiply(w_proj, above, grad_hidden, 0)
-    multiply(w_proj, below, grad_hidden, ROWS + 1)
     for part in range(ROWS // 2):
         cells = slice(part * 256, part * 256 + 256)
         multiply(w_exp, normed[:, cells], expanded, 2 + 2 * part)
-    for copy, c, first in ((copies[3], own_c_in, 7 * core), (copies[4], other_c_in, 7 - 7 * core)):
-        copy.wait()
-        for row in range(7):
-            cot[:, lane_block(first + row)] = c[row, 0]
-    for part in range(ROWS // 2):
-        cells = slice(part * 256, part * 256 + 256)
-        multiply(w_proj, cot[:, cells], grad_hidden, 1 + 2 * part)
     first_chip = jnp.where(chip > 0, 1.0, 0.0)
     last_chip = jnp.where(chip < 7, 1.0, 0.0)
 
@@ -388,8 +377,6 @@
         rows = pl.ds(pl.multiple_of(index * GROUP, GROUP), GROUP)
         tap = [taps[k, rows, :] for k in range(9)]
         running = {}
-        pool_sum = jnp.zeros((GROUP, COLS), f32)
-        gate_sum = jnp.zeros((GROUP, COLS), f32)
         for h in range(EXT):
             act, slope = gelu_pair(expanded[rows, h * 128 : h * 128 + 128])
             act1[rows, h * 128 : h * 128 + 128] = act.astype(bf16)
@@ -414,24 +401,33 @@
             slope2[rows, (m - 1) * 128 : m * 128] = slope.astype(bf16)
             if 2 <= m < ROWS + 2:
                 act2[rows, (m - 2) * 128 : (m - 1) * 128] = act.astype(bf16)
-                pool_sum = pool_sum + act
-                grad = grad_hidden[rows, (m - 1) * 128 : m * 128].astype(f32)
-                gate_sum = gate_sum + act * grad
-        pool[rows, :] = pool_sum
-        gate[rows, :] = gate_sum
         return carry
 
     lax.fori_loop(0, HALF // GROUP, one_group, 0, unroll=2)
-    for block in range(BLOCKS):
-        cells = slice(block * 128, block * 128 + 128)
-        pool_row = jnp.sum(pool[cells, :].T, axis=0, keepdims=True) * (0.5 / stretch)
-        gate_row = jnp.sum(gate[cells, :].T, axis=0, keepdims=True) * (0.5 / stretch)
-        for other in range(16):
-            sums[other, block : block + 1, :] = pool_row
-            sums[other, BLOCKS + block : BLOCKS + block + 1, :] = gate_row
-    proj_grad[...] = lax.dot_general(
+    cot[CH : CH + 16, :] = jnp.ones((16, ROWS * COLS), bf16)
+    for copy, c, first in ((copies[3], own_c_in, 7 * core), (copies[4], other_c_in, 7 - 7 * core)):
+        copy.wait()
+        for row in range(7):
+            cot[0:CH, lane_block(first + row)] = c[row, 0]
+    products = lax.dot_general(
         cot[...], act2[...], (((1,), (1,)), ((), ())), preferred_element_type=f32
     )
+    proj_grad[...] = products[0:CH]
+    pool = products[CH : CH + 1] * (0.5 / stretch)
+    gate = jnp.sum(products[0:CH] * w_proj[...].astype(f32), axis=0, keepdims=True)
+    gate = gate * (0.5 / stretch)
+    for other in range(16):
+        for block in range(BLOCKS):
+            cells = slice(block * 128, block * 128 + 128)
+            sums[other, block : block + 1, :] = pool[:, cells]
+            sums[other, BLOCKS + block : BLOCKS + block + 1, :] = gate[:, cells]
+    above = jnp.where(near_first, near[1, :, 128:256], far[1, :, 128:256])
+    below = jnp.where(near_first, far[1, :, 0:128], near[1, :, 0:128])
+    multiply(w_proj, above, grad_hidden, 0)
+    multiply(w_proj, below, grad_hidden, ROWS + 1)
+    for part in range(ROWS // 2):
+        cells = slice(part * 256, part * 256 + 256)
+        multiply(w_proj, cot[0:CH, cells], grad_hidden, 1 + 2 * part)
 
 
 def forward(weights, normed, near, far, own_c, other_c):
@@ -440,15 +436,13 @@
         in_specs=in_vmem(1) + in_hbm(5),
         out_specs=in_vmem(11),
         scratch_shapes=[
-            pltpu.VMEM((CH, ROWS * COLS), bf16),
+            pltpu.VMEM((CH + 16, ROWS * COLS), bf16),
             pltpu.VMEM((7, 1, CH, COLS), bf16),
             pltpu.VMEM((7, 1, CH, COLS), bf16),
             pltpu.VMEM((2, CH, 2 * COLS), bf16),
             pltpu.VMEM((2, CH, 2 * COLS), bf16),
             pltpu.VMEM((HALF, EXT * COLS), f32),
             pltpu.VMEM((9, HALF, 128), f32),
-            pltpu.VMEM((HALF, 128), f32),
-            pltpu.VMEM((HALF, 128), f32),
             pltpu.SemaphoreType.DMA((5,)),
         ],
         out_shape=[

time: 103 us -> 103 us (level)
  no operation moved by 1% of the time
where the time goes in v4:
time: 103 us; the launch traced here: 102 us
  Pallas kernels  30 us (29%)
  starting transfers between devices  24 us (23%)
  blocking collectives  22.1 us (21%)
  waiting for transfers between devices  21 us (20%)
  local copies, waits for them, and re-layouts  4.19 us (4%)
    all_to_all x2, blocking collectives, exchange(): lax.all_to_all(pieces, axes, 0, 0, tiled=True, axis_index_groups=members)  22.1 us
    all_to_all x3, waiting for transfers between devices, exchange(): lax.all_to_all(pieces, axes, 0, 0, tiled=True, axis_index_groups=members)  19.3 us
    all_to_all x3, starting transfers between devices, exchange(): lax.all_to_all(pieces, axes, 0, 0, tiled=True, axis_index_groups=members)  18.8 us
    pallas_call x1, Pallas kernels, forward(): pl.pallas_call(forward_kernel, in_specs=in_vmem(1) + in_hbm(5), out_specs...  10.5 us
    pallas_call x1, Pallas kernels, backward(): pl.pallas_call(backward_kernel, in_specs=in_vmem(11), out_specs=in_hbm(3)...  8.85 us
    ppermute x1, starting transfers between devices, body(): near = lax.ppermute(edge, 'tensor', edges)  4.27 us
    unnamed x24, local copies, waits for them, and re-layouts  4.19 us
    pallas_call x1, Pallas kernels, finish(): pl.pallas_call(finish_kernel, in_specs=in_vmem(8), out_specs=in_vmem(3),...  3.14 us
  transfers between devices with their start and end apart: 9, of which 5 were waited for; matrix products, arithmetic and copies ran while one was open for 0% of the time, Pallas kernels for 8%

profile of v4, /device:TPU:2, one launch (start us, length us, event | category | flops | bytes accessed | tf_op | source)
XLA Modules:
  0.0 102.0 jit_solution(10241756916968995631)
XLA Ops:
  0.6 0.1 collective-permute-start.1
  0.7 0.0 copy-start.1
  0.7 1.8 %start.1 = (bf16[8,32,128]{2,1,0:T(8,128)(2,1)}, bf16[2,2,1,256,128]{4,3,2,1,0:T(8,128)(2,1)S(1)}) custom-call(bf16[7,1,256,128]{3,2,1,0:T(8,128)(2,1)} %x.3, bf16[7,1,256,128]{3,2,1,0:T(8,128)(2,1)} %c.3, bf16[16,64]{1,0:T(8,128)(2,1)} %w_expand.1, bf16[16,64]{1,0:T(8,128)(2,1)} %w_project.1, bf16[9,64]{1,0:T(8,128)(2,1)} %bitcast.7, ...), custom_call_target="tpu_custom_call" | custom-call | flops 100000 | bytes 100000 | tf_op jit(solution)/shard_map/start/pallas_call | solution.py:179
  2.5 4.3 %collective-permute-start = (bf16[2,2,1,256,128]{4,3,2,1,0:T(8,128)(2,1)S(1)}, bf16[2,2,1,256,128]{4,3,2,1,0:T(8,128)(2,1)S(1)}, u32[]{:S(2)}, u32[]{:S(2)}) collective-permute-start(bf16[2,2,1,256,128]{4,3,2,1,0:T(8,128)(2,1)S(1)} %get-tuple-element.36), channel_id=1, source_target_pairs={{1,2},{3,4},{5,6},{7,8},{9,10},{11,12},{13,14},{2,1},{4,3},{6,5},{... | collective-permute-start | bytes 786440 | tf_op jit(solution)/shard_map/rows/ppermute | solution.py:801
  6.8 6.7 %all-to-all-start = ((bf16[8,32,128]{2,1,0:T(8,128)(2,1)}), bf16[8,32,128]{2,1,0:T(8,128)(2,1)S(1)}, u32[]{:S(2)}, u32[]{:S(2)}) async-start(bf16[8,32,128]{2,1,0:T(8,128)(2,1)} %get-tuple-element.35), calls=%async_computation | async-start | bytes 131072 | tf_op jit(solution)/shard_map/weights/all_to_all | solution.py:46
  13.6 0.0 collective-permute-done.1.other_x
  13.6 0.0 copy-start.8
  13.6 0.8 copy-done.8
  14.3 2.4 %main_norm.1 = (bf16[256,1792]{1,0:T(8,128)(2,1)}, f32[8,128]{1,0:T(8,128)S(1)}) custom-call(bf16[7,1,256,128]{3,2,1,0:T(8,128)(2,1)} %x.3, bf16[7,1,256,128]{3,2,1,0:T(8,128)(2,1)} %copy-done.8), custom_call_target="tpu_custom_call" | custom-call | flops 100000 | bytes 100000 | tf_op jit(solution)/shard_map/rows/main_norm/pallas_call | solution.py:267
  16.8 0.0 collective-permute-done.near
  16.8 0.8 edge_norm.1
  17.7 0.0 copy-start.10
  17.7 4.7 %all-to-all-done.lines = bf16[8,32,128]{2,1,0:T(8,128)(2,1)S(1)} async-done(((bf16[8,32,128]{2,1,0:T(8,128)(2,1)}), bf16[8,32,128]{2,1,0:T(8,128)(2,1)S(1)}, u32[]{:S(2)}, u32[]{:S(2)}) %all-to-all-start) | async-done | bytes 65568 | tf_op jit(solution)/shard_map/weights/all_to_all | solution.py:46
  22.4 1.0 spread.1
  23.3 7.2 %all-to-all-start.1 = ((bf16[16,11,16,128]{3,2,1,0:T(8,128)(2,1)}), bf16[16,11,16,128]{3,2,1,0:T(8,128)(2,1)S(1)}, u32[]{:S(2)}, u32[]{:S(2)}) async-start(bf16[16,11,16,128]{3,2,1,0:T(8,128)(2,1)} %spread.1), calls=%async_computation.1 | async-start | bytes 1441792 | tf_op jit(solution)/shard_map/weights/all_to_all | solution.py:46
  30.5 0.0 copy-done.1
  30.5 0.1 collective-permute-start.3
  30.6 0.0 copy-done.10
  30.7 0.5 collective-permute-start.2
  31.1 1.3 %collective-permute-done.3.other_c = bf16[7,1,256,128]{3,2,1,0:T(8,128)(2,1)S(1)} collective-permute-done((bf16[7,1,256,128]{3,2,1,0:T(8,128)(2,1)S(1)}, bf16[7,1,256,128]{3,2,1,0:T(8,128)(2,1)S(1)}, u32[]{:S(2)}, u32[]{:S(2)}) %collective-permute-start.3) | collective-permute-done | bytes 458784 | tf_op jit(solution)/shard_map/rows/ppermute | solution.py:803
  32.4 0.0 copy-start.9
  32.5 0.4 collective-permute-done.2.far_in
  32.8 0.0 copy-start.11
  32.8 9.3 %all-to-all-done.1 = bf16[16,11,16,128]{3,2,1,0:T(8,128)(2,1)S(1)} async-done(((bf16[16,11,16,128]{3,2,1,0:T(8,128)(2,1)}), bf16[16,11,16,128]{3,2,1,0:T(8,128)(2,1)S(1)}, u32[]{:S(2)}, u32[]{:S(2)}) %all-to-all-start.1) | async-done | bytes 720928 | tf_op jit(solution)/shard_map/weights/all_to_all | solution.py:46
  42.1 0.0 copy-done.11
  42.1 0.0 copy-done.9
  42.1 10.5 %forward.1 = (bf16[256,1792]{1,0:T(8,128)(2,1)S(1)}, bf16[512,2304]{1,0:T(8,128)(2,1)S(1)}, bf16[512,1792]{1,0:T(8,128)(2,1)S(1)}, bf16[512,1792]{1,0:T(8,128)(2...) custom-call(bf16[2,8,11,16,128]{4,3,2,1,0:T(8,128)(2,1)S(1)} %bitcas, ...), custom_call_target="tpu_custom_call" | custom-call | flops 1000000000 | bytes 50000000 | tf_op jit(solution)/shard_map/forward/pallas_call | solution.py:434
  52.7 0.0 copy-start.4
  52.7 0.0 copy-start.6
  52.7 0.1 collective-permute-start.4
  52.8 8.7 %all_to_all.25.sums = f32[16,8,128]{2,1,0:T(8,128)S(1)} all-to-all(f32[16,8,128]{2,1,0:T(8,128)S(1)} %get-tuple-element.41), channel_id=1, replica_groups=mesh['dp'=16,'tensor'=16] {'tensor'}, dimensions={0} | all-to-all | bytes 131072 | tf_op jit(solution)/shard_map/sums/all_to_all | solution.py:46
  61.5 0.0 collective-permute-done.4.other_rows
  61.5 0.5 excite.1.coef
  62.0 0.0 copy-start
  62.0 0.0 copy-start.2
  62.0 8.9 %backward.1 = (bf16[512,1792]{1,0:T(8,128)(2,1)}, bf16[2,8,9,16,128]{4,3,2,1,0:T(8,128)(2,1)}, bf16[2,7,256,128]{3,2,1,0:T(8,128)(2,1)}) custom-call(f32[8,512]{1,0:T(8,128)S(1)} %excite.1.coef, bf16[2,8,11,16,128]{4,3,2,1,0:T(8,128)(2,1)S(1)} %bitcast.5, bf16[256,1792]{1,0:T(8,128)(2,1)S(1)} %get-tuple-element.46.normed, ...), custom_call_target="tpu_custom_call" | custom-call | flops 1000000000 | bytes 45000000 | tf_op jit(solution)/shard_map/backward/pallas_call | solution.py:656
  70.9 0.0 copy-done.4
  70.9 0.0 copy-done.6
  70.9 0.2 collective-permute-start.5
  71.1 4.8 %all-to-all-start.3 = ((bf16[16,9,16,128]{3,2,1,0:T(8,128)(2,1)}), bf16[16,9,16,128]{3,2,1,0:T(8,128)(2,1)S(1)}, u32[]{:S(2)}, u32[]{:S(2)}) async-start(bf16[16,9,16,128]{3,2,1,0:T(8,128)(2,1)} %bitcast.6), calls=%async_computation.3 | async-start | bytes 1179648 | tf_op jit(solution)/shard_map/gradients/all_to_all | solution.py:46
  75.9 0.0 collective-permute-done.5.arrived
  75.9 0.0 copy-done
  75.9 0.0 copy-done.2
  75.9 0.0 copy-start.3
  76.0 1.5 %copy-done.3 = bf16[512,1792]{1,0:T(8,128)(2,1)S(1)} copy-done((bf16[512,1792]{1,0:T(8,128)(2,1)S(1)}, bf16[512,1792]{1,0:T(8,128)(2,1)}, u32[]{:S(2)}) %copy-start.3) | copy-done | bytes 1835032
  77.4 0.0 copy-start.5
  77.4 0.9 copy-done.5
  78.4 0.0 copy-start.7
  78.4 0.9 copy-done.7
  79.3 3.1 %finish.1 = (bf16[7,1,256,128]{3,2,1,0:T(8,128)(2,1)}, bf16[7,1,256,128]{3,2,1,0:T(8,128)(2,1)}, f32[8,128]{1,0:T(8,128)S(1)}) custom-call(f32[8,512]{1,0:T(8,128)S(1)} %excite.1.coef, bf16[256,512]{1,0:T(8,128)(2,1)S(1)} %copy-done.7, bf16[256,512]{1,0:T(8,128)(2,1)S(1)} %copy-done.5, bf16[512,1792]{1,0:T(8,128)(2,1)S(1)} %get-tuple-element.45.act2, ...), custom_call_target="tpu_custom_call" | custom-call | flops 100000 | bytes 100000 | tf_op jit(solution)/shard_map/finish/finish/pallas_call | solution.py:711
  82.5 5.3 %all-to-all-done.3.pieces = bf16[16,9,16,128]{3,2,1,0:T(8,128)(2,1)S(1)} async-done(((bf16[16,9,16,128]{3,2,1,0:T(8,128)(2,1)}), bf16[16,9,16,128]{3,2,1,0:T(8,128)(2,1)S(1)}, u32[]{:S(2)}, u32[]{:S(2)}) %all-to-all-start.3) | async-done | bytes 589856 | tf_op jit(solution)/shard_map/gradients/all_to_all | solution.py:46
  87.8 0.2 middle.1
  87.9 13.4 %all_to_all.26.lines = bf16[8,6,16,128]{3,2,1,0:T(8,128)(2,1)S(1)} all-to-all(bf16[8,6,16,128]{3,2,1,0:T(8,128)(2,1)S(1)} %middle.1), channel_id=1, replica_groups={{0,32,64,96,128,160,192,224},{16,48,80,112,144,176,208,240},{1,33,65,97..., dimensions={0} | all-to-all | bytes 393216 | tf_op jit(solution)/shard_map/gradients/all_to_all | solution.py:46
  101.3 0.7 tail.1
Async XLA Ops:
  0.6 12.9 %collective-permute-start.1 = (bf16[7,1,256,128]{3,2,1,0:T(8,128)(2,1)}, bf16[7,1,256,128]{3,2,1,0:T(8,128)(2,1)S(1)}, u32[]{:S(2)}, u32[]{:S(2)}) collective-permute-start(bf16[7,1,256,128]{3,2,1,0:T(8,128)(2,1)} %x.3), channel_id=1, source_target_pairs={{0,1},{1,0},{2,3},{3,2},{4,5},{5,4},{6,7},{7,6},{8,9},{9,8},{10,11... | collective-permute-start | bytes 1376264 | tf_op jit(solution)/shard_map/rows/ppermute | solution.py:802
  0.7 29.8 %copy-start.1 = (bf16[7,1,256,128]{3,2,1,0:T(8,128)(2,1)S(1)}, bf16[7,1,256,128]{3,2,1,0:T(8,128)(2,1)}, u32[]{:S(2)}) copy-start(bf16[7,1,256,128]{3,2,1,0:T(8,128)(2,1)} %c.3) | copy-start | bytes 1376260
  2.5 14.3 %collective-permute-start = (bf16[2,2,1,256,128]{4,3,2,1,0:T(8,128)(2,1)S(1)}, bf16[2,2,1,256,128]{4,3,2,1,0:T(8,128)(2,1)S(1)}, u32[]{:S(2)}, u32[]{:S(2)}) collective-permute-start(bf16[2,2,1,256,128]{4,3,2,1,0:T(8,128)(2,1)S(1)} %get-tuple-element.36), channel_id=1, source_target_pairs={{1,2},{3,4},{5,6},{7,8},{9,10},{11,12},{13,14},{2,1},{4,3},{6,5},{... | collective-permute-start | bytes 786440 | tf_op jit(solution)/shard_map/rows/ppermute | solution.py:801
  6.8 15.6 %all-to-all-start = ((bf16[8,32,128]{2,1,0:T(8,128)(2,1)}), bf16[8,32,128]{2,1,0:T(8,128)(2,1)S(1)}, u32[]{:S(2)}, u32[]{:S(2)}) async-start(bf16[8,32,128]{2,1,0:T(8,128)(2,1)} %get-tuple-element.35), calls=%async_computation | async-start | bytes 131072 | tf_op jit(solution)/shard_map/weights/all_to_all | solution.py:46
  13.6 0.8 copy-start.8
  17.7 13.0 %copy-start.10 = (bf16[2,256,256]{2,1,0:T(8,128)(2,1)S(1)}, bf16[2,256,256]{2,1,0:T(8,128)(2,1)}, u32[]{:S(2)}) copy-start(bf16[2,256,256]{2,1,0:T(8,128)(2,1)} %get-tuple-element.40.near_in) | copy-start | bytes 786436
  23.3 18.8 %all-to-all-start.1 = ((bf16[16,11,16,128]{3,2,1,0:T(8,128)(2,1)}), bf16[16,11,16,128]{3,2,1,0:T(8,128)(2,1)S(1)}, u32[]{:S(2)}, u32[]{:S(2)}) async-start(bf16[16,11,16,128]{3,2,1,0:T(8,128)(2,1)} %spread.1), calls=%async_computation.1 | async-start | bytes 1441792 | tf_op jit(solution)/shard_map/weights/all_to_all | solution.py:46
  30.5 1.9 %collective-permute-start.3 = (bf16[7,1,256,128]{3,2,1,0:T(8,128)(2,1)S(1)}, bf16[7,1,256,128]{3,2,1,0:T(8,128)(2,1)S(1)}, u32[]{:S(2)}, u32[]{:S(2)}) collective-permute-start(bf16[7,1,256,128]{3,2,1,0:T(8,128)(2,1)S(1)} %copy-done.1), channel_id=1, source_target_pairs={{0,1},{1,0},{2,3},{3,2},{4,5},{5,4},{6,7},{7,6},{8,9},{9,8},{10,11... | collective-permute-start | bytes 1376264 | tf_op jit(solution)/shard_map/rows/ppermute | solution.py:803
  30.7 2.2 %collective-permute-start.2 = (bf16[2,256,256]{2,1,0:T(8,128)(2,1)S(1)}, bf16[2,256,256]{2,1,0:T(8,128)(2,1)S(1)}, u32[]{:S(2)}, u32[]{:S(2)}) collective-permute-start(bf16[2,256,256]{2,1,0:T(8,128)(2,1)S(1)} %copy-done.10), channel_id=1, source_target_pairs={{0,1},{1,0},{2,3},{3,2},{4,5},{5,4},{6,7},{7,6},{8,9},{9,8},{10,11... | collective-permute-start | bytes 786440 | tf_op jit(solution)/shard_map/rows/ppermute | solution.py:806
  32.4 9.7 %copy-start.9 = (bf16[7,1,256,128]{3,2,1,0:T(8,128)(2,1)}, bf16[7,1,256,128]{3,2,1,0:T(8,128)(2,1)S(1)}, u32[]{:S(2)}) copy-start(bf16[7,1,256,128]{3,2,1,0:T(8,128)(2,1)S(1)} %collective-permute-done.3.other_c) | copy-start | bytes 1376260
  32.8 9.3 %copy-start.11 = (bf16[2,256,256]{2,1,0:T(8,128)(2,1)}, bf16[2,256,256]{2,1,0:T(8,128)(2,1)S(1)}, u32[]{:S(2)}) copy-start(bf16[2,256,256]{2,1,0:T(8,128)(2,1)S(1)} %collective-permute-done.2.far_in) | copy-start | bytes 786436
  52.7 18.2 %copy-start.4 = (bf16[256,512]{1,0:T(8,128)(2,1)}, bf16[256,512]{1,0:T(8,128)(2,1)S(1)}, u32[]{:S(2)}) copy-start(bf16[256,512]{1,0:T(8,128)(2,1)S(1)} %get-tuple-element.44.w_exp) | copy-start | bytes 786436
  52.7 18.2 %copy-start.6 = (bf16[256,512]{1,0:T(8,128)(2,1)}, bf16[256,512]{1,0:T(8,128)(2,1)S(1)}, u32[]{:S(2)}) copy-start(bf16[256,512]{1,0:T(8,128)(2,1)S(1)} %get-tuple-element.43.w_proj) | copy-start | bytes 786436
  52.7 8.8 %collective-permute-start.4 = (bf16[2,8,2,16,128]{4,3,2,1,0:T(8,128)(2,1)S(1)}, bf16[2,8,2,16,128]{4,3,2,1,0:T(8,128)(2,1)S(1)}, u32[]{:S(2)}, u32[]{:S(2)}) collective-permute-start(bf16[2,8,2,16,128]{4,3,2,1,0:T(8,128)(2,1)S(1)} %get-tuple-element.42.own_rows), channel_id=1, source_target_pairs={{0,1},{1,0},{2,3},{3,2},{4,5},{5,4},{6,7},{7,6},{8,9},{9,8},{10,11... | collective-permute-start | bytes 393224 | tf_op jit(solution)/shard_map/sums/ppermute | solution.py:815
  62.0 13.9 %copy-start = (bf16[7,1,256,128]{3,2,1,0:T(8,128)(2,1)S(1)}, bf16[7,1,256,128]{3,2,1,0:T(8,128)(2,1)}, u32[]{:S(2)}) copy-start(bf16[7,1,256,128]{3,2,1,0:T(8,128)(2,1)} %x.3) | copy-start | bytes 1376260
  62.0 13.9 %copy-start.2 = (bf16[7,1,256,128]{3,2,1,0:T(8,128)(2,1)S(1)}, bf16[7,1,256,128]{3,2,1,0:T(8,128)(2,1)}, u32[]{:S(2)}) copy-start(bf16[7,1,256,128]{3,2,1,0:T(8,128)(2,1)} %c.3) | copy-start | bytes 1376260
  70.9 5.0 %collective-permute-start.5 = (bf16[2,7,256,128]{3,2,1,0:T(8,128)(2,1)}, bf16[2,7,256,128]{3,2,1,0:T(8,128)(2,1)}, u32[]{:S(2)}, u32[]{:S(2)}) collective-permute-start(bf16[2,7,256,128]{3,2,1,0:T(8,128)(2,1)} %get-tuple-element.53), channel_id=1, source_target_pairs={{0,1},{1,0},{2,3},{3,2},{4,5},{5,4},{6,7},{7,6},{8,9},{9,8},{10,11... | collective-permute-start | bytes 2752520 | tf_op jit(solution)/shard_map/finish/ppermute | solution.py:822
  71.1 16.7 %all-to-all-start.3 = ((bf16[16,9,16,128]{3,2,1,0:T(8,128)(2,1)}), bf16[16,9,16,128]{3,2,1,0:T(8,128)(2,1)S(1)}, u32[]{:S(2)}, u32[]{:S(2)}) async-start(bf16[16,9,16,128]{3,2,1,0:T(8,128)(2,1)} %bitcast.6), calls=%async_computation.3 | async-start | bytes 1179648 | tf_op jit(solution)/shard_map/gradients/all_to_all | solution.py:46
  75.9 1.5 %copy-start.3 = (bf16[512,1792]{1,0:T(8,128)(2,1)S(1)}, bf16[512,1792]{1,0:T(8,128)(2,1)}, u32[]{:S(2)}) copy-start(bf16[512,1792]{1,0:T(8,128)(2,1)} %get-tuple-element.52.grad_expanded) | copy-start | bytes 5505028
  77.4 0.9 copy-start.5
  78.4 0.9 copy-start.7

commit v5 on v4

--- a/solution.py
+++ b/solution.py
@@ -330,9 +330,9 @@
     core, chip = tensor_place()
     copies = copy_all(
         (
+            (normed_in, normed),
             (near_in, near),
             (far_in, far),
-            (normed_in, normed),
             (own_c, own_c_in),
             (other_c, other_c_in),
         ),
@@ -362,14 +362,15 @@
             weight[...], source, (((0,), (0,)), ((), ())), preferred_element_type=f32
         ).astype(target.dtype)
 
-    for copy in copies[:3]:
+    copies[0].wait()
+    for part in range(ROWS // 2):
+        cells = slice(part * 256, part * 256 + 256)
+        multiply(w_exp, normed[:, cells], expanded, 2 + 2 * part)
+    for copy in copies[1:3]:
         copy.wait()
     near_first = core == 0
     multiply(w_exp, jnp.where(near_first, near[0], far[0]), expanded, 0)
     multiply(w_exp, jnp.where(near_first, far[0], near[0]), expanded, ROWS + 2)
-    for part in range(ROWS // 2):
-        cells = slice(part * 256, part * 256 + 256)
-        multiply(w_exp, normed[:, cells], expanded, 2 + 2 * part)
     first_chip = jnp.where(chip > 0, 1.0, 0.0)
     last_chip = jnp.where(chip < 7, 1.0, 0.0)
 
@@ -516,24 +517,14 @@
     coef[5:8, :] = jnp.zeros((3, HALF), f32)
 
 
-def excite(sums, own_rows, other_rows):
-    return pl.pallas_call(
-        excite_kernel,
-        in_specs=in_vmem(3),
-        out_specs=in_vmem(1)[0],
-        out_shape=held((8, HALF), f32),
-        compiler_params=params(),
-        cost_estimate=cost(SMALL, 4 * 10**6),
-        name="excite",
-    )(sums, *kept(own_rows), other_rows)
-
-
 def backward_kernel(
-    coef, weights, normed, act1, slope1, slope2, grad_hidden, proj_grad, w_proj, w_exp, act2,
-    grad_out, pieces_out, other_out,
+    all_sums, own_rows, other_rows,
+    weights, normed, act1, slope1, slope2, grad_hidden, proj_grad, w_proj, w_exp, act2,
+    coef, grad_out, pieces_out, other_out,
     grad_expanded, pieces, other, copied, pieces_copied, other_copied,
     taps, gates, pools, kernel_sums, tap_rows,
 ):
+    excite_kernel(all_sums, own_rows, other_rows, coef)
     for block in range(BLOCKS):
         cells = slice(block * 128, block * 128 + 128)
         spread_taps(
@@ -602,7 +593,7 @@
 
     def one_block(block, carry):
         first = block * (128 // GROUP)
-        lax.fori_loop(0, 128 // GROUP, lambda i, c: one_group(first + i, c), 0, unroll=2)
+        lax.fori_loop(0, 128 // GROUP, lambda i, c: one_group(first + i, c), 0, unroll=4)
         block_copy(block).start()
         return carry
 
@@ -652,11 +643,11 @@
         copy.wait()
 
 
-def backward(coef, weights, normed, act1, slope1, slope2, grad_hidden, proj_grad, w_proj, w_exp, act2):
+def backward(all_sums, own_rows, other_rows, weights, normed, act1, slope1, slope2, grad_hidden, proj_grad, w_proj, w_exp, act2):
     return pl.pallas_call(
         backward_kernel,
-        in_specs=in_vmem(11),
-        out_specs=in_hbm(3),
+        in_specs=in_vmem(13),
+        out_specs=in_vmem(1) + in_hbm(3),
         scratch_shapes=[
             pltpu.VMEM((HALF, ROWS * COLS), bf16),
             pltpu.VMEM((2, 8, 9, 16, 128), bf16),
@@ -671,6 +662,7 @@
             pltpu.VMEM((16, 128), f32),
         ],
         out_shape=[
+            held((8, HALF), f32),
             pltpu.HBM((HALF, ROWS * COLS), bf16),
             pltpu.HBM((2, 8, 9, 16, 128), bf16),
             pltpu.HBM((2, 7, CH, COLS), bf16),
@@ -679,8 +671,11 @@
         cost_estimate=cost(10**9, 45 * 10**6),
         name="backward",
     )(
+        all_sums,
+        *kept(own_rows),
+        other_rows,
         *kept(
-            coef, weights, normed, act1, slope1, slope2, grad_hidden, proj_grad, w_proj, w_exp, act2
+            weights, normed, act1, slope1, slope2, grad_hidden, proj_grad, w_proj, w_exp, act2
         )
     )
 
@@ -814,9 +809,8 @@
     with jax.named_scope("sums"):
         other_rows = lax.ppermute(own_rows, "tensor", swap)
         all_sums = exchange(sums, "tensor")
-    coef = excite(all_sums, own_rows, other_rows)
-    grad_expanded, pieces, partial_out = backward(
-        coef, weights, normed, act1, slope1, slope2, grad_hidden, proj_grad, w_proj, w_exp, act2
+    coef, grad_expanded, pieces, partial_out = backward(
+        all_sums, own_rows, other_rows, weights, normed, act1, slope1, slope2, grad_hidden, proj_grad, w_proj, w_exp, act2
     )
     with jax.named_scope("finish"):
         arrived = lax.ppermute(partial_out, "tensor", swap)

time: 103 us -> 102 us (level)
    pallas_call x2 -> x1, Pallas kernels: 9.39 us -> 9.11 us  [backward(): pl.pallas_call(backward_kernel, in_specs=in_vmem(13), out_specs=in_vmem(1...]
where the time goes in v5:
time: 102 us
  Pallas kernels  29.6 us (29%)
  starting transfers between devices  24 us (24%)
  blocking collectives  22.1 us (22%)
  waiting for transfers between devices  21 us (21%)
  local copies, waits for them, and re-layouts  4.19 us (4%)
    all_to_all x2, blocking collectives, exchange(): lax.all_to_all(pieces, axes, 0, 0, tiled=True, axis_index_groups=members)  22.1 us
    all_to_all x3, waiting for transfers between devices, exchange(): lax.all_to_all(pieces, axes, 0, 0, tiled=True, axis_index_groups=members)  19.3 us
    all_to_all x3, starting transfers between devices, exchange(): lax.all_to_all(pieces, axes, 0, 0, tiled=True, axis_index_groups=members)  18.8 us
    pallas_call x1, Pallas kernels, forward(): pl.pallas_call(forward_kernel, in_specs=in_vmem(1) + in_hbm(5), out_specs...  10.4 us
    pallas_call x1, Pallas kernels, backward(): pl.pallas_call(backward_kernel, in_specs=in_vmem(13), out_specs=in_vmem(1...  9.11 us
    ppermute x1, starting transfers between devices, body(): near = lax.ppermute(edge, 'tensor', edges)  4.27 us
    unnamed x24, local copies, waits for them, and re-layouts  4.19 us
    pallas_call x1, Pallas kernels, finish(): pl.pallas_call(finish_kernel, in_specs=in_vmem(8), out_specs=in_vmem(3),...  3.14 us
  transfers between devices with their start and end apart: 9, of which 5 were waited for; matrix products, arithmetic and copies ran while one was open for 0% of the time, Pallas kernels for 8%

profile of v5, /device:TPU:2, one launch (start us, length us, event | category | flops | bytes accessed | tf_op | source)
XLA Modules:
  0.0 101.6 jit_solution(8839090785059947822)
XLA Ops:
  0.6 0.1 collective-permute-start.1
  0.7 0.0 copy-start.1
  0.7 1.8 %start.1 = (bf16[8,32,128]{2,1,0:T(8,128)(2,1)}, bf16[2,2,1,256,128]{4,3,2,1,0:T(8,128)(2,1)S(1)}) custom-call(bf16[7,1,256,128]{3,2,1,0:T(8,128)(2,1)} %x.3, bf16[7,1,256,128]{3,2,1,0:T(8,128)(2,1)} %c.3, bf16[16,64]{1,0:T(8,128)(2,1)} %w_expand.1, bf16[16,64]{1,0:T(8,128)(2,1)} %w_project.1, bf16[9,64]{1,0:T(8,128)(2,1)} %bitcast.7, ...), custom_call_target="tpu_custom_call" | custom-call | flops 100000 | bytes 100000 | tf_op jit(solution)/shard_map/start/pallas_call | solution.py:179
  2.5 4.3 %collective-permute-start = (bf16[2,2,1,256,128]{4,3,2,1,0:T(8,128)(2,1)S(1)}, bf16[2,2,1,256,128]{4,3,2,1,0:T(8,128)(2,1)S(1)}, u32[]{:S(2)}, u32[]{:S(2)}) collective-permute-start(bf16[2,2,1,256,128]{4,3,2,1,0:T(8,128)(2,1)S(1)} %get-tuple-element.37), channel_id=1, source_target_pairs={{1,2},{3,4},{5,6},{7,8},{9,10},{11,12},{13,14},{2,1},{4,3},{6,5},{... | collective-permute-start | bytes 786440 | tf_op jit(solution)/shard_map/rows/ppermute | solution.py:796
  6.8 6.7 %all-to-all-start = ((bf16[8,32,128]{2,1,0:T(8,128)(2,1)}), bf16[8,32,128]{2,1,0:T(8,128)(2,1)S(1)}, u32[]{:S(2)}, u32[]{:S(2)}) async-start(bf16[8,32,128]{2,1,0:T(8,128)(2,1)} %get-tuple-element.36), calls=%async_computation | async-start | bytes 131072 | tf_op jit(solution)/shard_map/weights/all_to_all | solution.py:46
  13.6 0.0 collective-permute-done.1.other_x
  13.6 0.0 copy-start.8
  13.6 0.8 copy-done.8
  14.3 2.4 %main_norm.1 = (bf16[256,1792]{1,0:T(8,128)(2,1)}, f32[8,128]{1,0:T(8,128)S(1)}) custom-call(bf16[7,1,256,128]{3,2,1,0:T(8,128)(2,1)} %x.3, bf16[7,1,256,128]{3,2,1,0:T(8,128)(2,1)} %copy-done.8), custom_call_target="tpu_custom_call" | custom-call | flops 100000 | bytes 100000 | tf_op jit(solution)/shard_map/rows/main_norm/pallas_call | solution.py:267
  16.8 0.0 collective-permute-done.near
  16.8 0.8 edge_norm.1
  17.7 0.0 copy-start.10
  17.7 4.7 %all-to-all-done.lines = bf16[8,32,128]{2,1,0:T(8,128)(2,1)S(1)} async-done(((bf16[8,32,128]{2,1,0:T(8,128)(2,1)}), bf16[8,32,128]{2,1,0:T(8,128)(2,1)S(1)}, u32[]{:S(2)}, u32[]{:S(2)}) %all-to-all-start) | async-done | bytes 65568 | tf_op jit(solution)/shard_map/weights/all_to_all | solution.py:46
  22.4 1.0 spread.1
  23.3 7.2 %all-to-all-start.1 = ((bf16[16,11,16,128]{3,2,1,0:T(8,128)(2,1)}), bf16[16,11,16,128]{3,2,1,0:T(8,128)(2,1)S(1)}, u32[]{:S(2)}, u32[]{:S(2)}) async-start(bf16[16,11,16,128]{3,2,1,0:T(8,128)(2,1)} %spread.1), calls=%async_computation.1 | async-start | bytes 1441792 | tf_op jit(solution)/shard_map/weights/all_to_all | solution.py:46
  30.5 0.0 copy-done.1
  30.5 0.1 collective-permute-start.3
  30.6 0.0 copy-done.10
  30.7 0.5 collective-permute-start.2
  31.1 1.3 %collective-permute-done.3.other_c = bf16[7,1,256,128]{3,2,1,0:T(8,128)(2,1)S(1)} collective-permute-done((bf16[7,1,256,128]{3,2,1,0:T(8,128)(2,1)S(1)}, bf16[7,1,256,128]{3,2,1,0:T(8,128)(2,1)S(1)}, u32[]{:S(2)}, u32[]{:S(2)}) %collective-permute-start.3) | collective-permute-done | bytes 458784 | tf_op jit(solution)/shard_map/rows/ppermute | solution.py:798
  32.4 0.0 copy-start.9
  32.5 0.4 collective-permute-done.2.far_in
  32.8 0.0 copy-start.11
  32.8 9.3 %all-to-all-done.1 = bf16[16,11,16,128]{3,2,1,0:T(8,128)(2,1)S(1)} async-done(((bf16[16,11,16,128]{3,2,1,0:T(8,128)(2,1)}), bf16[16,11,16,128]{3,2,1,0:T(8,128)(2,1)S(1)}, u32[]{:S(2)}, u32[]{:S(2)}) %all-to-all-start.1) | async-done | bytes 720928 | tf_op jit(solution)/shard_map/weights/all_to_all | solution.py:46
  42.1 0.0 copy-done.11
  42.1 0.0 copy-done.9
  42.1 10.4 %forward.1 = (bf16[256,1792]{1,0:T(8,128)(2,1)S(1)}, bf16[512,2304]{1,0:T(8,128)(2,1)S(1)}, bf16[512,1792]{1,0:T(8,128)(2,1)S(1)}, bf16[512,1792]{1,0:T(8,128)(2...) custom-call(bf16[2,8,11,16,128]{4,3,2,1,0:T(8,128)(2,1)S(1)} %bitcas, ...), custom_call_target="tpu_custom_call" | custom-call | flops 1000000000 | bytes 50000000 | tf_op jit(solution)/shard_map/forward/pallas_call | solution.py:435
  52.5 0.0 copy-start.4
  52.5 0.0 copy-start.6
  52.5 0.1 collective-permute-start.4
  52.6 8.7 %all_to_all.25.all_sums = f32[16,8,128]{2,1,0:T(8,128)S(1)} all-to-all(f32[16,8,128]{2,1,0:T(8,128)S(1)} %get-tuple-element.42), channel_id=1, replica_groups=mesh['dp'=16,'tensor'=16] {'tensor'}, dimensions={0} | all-to-all | bytes 131072 | tf_op jit(solution)/shard_map/sums/all_to_all | solution.py:46
  61.3 0.0 collective-permute-done.4.other_rows
  61.3 0.0 copy-start
  61.3 0.0 copy-start.2
  61.3 9.1 %backward.1 = (f32[8,512]{1,0:T(8,128)S(1)}, bf16[512,1792]{1,0:T(8,128)(2,1)}, bf16[2,8,9,16,128]{4,3,2,1,0:T(8,128)(2,1)}, bf16[2,7,256,128]{3,2,1,0:T(8,128)(2,1)}) custom-call(f32[16,8,128]{2,1,0:T(8,128)S(1)} %all_to_all.25.all_sums, bf16[2,8,2,16,128]{4,3,2,1,0:T(8,128)(2,1)S(1)} %get-tuple-element.43.own_rows, ...), custom_call_target="tpu_custom_call" | custom-call | flops 1000000000 | bytes 45000000 | tf_op jit(solution)/shard_map/backward/pallas_call | solution.py:647
  70.5 0.0 copy-done.4
  70.5 0.0 copy-done.6
  70.5 0.2 collective-permute-start.5
  70.7 4.8 %all-to-all-start.3 = ((bf16[16,9,16,128]{3,2,1,0:T(8,128)(2,1)}), bf16[16,9,16,128]{3,2,1,0:T(8,128)(2,1)S(1)}, u32[]{:S(2)}, u32[]{:S(2)}) async-start(bf16[16,9,16,128]{3,2,1,0:T(8,128)(2,1)} %bitcast.6), calls=%async_computation.3 | async-start | bytes 1179648 | tf_op jit(solution)/shard_map/gradients/all_to_all | solution.py:46
  75.5 0.0 collective-permute-done.5.arrived
  75.5 0.0 copy-done
  75.5 0.0 copy-done.2
  75.5 0.0 copy-start.3
  75.5 1.5 %copy-done.3 = bf16[512,1792]{1,0:T(8,128)(2,1)S(1)} copy-done((bf16[512,1792]{1,0:T(8,128)(2,1)S(1)}, bf16[512,1792]{1,0:T(8,128)(2,1)}, u32[]{:S(2)}) %copy-start.3) | copy-done | bytes 1835032
  77.0 0.0 copy-start.5
  77.0 0.9 copy-done.5
  78.0 0.0 copy-start.7
  78.0 0.9 copy-done.7
  78.9 3.1 %finish.1 = (bf16[7,1,256,128]{3,2,1,0:T(8,128)(2,1)}, bf16[7,1,256,128]{3,2,1,0:T(8,128)(2,1)}, f32[8,128]{1,0:T(8,128)S(1)}) custom-call(f32[8,512]{1,0:T(8,128)S(1)} %get-tuple-element.53.coef, bf16[256,512]{1,0:T(8,128)(2,1)S(1)} %copy-done.7, bf16[256,512]{1,0:T(8,128)(2,1)S(1)} %copy-done.5, bf16[512,1792]{1,0:T(8,128)(2,1)S(1)} %get-tuple-element.52.act2, ...), custom_call_target="tpu_custom_call" | custom-call | flops 100000 | bytes 100000 | tf_op jit(solution)/shard_map/finish/finish/pallas_call | solution.py:706
  82.1 5.3 %all-to-all-done.3.pieces = bf16[16,9,16,128]{3,2,1,0:T(8,128)(2,1)S(1)} async-done(((bf16[16,9,16,128]{3,2,1,0:T(8,128)(2,1)}), bf16[16,9,16,128]{3,2,1,0:T(8,128)(2,1)S(1)}, u32[]{:S(2)}, u32[]{:S(2)}) %all-to-all-start.3) | async-done | bytes 589856 | tf_op jit(solution)/shard_map/gradients/all_to_all | solution.py:46
  87.3 0.2 middle.1
  87.5 13.4 %all_to_all.26.lines = bf16[8,6,16,128]{3,2,1,0:T(8,128)(2,1)S(1)} all-to-all(bf16[8,6,16,128]{3,2,1,0:T(8,128)(2,1)S(1)} %middle.1), channel_id=1, replica_groups={{0,32,64,96,128,160,192,224},{16,48,80,112,144,176,208,240},{1,33,65,97..., dimensions={0} | all-to-all | bytes 393216 | tf_op jit(solution)/shard_map/gradients/all_to_all | solution.py:46
  100.9 0.7 tail.1
Async XLA Ops:
  0.6 12.9 %collective-permute-start.1 = (bf16[7,1,256,128]{3,2,1,0:T(8,128)(2,1)}, bf16[7,1,256,128]{3,2,1,0:T(8,128)(2,1)S(1)}, u32[]{:S(2)}, u32[]{:S(2)}) collective-permute-start(bf16[7,1,256,128]{3,2,1,0:T(8,128)(2,1)} %x.3), channel_id=1, source_target_pairs={{0,1},{1,0},{2,3},{3,2},{4,5},{5,4},{6,7},{7,6},{8,9},{9,8},{10,11... | collective-permute-start | bytes 1376264 | tf_op jit(solution)/shard_map/rows/ppermute | solution.py:797
  0.7 29.8 %copy-start.1 = (bf16[7,1,256,128]{3,2,1,0:T(8,128)(2,1)S(1)}, bf16[7,1,256,128]{3,2,1,0:T(8,128)(2,1)}, u32[]{:S(2)}) copy-start(bf16[7,1,256,128]{3,2,1,0:T(8,128)(2,1)} %c.3) | copy-start | bytes 1376260
  2.5 14.3 %collective-permute-start = (bf16[2,2,1,256,128]{4,3,2,1,0:T(8,128)(2,1)S(1)}, bf16[2,2,1,256,128]{4,3,2,1,0:T(8,128)(2,1)S(1)}, u32[]{:S(2)}, u32[]{:S(2)}) collective-permute-start(bf16[2,2,1,256,128]{4,3,2,1,0:T(8,128)(2,1)S(1)} %get-tuple-element.37), channel_id=1, source_target_pairs={{1,2},{3,4},{5,6},{7,8},{9,10},{11,12},{13,14},{2,1},{4,3},{6,5},{... | collective-permute-start | bytes 786440 | tf_op jit(solution)/shard_map/rows/ppermute | solution.py:796
  6.8 15.6 %all-to-all-start = ((bf16[8,32,128]{2,1,0:T(8,128)(2,1)}), bf16[8,32,128]{2,1,0:T(8,128)(2,1)S(1)}, u32[]{:S(2)}, u32[]{:S(2)}) async-start(bf16[8,32,128]{2,1,0:T(8,128)(2,1)} %get-tuple-element.36), calls=%async_computation | async-start | bytes 131072 | tf_op jit(solution)/shard_map/weights/all_to_all | solution.py:46
  13.6 0.8 copy-start.8
  17.7 13.0 %copy-start.10 = (bf16[2,256,256]{2,1,0:T(8,128)(2,1)S(1)}, bf16[2,256,256]{2,1,0:T(8,128)(2,1)}, u32[]{:S(2)}) copy-start(bf16[2,256,256]{2,1,0:T(8,128)(2,1)} %get-tuple-element.41.near_in) | copy-start | bytes 786436
  23.3 18.8 %all-to-all-start.1 = ((bf16[16,11,16,128]{3,2,1,0:T(8,128)(2,1)}), bf16[16,11,16,128]{3,2,1,0:T(8,128)(2,1)S(1)}, u32[]{:S(2)}, u32[]{:S(2)}) async-start(bf16[16,11,16,128]{3,2,1,0:T(8,128)(2,1)} %spread.1), calls=%async_computation.1 | async-start | bytes 1441792 | tf_op jit(solution)/shard_map/weights/all_to_all | solution.py:46
  30.5 1.9 %collective-permute-start.3 = (bf16[7,1,256,128]{3,2,1,0:T(8,128)(2,1)S(1)}, bf16[7,1,256,128]{3,2,1,0:T(8,128)(2,1)S(1)}, u32[]{:S(2)}, u32[]{:S(2)}) collective-permute-start(bf16[7,1,256,128]{3,2,1,0:T(8,128)(2,1)S(1)} %copy-done.1), channel_id=1, source_target_pairs={{0,1},{1,0},{2,3},{3,2},{4,5},{5,4},{6,7},{7,6},{8,9},{9,8},{10,11... | collective-permute-start | bytes 1376264 | tf_op jit(solution)/shard_map/rows/ppermute | solution.py:798
  30.7 2.2 %collective-permute-start.2 = (bf16[2,256,256]{2,1,0:T(8,128)(2,1)S(1)}, bf16[2,256,256]{2,1,0:T(8,128)(2,1)S(1)}, u32[]{:S(2)}, u32[]{:S(2)}) collective-permute-start(bf16[2,256,256]{2,1,0:T(8,128)(2,1)S(1)} %copy-done.10), channel_id=1, source_target_pairs={{0,1},{1,0},{2,3},{3,2},{4,5},{5,4},{6,7},{7,6},{8,9},{9,8},{10,11... | collective-permute-start | bytes 786440 | tf_op jit(solution)/shard_map/rows/ppermute | solution.py:801
  32.4 9.7 %copy-start.9 = (bf16[7,1,256,128]{3,2,1,0:T(8,128)(2,1)}, bf16[7,1,256,128]{3,2,1,0:T(8,128)(2,1)S(1)}, u32[]{:S(2)}) copy-start(bf16[7,1,256,128]{3,2,1,0:T(8,128)(2,1)S(1)} %collective-permute-done.3.other_c) | copy-start | bytes 1376260
  32.8 9.3 %copy-start.11 = (bf16[2,256,256]{2,1,0:T(8,128)(2,1)}, bf16[2,256,256]{2,1,0:T(8,128)(2,1)S(1)}, u32[]{:S(2)}) copy-start(bf16[2,256,256]{2,1,0:T(8,128)(2,1)S(1)} %collective-permute-done.2.far_in) | copy-start | bytes 786436
  52.5 18.0 %copy-start.4 = (bf16[256,512]{1,0:T(8,128)(2,1)}, bf16[256,512]{1,0:T(8,128)(2,1)S(1)}, u32[]{:S(2)}) copy-start(bf16[256,512]{1,0:T(8,128)(2,1)S(1)} %get-tuple-element.51.w_exp) | copy-start | bytes 786436
  52.5 17.9 %copy-start.6 = (bf16[256,512]{1,0:T(8,128)(2,1)}, bf16[256,512]{1,0:T(8,128)(2,1)S(1)}, u32[]{:S(2)}) copy-start(bf16[256,512]{1,0:T(8,128)(2,1)S(1)} %get-tuple-element.50.w_proj) | copy-start | bytes 786436
  52.5 8.8 %collective-permute-start.4 = (bf16[2,8,2,16,128]{4,3,2,1,0:T(8,128)(2,1)S(1)}, bf16[2,8,2,16,128]{4,3,2,1,0:T(8,128)(2,1)S(1)}, u32[]{:S(2)}, u32[]{:S(2)}) collective-permute-start(bf16[2,8,2,16,128]{4,3,2,1,0:T(8,128)(2,1)S(1)} %get-tuple-element.43.own_rows), channel_id=1, source_target_pairs={{0,1},{1,0},{2,3},{3,2},{4,5},{5,4},{6,7},{7,6},{8,9},{9,8},{10,11... | collective-permute-start | bytes 393224 | tf_op jit(solution)/shard_map/sums/ppermute | solution.py:810
  61.3 14.2 %copy-start = (bf16[7,1,256,128]{3,2,1,0:T(8,128)(2,1)S(1)}, bf16[7,1,256,128]{3,2,1,0:T(8,128)(2,1)}, u32[]{:S(2)}) copy-start(bf16[7,1,256,128]{3,2,1,0:T(8,128)(2,1)} %x.3) | copy-start | bytes 1376260
  61.3 14.2 %copy-start.2 = (bf16[7,1,256,128]{3,2,1,0:T(8,128)(2,1)S(1)}, bf16[7,1,256,128]{3,2,1,0:T(8,128)(2,1)}, u32[]{:S(2)}) copy-start(bf16[7,1,256,128]{3,2,1,0:T(8,128)(2,1)} %c.3) | copy-start | bytes 1376260
  70.5 5.0 %collective-permute-start.5 = (bf16[2,7,256,128]{3,2,1,0:T(8,128)(2,1)}, bf16[2,7,256,128]{3,2,1,0:T(8,128)(2,1)}, u32[]{:S(2)}, u32[]{:S(2)}) collective-permute-start(bf16[2,7,256,128]{3,2,1,0:T(8,128)(2,1)} %get-tuple-element.55), channel_id=1, source_target_pairs={{0,1},{1,0},{2,3},{3,2},{4,5},{5,4},{6,7},{7,6},{8,9},{9,8},{10,11... | collective-permute-start | bytes 2752520 | tf_op jit(solution)/shard_map/finish/ppermute | solution.py:816
  70.7 16.7 %all-to-all-start.3 = ((bf16[16,9,16,128]{3,2,1,0:T(8,128)(2,1)}), bf16[16,9,16,128]{3,2,1,0:T(8,128)(2,1)S(1)}, u32[]{:S(2)}, u32[]{:S(2)}) async-start(bf16[16,9,16,128]{3,2,1,0:T(8,128)(2,1)} %bitcast.6), calls=%async_computation.3 | async-start | bytes 1179648 | tf_op jit(solution)/shard_map/gradients/all_to_all | solution.py:46
  75.5 1.5 %copy-start.3 = (bf16[512,1792]{1,0:T(8,128)(2,1)S(1)}, bf16[512,1792]{1,0:T(8,128)(2,1)}, u32[]{:S(2)}) copy-start(bf16[512,1792]{1,0:T(8,128)(2,1)} %get-tuple-element.54.grad_expanded) | copy-start | bytes 5505028
  77.0 0.9 copy-start.5
  78.0 0.9 copy-start.7
